TPU v7x, 1024 devices: a whole 4x8x16 slice. The times are simulated.
1024 devices in a mesh: blk: 32 (over z_lo, y), owner: 32 (over z_hi, x, core).
Axes of the slice: x: 4, y: 8, z: 16 (z_hi: 4, z_lo: 4; z = z_hi * 4 + z_lo), core: 2. Of those that a mesh axis runs over, the one named last changes fastest.
Arguments:
- amplitudes: bfloat16 [64, 32, 32768], P('owner', None, 'blk'), may hold values from -6 to 6
- integrals: bfloat16 [32, 1024, 1024], P('owner', 'blk'), may hold values from -0.1875 to 0.1875
- cd_tiles: int32 [32, 32], replicated, may hold values from 0 to 63, as said below
- cd_count: int32 [32], replicated, may hold values from 16 to 32, as said below
- ab_tiles: int32 [32, 32], replicated, may hold values from 0 to 63, as said below
- ab_count: int32 [32], replicated, may hold values from 16 to 32, as said below
Outputs:
- residual: float32 [64, 32, 32768], P('owner', None, 'blk')
Inputs may be any that keep to these rules, and one draw needn't show every extreme that they name: `cd_tiles`: tile t is held by owner t // 2. The entries of one task's list are distinct, and at most 1 of them lie with one owner; only the first cd_count entries are used. `cd_count`: some task has 32 live entries. `ab_tiles`: tile t is held by owner t // 2. The entries of one task's list are distinct, and at most 1 of them lie with one owner; only the first ab_count entries are used. `ab_count`: some task has 32 live entries.
All inputs are finite; a program needn't handle non-finite values.
Results may differ from a plain program's by a relative error of at most 0.0029.
Values may be sent and summed in bfloat16 or wider, within the bound.
No kernel may reach another device: no remote copies, remote signals or barrier semaphores. Data moves between devices by JAX's collectives and lax.ppermute only.
A program may use at most 32 MiB of HBM per device.

v0:
```python
import jax
import jax.numpy as jnp
from jax import lax
from jax.sharding import PartitionSpec as P


def slot_tables(tile_list, is_live, tile_dev):
    target = tile_list // tile_dev
    order_idx = jnp.arange(tile_list.shape[-1], dtype=jnp.int32)
    earlier = order_idx[None, :] < order_idx[:, None]
    same_owner = (target[..., :, None] == target[..., None, :]) & is_live[..., None, :] & earlier
    slot_rank = jnp.sum(same_owner.astype(jnp.int32), axis=-1)
    return (target, slot_rank)


def shards(amplitudes, integrals, cd_tiles, cd_count, ab_tiles, ab_count):
    tile_dev = amplitudes.shape[0]
    owners = lax.axis_size("owner")
    own_index = lax.axis_index("owner")
    list_len = cd_tiles.shape[1]
    capacity = (list_len + owners - 1) // owners
    positions = jnp.arange(list_len, dtype=jnp.int32)
    slot_idx = jnp.arange(capacity, dtype=jnp.int32)
    owner_idx = jnp.arange(owners, dtype=jnp.int32)
    local_idx = jnp.arange(tile_dev, dtype=jnp.int32)
    cd_live = positions[None, :] < cd_count[:, None]
    cd_target, cd_rank = slot_tables(cd_tiles, cd_live, tile_dev)
    cd_mine = cd_live & (cd_target == own_index)
    choose = (
        cd_mine[:, None, :, None]
        & (cd_rank[:, None, :, None] == slot_idx[None, :, None, None])
        & ((cd_tiles % tile_dev)[:, None, :, None] == local_idx[None, None, None, :])
    )
    choose = jnp.sum(choose.astype(jnp.int32), axis=2).astype(jnp.bfloat16)
    outgoing = jnp.einsum(
        "qcl,lxy->qcxy", choose, amplitudes, preferred_element_type=jnp.float32
    ).astype(jnp.bfloat16)
    arrived = lax.all_to_all(outgoing, "owner", split_axis=0, concat_axis=0, tiled=True)
    own_cd = lax.dynamic_index_in_dim(cd_target, own_index, 0, keepdims=False)
    own_rank = lax.dynamic_index_in_dim(cd_rank, own_index, 0, keepdims=False)
    own_live = lax.dynamic_index_in_dim(cd_live, own_index, 0, keepdims=False)
    select = (
        own_live[:, None, None]
        & (own_cd[:, None, None] == owner_idx[None, :, None])
        & (own_rank[:, None, None] == slot_idx[None, None, :])
    ).astype(jnp.bfloat16)
    gathered_amps = jnp.einsum(
        "kpc,pcxy->kxy", select, arrived, preferred_element_type=jnp.float32
    ).astype(jnp.bfloat16)
    tile_width = gathered_amps.shape[1]
    occ_width = gathered_amps.shape[2]
    gathered_amps = gathered_amps.reshape(list_len * tile_width, occ_width)
    row_block = integrals[0]
    product = jnp.dot(
        lax.all_gather(row_block, "blk", axis=0, tiled=True),
        gathered_amps,
        preferred_element_type=jnp.float32,
    )
    partial_tiles = product.astype(jnp.bfloat16).reshape(list_len, tile_width, occ_width)
    ab_live = positions[None, :] < ab_count[:, None]
    ab_target, ab_rank = slot_tables(ab_tiles, ab_live, tile_dev)
    own_ab = lax.dynamic_index_in_dim(ab_target, own_index, 0, keepdims=False)
    own_ab_rank = lax.dynamic_index_in_dim(ab_rank, own_index, 0, keepdims=False)
    own_ab_live = lax.dynamic_index_in_dim(ab_live, own_index, 0, keepdims=False)
    send_map = (
        own_ab_live[:, None, None]
        & (own_ab[:, None, None] == owner_idx[None, :, None])
        & (own_ab_rank[:, None, None] == slot_idx[None, None, :])
    ).astype(jnp.bfloat16)
    send_back = jnp.einsum(
        "kpc,kxy->pcxy", send_map, partial_tiles, preferred_element_type=jnp.float32
    ).astype(jnp.bfloat16)
    returned = lax.all_to_all(send_back, "owner", split_axis=0, concat_axis=0, tiled=True)
    ab_mine = ab_live & (ab_target == own_index)
    placing = (
        ab_mine[None, :, None, :]
        & (ab_rank[None, :, None, :] == slot_idx[None, None, :, None])
        & ((ab_tiles % tile_dev)[None, :, None, :] == local_idx[:, None, None, None])
    )
    placing = jnp.sum(placing.astype(jnp.int32), axis=3).astype(jnp.bfloat16)
    return jnp.einsum("lqc,qcxy->lxy", placing, returned, preferred_element_type=jnp.float32)


def solution(mesh):
    placed = (P("owner", None, "blk"), P("owner", "blk", None), P(), P(), P(), P())
    return jax.shard_map(
        shards, mesh=mesh, in_specs=placed, out_specs=P("owner", None, "blk"), check_vma=False
    )
```

profile of v0, /device:TPU:21, one launch (start us, length us, event | category | flops | bytes accessed | tf_op | source)
XLA Modules:
  0.0 368.1 jit_solution(8858480427432200272)
XLA Ops:
  6.5 0.0 copy-start
  6.5 0.8 iota_compare_fusion.6
  7.3 0.7 iota_compare_fusion.3
  8.0 0.8 add_select_fusion.1
  8.8 1.5 convert_reduce_fusion.1
  10.3 0.8 compare_and_fusion
  11.1 0.1 convert_reduce_fusion.2
  11.2 0.0 copy-done
  11.2 0.8 convert_bitcast_fusion.1
  12.0 2.5 copy.23
  14.4 22.2 %all-to-all-start = ((bf16[32,1,32,1024]{3,2,1,0:T(8,128)(2,1)}), bf16[32,1,32,1024]{3,2,1,0:T(8,128)(2,1)S(1)}, u32[]{:S(2)}, u32[]{:S(2)}) async-start(bf16[32,1,32,1024]{3,2,1,0:T(8,128)(2,1)} %copy.23), calls=%async_computation | async-start | bytes 4194304 | tf_op jit(solution)/shard_map/all_to_all | solution.py:38
  36.6 0.2 all-gather.3.cloned.1.call-start
  36.8 0.5 all-gather.3.cloned.1.call-update
  37.4 55.4 %all-to-all-done = bf16[32,1,32,1024]{3,2,1,0:T(8,128)(2,1)S(1)} async-done(((bf16[32,1,32,1024]{3,2,1,0:T(8,128)(2,1)}), bf16[32,1,32,1024]{3,2,1,0:T(8,128)(2,1)S(1)}, u32[]{:S(2)}, u32[]{:S(2)}) %all-to-all-start) | async-done | bytes 2097184 | tf_op jit(solution)/shard_map/all_to_all | solution.py:38
  92.8 2.9 fusion.12
  95.7 1.2 copy.25
  96.8 123.3 %all-gather.3.cloned.1.call-done = bf16[1,1024,1024]{2,1,0:T(8,128)(2,1)} async-done(((bf16[1,32,1024]{2,1,0:T(8,128)(2,1)}), bf16[1,1024,1024]{2,1,0:T(8,128)(2,1)}) %all-gather.3.cloned.1.call-update) | async-done | bytes 2097168 | tf_op jit(solution)/shard_map/all_gather | solution.py:55
  220.1 3.9 %fusion.15 = bf16[1024,1024]{0,1:T(8,128)(2,1)S(1)} fusion(bf16[1024,1024]{1,0:T(8,128)(2,1)S(1)} %bitcast.47, bf16[1,1024,1024]{2,1,0:T(8,128)(2,1)} %all-gather.3.cloned.1.call-done), kind=kOutput, calls=%fused_computation.13 | convolution fusion | flops 2148532224 | bytes 6291456 | tf_op jit(solution)/shard_map/dot_general | solution.py:54
  224.1 2.9 convert_bitcast_fusion
  226.9 2.5 copy.27
  229.4 0.0 copy-start.1
  229.4 0.0 copy-start.2
  229.4 38.8 %all-to-all-start.1 = ((bf16[32,1,32,1024]{3,2,1,0:T(8,128)(2,1)}), bf16[32,1,32,1024]{3,2,1,0:T(8,128)(2,1)S(1)}, u32[]{:S(2)}, u32[]{:S(2)}) async-start(bf16[32,1,32,1024]{3,2,1,0:T(8,128)(2,1)} %copy.27), calls=%async_computation.1 | async-start | bytes 4194304 | tf_op jit(solution)/shard_map/all_to_all | solution.py:73
  268.2 0.0 copy-done.1
  268.2 0.0 copy-done.2
  268.2 0.1 compare_and_fusion.1
  268.3 0.1 convert_reduce_fusion.3
  268.4 89.7 %all-to-all-done.1 = bf16[32,1,32,1024]{3,2,1,0:T(8,128)(2,1)S(1)} async-done(((bf16[32,1,32,1024]{3,2,1,0:T(8,128)(2,1)}), bf16[32,1,32,1024]{3,2,1,0:T(8,128)(2,1)S(1)}, u32[]{:S(2)}, u32[]{:S(2)}) %all-to-all-start.1) | async-done | bytes 2097184 | tf_op jit(solution)/shard_map/all_to_all | solution.py:73
  358.2 2.3 fusion
  360.5 0.8 copy.29
  (6 shorter events, 0.1 us)
Async XLA Ops:
  6.5 4.7 %copy-start = (bf16[2,32,1024]{2,1,0:T(8,128)(2,1)S(1)}, bf16[2,32,1024]{2,1,0:T(8,128)(2,1)}, u32[]{:S(2)}) copy-start(bf16[2,32,1024]{2,1,0:T(8,128)(2,1)} %param.6) | copy-start | bytes 393220
  14.4 78.4 %all-to-all-start = ((bf16[32,1,32,1024]{3,2,1,0:T(8,128)(2,1)}), bf16[32,1,32,1024]{3,2,1,0:T(8,128)(2,1)S(1)}, u32[]{:S(2)}, u32[]{:S(2)}) async-start(bf16[32,1,32,1024]{3,2,1,0:T(8,128)(2,1)} %copy.23), calls=%async_computation | async-start | bytes 4194304 | tf_op jit(solution)/shard_map/all_to_all | solution.py:38
  36.6 183.5 %all-gather.3.cloned.1.call-start = ((), (), s32[]{:S(2)}) async-start(), calls=%async_computation.2 | async-start | bytes 2162688 | tf_op jit(solution)/shard_map/all_gather | solution.py:55
  229.4 38.8 %copy-start.1 = (s32[32,32]{1,0:T(8,128)S(1)}, s32[32,32]{1,0:T(8,128)}, u32[]{:S(2)}) copy-start(s32[32,32]{1,0:T(8,128)} %param.10) | copy-start | bytes 12292
  229.4 38.8 %copy-start.2 = (s32[32]{0:T(128)S(1)}, s32[32]{0:T(128)}, u32[]{:S(2)}) copy-start(s32[32]{0:T(128)} %param.11) | copy-start | bytes 388
  229.4 128.7 %all-to-all-start.1 = ((bf16[32,1,32,1024]{3,2,1,0:T(8,128)(2,1)}), bf16[32,1,32,1024]{3,2,1,0:T(8,128)(2,1)S(1)}, u32[]{:S(2)}, u32[]{:S(2)}) async-start(bf16[32,1,32,1024]{3,2,1,0:T(8,128)(2,1)} %copy.27), calls=%async_computation.1 | async-start | bytes 4194304 | tf_op jit(solution)/shard_map/all_to_all | solution.py:73
Sparse Core Ops, SparseCore 0:
  40.1 179.9 all-gather.2
where the time goes:
time: 369 us; the launch traced here: 368 us
  waiting for transfers between devices  269 us (73%)
  starting transfers between devices  61.2 us (17%)
  between operations  13.5 us (4%)
  matrix products  12.8 us (3%)
  local copies, waits for them, and re-layouts  6.95 us (2%)
  other arithmetic  4.86 us (1%)
    all_gather x1, waiting for transfers between devices, shards(): lax.all_gather(row_block, 'blk', axis=0, tiled=True)  123 us
    all_to_all x1, waiting for transfers between devices, shards(): lax.all_to_all(send_back, 'owner', split_axis=0, concat_axis=0, tiled=True)  89.7 us
    all_to_all x1, waiting for transfers between devices, shards(): lax.all_to_all(outgoing, 'owner', split_axis=0, concat_axis=0, tiled=True)  55.4 us
    all_to_all x1, starting transfers between devices, shards(): lax.all_to_all(send_back, 'owner', split_axis=0, concat_axis=0, tiled=True)  38.8 us
    all_to_all x1, starting transfers between devices, shards(): lax.all_to_all(outgoing, 'owner', split_axis=0, concat_axis=0, tiled=True)  22.2 us
  transfers between devices with their start and end apart: 3, of which 3 were waited for; matrix products, arithmetic and copies ran while one was open for 1% of the time, Pallas kernels for 0%

commit v1 on v0

v1 whole, which is shorter than its diff:
```python
import jax
import jax.numpy as jnp
from jax import lax
from jax.sharding import PartitionSpec as P


def shards(amplitudes, integrals, cd_tiles, cd_count, ab_tiles, ab_count):
    tile_dev, width, occ = amplitudes.shape
    owners = lax.axis_size("owner")
    own = lax.axis_index("owner")
    tasks, list_len = cd_tiles.shape
    tiles = owners * tile_dev
    positions = jnp.arange(list_len, dtype=jnp.int32)

    gathered = lax.all_gather(amplitudes, "owner", axis=0, tiled=True)

    rows = lax.all_to_all(
        integrals[0].reshape(width, list_len, width),
        "blk", split_axis=0, concat_axis=0, tiled=True,
    )
    my_ab = lax.dynamic_index_in_dim(ab_tiles, own, 0, keepdims=False)
    my_ab_live = positions < lax.dynamic_index_in_dim(ab_count, own, 0, keepdims=False)
    route = (
        (jnp.arange(owners, dtype=jnp.int32)[:, None] == (my_ab // tile_dev)[None, :])
        & my_ab_live[None, :]
    ).astype(jnp.bfloat16)
    outgoing = jnp.einsum(
        "ok,kpc->opc", route, rows, preferred_element_type=jnp.float32
    ).astype(jnp.bfloat16)
    arrived = lax.all_to_all(outgoing, "owner", split_axis=0, concat_axis=0, tiled=True)
    ab_live = positions[None, :] < ab_count[:, None]
    local_idx = jnp.arange(tile_dev, dtype=jnp.int32)
    put_ab = jnp.sum(
        (
            (ab_tiles[None] == (own * tile_dev + local_idx)[:, None, None]) & ab_live[None]
        ).astype(jnp.float32),
        axis=2,
    )
    cd_live = positions[None, :] < cd_count[:, None]
    put_cd = (
        (jnp.arange(tiles, dtype=jnp.int32)[:, None, None] == cd_tiles[None]) & cd_live[None]
    ).astype(jnp.float32)
    place = (put_ab[:, None, :, None] * put_cd[None]).astype(jnp.bfloat16)
    summed = jnp.einsum("luqp,qpc->luc", place, arrived, preferred_element_type=jnp.float32)
    high = summed.astype(jnp.bfloat16)
    low = (summed - high.astype(jnp.float32)).astype(jnp.bfloat16)
    both = jnp.stack([high, low]).reshape(2 * tile_dev, tiles * width)
    weights = lax.all_gather(both, "blk", axis=0, tiled=False)
    weights = jnp.transpose(weights, (1, 0, 2)).reshape(2 * tile_dev * width, tiles * width)
    out = jnp.dot(
        weights, gathered.reshape(tiles * width, occ), preferred_element_type=jnp.float32
    ).reshape(2, tile_dev, width, occ)
    return out[0] + out[1]


def solution(mesh):
    placed = (P("owner", None, "blk"), P("owner", "blk", None), P(), P(), P(), P())
    return jax.shard_map(
        shards, mesh=mesh, in_specs=placed, out_specs=P("owner", None, "blk"), check_vma=False
    )
```

time: 369 us -> 178 us (0.48)
  the two profiles are of different devices: /device:TPU:21 before, /device:TPU:6 now
where the time goes in v1:
time: 178 us; the launch traced here: 177 us
  blocking collectives  97.4 us (55%)
  starting transfers between devices  32 us (18%)
  waiting for transfers between devices  19.9 us (11%)
  between operations  13.5 us (8%)
  local copies, waits for them, and re-layouts  6.17 us (3%)
  other arithmetic  4.67 us (3%)
  matrix products  3.55 us (2%)
    all_gather x1, blocking collectives, shards(): weights = lax.all_gather(both, 'blk', axis=0, tiled=False)  97.4 us
    all_to_all x1, starting transfers between devices, shards(): lax.all_to_all(outgoing, 'owner', split_axis=0, concat_axis=0, tiled=True)  19.1 us
    all_to_all x1, starting transfers between devices, shards(): lax.all_to_all(integrals[0].reshape(width, list_len, width), 'blk', split...  12.9 us
    all_to_all x1, waiting for transfers between devices, shards(): lax.all_to_all(outgoing, 'owner', split_axis=0, concat_axis=0, tiled=True)  12.9 us
    all_to_all x1, waiting for transfers between devices, shards(): lax.all_to_all(integrals[0].reshape(width, list_len, width), 'blk', split...  6.31 us
  transfers between devices with their start and end apart: 3, of which 2 were waited for; matrix products, arithmetic and copies ran while one was open for 6% of the time, Pallas kernels for 0%

profile of v1, /device:TPU:6, one launch (start us, length us, event | category | flops | bytes accessed | tf_op | source)
XLA Modules:
  0.0 177.3 jit_solution(14579235212025303046)
XLA Ops:
  6.5 0.0 all-gather.2.cloned.1.call-start
  6.5 0.7 all-gather.2.cloned.1.call-update
  7.3 1.1 reshape_squeeze.3
  8.3 0.9 reshape.69
  9.2 12.9 %all-to-all-start = ((bf16[32,2,512]{2,1,0:T(2,128)(2,1)}), bf16[32,2,512]{2,1,0:T(2,128)(2,1)S(1)}, u32[]{:S(2)}, u32[]{:S(2)}) async-start(bf16[32,2,512]{2,1,0:T(2,128)(2,1)} %reshape.69), calls=%async_computation | async-start | bytes 131072 | tf_op jit(solution)/shard_map/all_to_all | solution.py:17
  22.1 1.3 dynamic_slice.9
  23.4 0.7 fusion.12
  24.1 0.6 iota_compare_fusion.4
  24.7 0.7 iota_compare_fusion.3
  25.4 0.7 iota_compare_fusion.2
  26.1 6.3 %all-to-all-done = bf16[32,2,512]{2,1,0:T(2,128)(2,1)S(1)} async-done(((bf16[32,2,512]{2,1,0:T(2,128)(2,1)}), bf16[32,2,512]{2,1,0:T(2,128)(2,1)S(1)}, u32[]{:S(2)}, u32[]{:S(2)}) %all-to-all-start) | async-done | bytes 65568 | tf_op jit(solution)/shard_map/all_to_all | solution.py:17
  32.4 0.2 reshape.70
  32.6 0.2 convolution_convert_fusion
  32.8 0.1 copy.30
  32.9 0.9 reshape.71
  33.8 19.1 %all-to-all-start.1 = ((bf16[32,2,512]{2,1,0:T(2,128)(2,1)}), bf16[32,2,512]{2,1,0:T(2,128)(2,1)S(1)}, u32[]{:S(2)}, u32[]{:S(2)}) async-start(bf16[32,2,512]{2,1,0:T(2,128)(2,1)} %reshape.71), calls=%async_computation.1 | async-start | bytes 131072 | tf_op jit(solution)/shard_map/all_to_all | solution.py:30
  52.9 0.9 convert_reduce_fusion
  53.8 0.8 copy.28
  54.6 0.3 fusion.3
  54.9 12.9 %all-to-all-done.1 = bf16[32,2,512]{2,1,0:T(2,128)(2,1)S(1)} async-done(((bf16[32,2,512]{2,1,0:T(2,128)(2,1)}), bf16[32,2,512]{2,1,0:T(2,128)(2,1)S(1)}, u32[]{:S(2)}, u32[]{:S(2)}) %all-to-all-start.1) | async-done | bytes 65568 | tf_op jit(solution)/shard_map/all_to_all | solution.py:30
  67.8 0.2 reshape.72
  68.0 0.3 copy.31
  68.3 0.4 convert_bitcast_fusion
  68.8 0.1 copy.32
  68.9 0.1 all_gather_reshape.3
  69.0 97.4 %all_gather.6 = bf16[32,4,2048]{2,1,0:T(4,128)(2,1)S(1)} all-gather(bf16[1,4,2048]{2,1,0:T(4,128)(2,1)S(1)} %all_gather_reshape.3), channel_id=1, replica_groups=mesh['blk'=32,'owner'=32] {'blk'}, dimensions={0}, use_global_device_ids=true | all-gather | bytes 540672 | tf_op jit(solution)/shard_map/all_gather | solution.py:48
  166.5 0.3 copy.33
  166.8 0.0 all-gather.2.cloned.1.call-done
  166.8 2.9 %fusion.15 = f32[128,1024]{1,0:T(8,128)S(1)} fusion(bf16[128,2048]{1,0:T(8,128)(2,1)S(1)} %bitcast.30, bf16[2048,1024]{1,0:T(8,128)(2,1)} %bitcast.29), kind=kOutput, calls=%fused_computation.30 | convolution fusion | flops 536870912 | bytes 5242880 | tf_op jit(solution)/shard_map/dot_general | solution.py:50
  169.7 0.7 slice_add_fusion
  (2 shorter events, 0.0 us)
Async XLA Ops:
  6.5 160.3 %all-gather.2.cloned.1.call-start = ((), (), s32[]{:S(2)}) async-start(), calls=%async_computation.2 | async-start | bytes 4325376 | tf_op jit(solution)/shard_map/all_gather | solution.py:15
  9.2 23.2 %all-to-all-start = ((bf16[32,2,512]{2,1,0:T(2,128)(2,1)}), bf16[32,2,512]{2,1,0:T(2,128)(2,1)S(1)}, u32[]{:S(2)}, u32[]{:S(2)}) async-start(bf16[32,2,512]{2,1,0:T(2,128)(2,1)} %reshape.69), calls=%async_computation | async-start | bytes 131072 | tf_op jit(solution)/shard_map/all_to_all | solution.py:17
  33.8 34.0 %all-to-all-start.1 = ((bf16[32,2,512]{2,1,0:T(2,128)(2,1)}), bf16[32,2,512]{2,1,0:T(2,128)(2,1)S(1)}, u32[]{:S(2)}, u32[]{:S(2)}) async-start(bf16[32,2,512]{2,1,0:T(2,128)(2,1)} %reshape.71), calls=%async_computation.1 | async-start | bytes 131072 | tf_op jit(solution)/shard_map/all_to_all | solution.py:30
Sparse Core Ops, SparseCore 0:
  11.7 113.7 all-gather.1

commit v2 on v1

v2 whole, which is shorter than its diff:
```python
import functools

import jax
import jax.numpy as jnp
from jax import lax
from jax.experimental import pallas as pl
from jax.experimental.pallas import tpu as pltpu
from jax.sharding import PartitionSpec as P

NZ, NX, NC = 4, 4, 2
SUB, LANE = 8, 128
SMEM = pl.BlockSpec(memory_space=pltpu.SMEM)
VMEM = pl.BlockSpec(memory_space=pltpu.VMEM)


def owner_index(z, x, core):
    return (z * NX + x) * NC + core


def lane_group(shape, width):
    return lax.broadcasted_iota(jnp.int32, shape, len(shape) - 1) // width


def order_columns(tiles_ref, count_ref, rows_ref, out_ref, total):
    own = lax.axis_index("owner")
    width, columns = rows_ref.shape
    list_len = tiles_ref.shape[1]
    groups = LANE // width
    total[...] = jnp.zeros_like(total)
    count = count_ref[own]
    group = lane_group((width, LANE), width)
    for place in range(list_len):
        if place % groups == 0:
            chunk = rows_ref[:, place // groups * LANE : (place // groups + 1) * LANE].astype(jnp.float32)
        owner = tiles_ref[own, place] // 2
        spot = (owner // NC) % NX
        target = owner // (NX * NC) * NC + owner % NC
        turned = pltpu.roll(chunk, (spot - place % groups + groups) % groups * width, 1)
        keep = (group == spot) & (place < count)
        total[target] += jnp.where(keep, turned, 0.0)
    for part in range(width // SUB):
        for target in range(NZ * NC):
            out_ref[part, target] = total[target, part * SUB : (part + 1) * SUB, :].astype(out_ref.dtype)


def regroup(tiles, width):
    count = len(tiles)
    group = lane_group(tiles[0].shape, width)
    results = []
    for i in range(count):
        merged = None
        for j in range(count):
            shift = (j - i) % count * width
            turned = pltpu.roll(tiles[j], shift, tiles[j].ndim - 1) if shift else tiles[j]
            merged = turned if merged is None else jnp.where(group == j, turned, merged)
        results.append(merged)
    return results


def route(tiles_ref, count_ref, rows_ref, out_ref, held):
    own = lax.axis_index("owner")
    list_len = tiles_ref.shape[1]
    held[...] = jnp.zeros_like(held)
    count = count_ref[own]
    for place in range(list_len):
        owner = tiles_ref[own, place] // 2
        held[owner] += jnp.where(place < count, rows_ref[place].astype(jnp.float32), 0.0)
    for z in range(NZ):
        for core in range(NC):
            moved = regroup([held[owner_index(z, x, core)] for x in range(NX)], LANE // NX)
            for x in range(NX):
                out_ref[owner_index(z, x, core)] = moved[x].astype(out_ref.dtype)


def accumulate(ab_ref, ab_count_ref, cd_ref, cd_count_ref, rows_ref, out_ref, mask):
    own, piece = lax.axis_index("owner"), lax.axis_index("blk")
    chunk = piece % (NZ * NC)
    z, x, core = own // (NX * NC), (own // NC) % NX, own % NC
    tasks, list_len = ab_ref.shape
    place = lax.broadcasted_iota(jnp.int32, (tasks, list_len), 1)
    ab_list = jnp.where(place < ab_count_ref[...], ab_ref[...], -1)
    cd_list = jnp.where(place < cd_count_ref[...], cd_ref[...], -1)
    cd_owner = owner_index(chunk // NC, x, chunk % NC)
    group = lane_group((tasks, LANE), LANE // NX)
    cd_hit = [
        jnp.max((cd_list == cd_owner * 2 + par).astype(jnp.float32), axis=1, keepdims=True) for par in range(2)
    ]
    for low in range(2):
        ab_hit = jnp.zeros((tasks, LANE), jnp.float32)
        for spot in range(NX):
            tile = owner_index(z, spot, core) * 2 + low
            hit = jnp.max((ab_list == tile).astype(jnp.float32), axis=1, keepdims=True)
            ab_hit = jnp.where(group == spot, hit, ab_hit)
        for par in range(2):
            mask[low * 2 + par] = ab_hit * cd_hit[par]
    totals = [jnp.zeros((SUB, LANE), jnp.float32) for _ in range(4)]
    for task in range(tasks):
        rows = rows_ref[task].astype(jnp.float32)
        for kind in range(4):
            totals[kind] += rows * mask[kind, task : task + 1, :]
    for kind in range(4):
        rounded = totals[kind].astype(out_ref.dtype)
        for target in range(out_ref.shape[0]):
            out_ref[target, kind] = rounded


def multiply(weights_ref, amps_ref, out_ref, left):
    width = amps_ref.shape[2]
    chunks = NZ * NC
    groups = LANE // width
    half = chunks // groups
    for kind in range(4):
        low, par = kind // 2, kind % 2
        for side in range(half):
            parts = []
            for part in range(width // SUB):
                tiles = [
                    weights_ref[part * chunks + side * groups + j, kind].astype(jnp.float32) for j in range(groups)
                ]
                parts.append(regroup(tiles, width))
            for spot in range(NX):
                rows = jnp.concatenate([p[spot] for p in parts], axis=0)
                row, col = (spot * 2 + low) * width, (par * half + side) * LANE
                left[row : row + width, col : col + LANE] = rows.astype(left.dtype)
    deep = chunks * width
    occ = amps_ref.shape[3]
    step = 256
    for col in range(0, occ, step):
        total = None
        for par in range(2):
            right = amps_ref[:, par, :, col : col + step].reshape(deep, step)
            term = jnp.dot(left[:, par * deep : (par + 1) * deep], right, preferred_element_type=jnp.float32)
            total = term if total is None else total + term
        out_ref[:, :, col : col + step] = total.reshape(NX, 2 * width, step).astype(out_ref.dtype)


def shards(amplitudes, integrals, cd_tiles, cd_count, ab_tiles, ab_count):
    tile_dev, width, occ = amplitudes.shape
    owners, pieces = lax.axis_size("owner"), lax.axis_size("blk")
    tasks = cd_tiles.shape[0]
    side_groups = [[owner_index(z, x, core) for z in range(NZ) for core in range(NC)] for x in range(NX)]
    x_groups = [[owner_index(z, x, core) for x in range(NX)] for z in range(NZ) for core in range(NC)]
    bf16, f32 = jnp.bfloat16, jnp.float32

    gathered = lax.all_gather(amplitudes, "owner", axis=0, tiled=True, axis_index_groups=side_groups)
    gathered = gathered.reshape(NZ * NC, tile_dev, width, occ)

    ordered = pl.pallas_call(
        order_columns,
        out_shape=jax.ShapeDtypeStruct((width // SUB, NZ * NC, SUB, LANE), bf16),
        in_specs=[SMEM, SMEM, VMEM],
        out_specs=VMEM,
        scratch_shapes=[pltpu.VMEM((NZ * NC, width, LANE), f32)],
        name="order_columns",
    )(cd_tiles, cd_count, integrals[0])
    ordered = ordered.reshape(pieces, SUB, LANE)
    mine = lax.all_to_all(ordered, "blk", split_axis=0, concat_axis=0, tiled=True)
    outgoing = pl.pallas_call(
        route,
        out_shape=jax.ShapeDtypeStruct((owners, SUB, LANE), bf16),
        in_specs=[SMEM, SMEM, VMEM],
        out_specs=VMEM,
        scratch_shapes=[pltpu.VMEM((owners, SUB, LANE), f32)],
        name="route",
    )(ab_tiles, ab_count, mine)
    arrived = lax.all_to_all(outgoing, "owner", split_axis=0, concat_axis=0, tiled=True)
    spread = pl.pallas_call(
        accumulate,
        out_shape=jax.ShapeDtypeStruct((pieces, 4, SUB, LANE), bf16),
        in_specs=[VMEM] * 5,
        out_specs=VMEM,
        scratch_shapes=[pltpu.VMEM((4, tasks, LANE), f32)],
        name="accumulate",
    )(ab_tiles, ab_count[:, None], cd_tiles, cd_count[:, None], arrived)
    weights = lax.all_to_all(spread, "blk", split_axis=0, concat_axis=0, tiled=True)
    partial = pl.pallas_call(
        multiply,
        out_shape=jax.ShapeDtypeStruct((NX, tile_dev * width, occ), f32),
        in_specs=[VMEM, VMEM],
        out_specs=VMEM,
        scratch_shapes=[pltpu.VMEM((NX * tile_dev * width, NZ * NC * tile_dev * width), bf16)],
        compiler_params=pltpu.CompilerParams(vmem_limit_bytes=32 * 1024 * 1024),
        name="multiply",
    )(weights, gathered)
    parts = lax.all_to_all(
        partial, "owner", split_axis=0, concat_axis=0, tiled=True, axis_index_groups=x_groups
    )
    return jnp.sum(parts, axis=0).reshape(tile_dev, width, occ)


def solution(mesh):
    placed = (P("owner", None, "blk"), P("owner", "blk", None), P(), P(), P(), P())
    return jax.shard_map(
        shards, mesh=mesh, in_specs=placed, out_specs=P("owner", None, "blk"), check_vma=False
    )
```

time: 178 us -> 120 us (0.67)
  blocking collectives: 97.4 us -> 61.1 us
  starting transfers between devices: 32 us -> 19.1 us
  waiting for transfers between devices: 19.9 us -> 12.3 us
  Pallas kernels: 0 us -> 6.63 us
  other arithmetic: 4.67 us -> 0.77 us
  matrix products: 3.55 us -> 0 us
    all_gather x1 -> x0, blocking collectives: 97.4 us -> none  [shards(): weights = lax.all_gather(both, 'blk', axis=0, tiled=False)]
    all_to_all x0 -> x3, blocking collectives: none -> 61.1 us  [the longest x1 23.3 us: shards(): lax.all_to_all(ordered, 'blk', split_axis=0, concat_axis=0, tiled=True)]
    all_to_all x1 -> x0, starting transfers between devices: 12.9 us -> none  [shards(): lax.all_to_all(integrals[0].reshape(width, list_len, width), 'blk', split...]
    pallas_call x0 -> x4, Pallas kernels: none -> 6.63 us  [the longest x1 2.29 us: shards(): pl.pallas_call(order_columns, out_shape=jax.ShapeDtypeStruct((width // SU...]
    all_to_all x1 -> x0, waiting for transfers between devices: 6.31 us -> none  [shards(): lax.all_to_all(integrals[0].reshape(width, list_len, width), 'blk', split...]
    dot_general x3 -> x0, matrix products: 3.55 us -> none  [the longest x1 2.9 us: shards(): jnp.dot(weights, gathered.reshape(tiles * width, occ), preferred_element_...]
    lt x3 -> x0, other arithmetic: 2 us -> none  [the longest x1 0.73 us: shards(): ab_live = positions[None, :] < ab_count[:, None]]
  transfers between devices with their start and end apart: 3 -> 2, of which waited for: 2 -> 1; matrix products, arithmetic and copies ran while one was open for 6% -> 1% of each run, Pallas kernels for 0% -> 5%
where the time goes in v2:
time: 120 us; the launch traced here: 118 us
  blocking collectives  61.1 us (51%)
  starting transfers between devices  19.1 us (16%)
  between operations  13.4 us (11%)
  waiting for transfers between devices  12.3 us (10%)
  Pallas kernels  6.63 us (6%)
  local copies, waits for them, and re-layouts  4.53 us (4%)
    all_to_all x1, blocking collectives, shards(): lax.all_to_all(ordered, 'blk', split_axis=0, concat_axis=0, tiled=True)  23.3 us
    all_to_all x1, blocking collectives, shards(): lax.all_to_all(spread, 'blk', split_axis=0, concat_axis=0, tiled=True)  20.8 us
    all_to_all x1, starting transfers between devices, shards(): lax.all_to_all(outgoing, 'owner', split_axis=0, concat_axis=0, tiled=True)  19.1 us
    all_to_all x1, blocking collectives, shards(): lax.all_to_all(partial, 'owner', split_axis=0, concat_axis=0, tiled=True,...  17 us
    all_to_all x1, waiting for transfers between devices, shards(): lax.all_to_all(outgoing, 'owner', split_axis=0, concat_axis=0, tiled=True)  11.6 us
    unnamed x8, local copies, waits for them, and re-layouts  3.15 us
  transfers between devices with their start and end apart: 2, of which 1 were waited for; matrix products, arithmetic and copies ran while one was open for 1% of the time, Pallas kernels for 5%

profile of v2, /device:TPU:6, one launch (start us, length us, event | category | flops | bytes accessed | tf_op | source)
XLA Modules:
  0.0 117.9 jit_solution(17244941820288799931)
XLA Ops:
  6.5 0.0 all-gather.2.cloned.1.call-start
  6.5 0.7 all-gather.2.cloned.1.call-update
  7.3 2.3 %order_columns.1 = bf16[4,8,8,128]{3,2,1,0:T(8,128)(2,1)} custom-call(s32[32,32]{1,0:T(8,128)} %cd_ref.1, s32[32]{0:T(128)} %count_ref.2, bf16[32,1024]{1,0:T(8,128)(2,1)} %bitcast.8), custom_call_target="tpu_custom_call" | custom-call | tf_op jit(solution)/shard_map/order_columns/pallas_call | solution.py:148
  9.5 23.3 %all_to_all.20.rows_ref = bf16[32,8,128]{2,1,0:T(8,128)(2,1)} all-to-all(bf16[32,8,128]{2,1,0:T(8,128)(2,1)} %bitcast.7), channel_id=1, replica_groups=mesh['blk'=32,'owner'=32] {'blk'}, dimensions={0} | all-to-all | bytes 131072 | tf_op jit(solution)/shard_map/all_to_all | solution.py:157
  32.9 1.9 %route.1 = bf16[32,8,128]{2,1,0:T(8,128)(2,1)} custom-call(s32[32,32]{1,0:T(8,128)} %ab_ref.1, s32[32]{0:T(128)} %count_ref.3, bf16[32,8,128]{2,1,0:T(8,128)(2,1)} %all_to_all.20.rows_ref), custom_call_target="tpu_custom_call" | custom-call | tf_op jit(solution)/shard_map/route/pallas_call | solution.py:158
  34.8 19.1 %all-to-all-start.1 = ((bf16[32,8,128]{2,1,0:T(8,128)(2,1)}), bf16[32,8,128]{2,1,0:T(8,128)(2,1)S(1)}, u32[]{:S(2)}, u32[]{:S(2)}) async-start(bf16[32,8,128]{2,1,0:T(8,128)(2,1)} %route.1), calls=%async_computation.1 | async-start | bytes 131072 | tf_op jit(solution)/shard_map/all_to_all | solution.py:166
  53.9 0.0 copy-start.2
  53.9 0.6 copy-done.2
  54.5 0.7 copy.9.ab_count_ref
  55.2 0.0 copy-start.3
  55.2 0.7 copy-done.3
  55.9 0.7 copy.10.cd_count_ref
  56.6 11.6 %all-to-all-done.1.rows_ref = bf16[32,8,128]{2,1,0:T(8,128)(2,1)S(1)} async-done(((bf16[32,8,128]{2,1,0:T(8,128)(2,1)}), bf16[32,8,128]{2,1,0:T(8,128)(2,1)S(1)}, u32[]{:S(2)}, u32[]{:S(2)}) %all-to-all-start.1) | async-done | bytes 65568 | tf_op jit(solution)/shard_map/all_to_all | solution.py:166
  68.2 0.0 copy-start.1
  68.2 0.6 copy-done.1
  68.8 1.9 %accumulate.1 = bf16[32,4,8,128]{3,2,1,0:T(8,128)(2,1)} custom-call(s32[32,32]{1,0:T(8,128)} %ab_ref.1, s32[32,1]{1,0:T(8,128)} %copy.9.ab_count_ref, s32[32,32]{1,0:T(8,128)} %cd_ref.1, s32[32,1]{1,0:T(8,128)} %copy.10.cd_count_ref, bf16[32,8,128]{2,1,0:T(8,128)(2,1)} %copy-done.1), custom_call_target="tpu_custom_call" | custom-call | tf_op jit(solution)/shard_map/accumulate/pallas_call | solution.py:167
  70.7 20.8 %all_to_all.21.weights_ref = bf16[32,4,8,128]{3,2,1,0:T(8,128)(2,1)S(1)} all-to-all(bf16[32,4,8,128]{3,2,1,0:T(8,128)(2,1)} %accumulate.1), channel_id=1, replica_groups=mesh['blk'=32,'owner'=32] {'blk'}, dimensions={0} | all-to-all | bytes 524288 | tf_op jit(solution)/shard_map/all_to_all | solution.py:175
  91.5 0.0 all-gather.2.cloned.1.call-done
  91.5 0.0 copy-start
  91.5 1.2 %copy-done = bf16[16,32,1024]{2,1,0:T(8,128)(2,1)S(1)} copy-done((bf16[16,32,1024]{2,1,0:T(8,128)(2,1)S(1)}, bf16[16,32,1024]{2,1,0:T(8,128)(2,1)}, u32[]{:S(2)}) %copy-start) | copy-done | bytes 1048600
  92.7 0.6 multiply.1
  93.3 17.0 %all_to_all.22 = f32[4,64,1024]{2,1,0:T(8,128)S(1)} all-to-all(f32[4,64,1024]{2,1,0:T(8,128)S(1)} %multiply.1), channel_id=1, replica_groups={{0,2,4,6},{1,3,5,7},{8,10,12,14},{9,11,13,15},{16,18,20,22},{17,19,21,2..., dimensions={0} | all-to-all | bytes 2097152 | tf_op jit(solution)/shard_map/all_to_all | solution.py:185
  110.3 0.8 reduce_sum.9
Async XLA Ops:
  6.5 85.0 %all-gather.2.cloned.1.call-start = ((), (), s32[]{:S(2)}) async-start(), calls=%async_computation.4 | async-start | bytes 1179648 | tf_op jit(solution)/shard_map/all_gather | solution.py:145
  34.8 33.4 %all-to-all-start.1 = ((bf16[32,8,128]{2,1,0:T(8,128)(2,1)}), bf16[32,8,128]{2,1,0:T(8,128)(2,1)S(1)}, u32[]{:S(2)}, u32[]{:S(2)}) async-start(bf16[32,8,128]{2,1,0:T(8,128)(2,1)} %route.1), calls=%async_computation.1 | async-start | bytes 131072 | tf_op jit(solution)/shard_map/all_to_all | solution.py:166
  53.9 0.7 copy-start.2
  55.2 0.7 copy-start.3
  68.2 0.6 copy-start.1
  91.5 1.2 %copy-start = (bf16[16,32,1024]{2,1,0:T(8,128)(2,1)S(1)}, bf16[16,32,1024]{2,1,0:T(8,128)(2,1)}, u32[]{:S(2)}) copy-start(bf16[16,32,1024]{2,1,0:T(8,128)(2,1)} %all-gather.2.cloned.1.call-done) | copy-start | bytes 3145732
Sparse Core Ops, SparseCore 0:
  10.1 61.5 all-gather.1

commit v3 on v2

--- a/solution.py
+++ b/solution.py
@@ -11,6 +11,8 @@
 SUB, LANE = 8, 128
 SMEM = pl.BlockSpec(memory_space=pltpu.SMEM)
 VMEM = pl.BlockSpec(memory_space=pltpu.VMEM)
+ANY = pl.BlockSpec(memory_space=pl.ANY)
+STEPS = (0, -1, 1, 2)
 
 
 def owner_index(z, x, core):
@@ -57,7 +59,8 @@
     return results
 
 
-def route(tiles_ref, count_ref, rows_ref, out_ref, held):
+def route(tiles_ref, count_ref, rows_ref, *rest):
+    out_ref, held = rest[-2:]
     own = lax.axis_index("owner")
     list_len = tiles_ref.shape[1]
     held[...] = jnp.zeros_like(held)
@@ -72,7 +75,8 @@
                 out_ref[owner_index(z, x, core)] = moved[x].astype(out_ref.dtype)
 
 
-def accumulate(ab_ref, ab_count_ref, cd_ref, cd_count_ref, rows_ref, out_ref, mask):
+def accumulate(ab_ref, ab_count_ref, cd_ref, cd_count_ref, rows_ref, *rest):
+    out_ref, mask = rest[-2:]
     own, piece = lax.axis_index("owner"), lax.axis_index("blk")
     chunk = piece % (NZ * NC)
     z, x, core = own // (NX * NC), (own // NC) % NX, own % NC
@@ -104,46 +108,53 @@
             out_ref[target, kind] = rounded
 
 
-def multiply(weights_ref, amps_ref, out_ref, left):
-    width = amps_ref.shape[2]
+def multiply(weights_ref, own_ref, other_ref, out_ref, left):
+    own = lax.axis_index("owner")
+    z, core = own // (NX * NC), own % NC
+    width, occ = own_ref.shape[2:]
     chunks = NZ * NC
-    groups = LANE // width
-    half = chunks // groups
     for kind in range(4):
         low, par = kind // 2, kind % 2
-        for side in range(half):
+        for side in range(NC):
             parts = []
             for part in range(width // SUB):
-                tiles = [
-                    weights_ref[part * chunks + side * groups + j, kind].astype(jnp.float32) for j in range(groups)
-                ]
+                tiles = []
+                for step in STEPS:
+                    chunk = (z + step + NZ) % NZ * NC + (core + side) % NC
+                    tiles.append(weights_ref[part * chunks + chunk, kind].astype(jnp.float32))
                 parts.append(regroup(tiles, width))
             for spot in range(NX):
                 rows = jnp.concatenate([p[spot] for p in parts], axis=0)
-                row, col = (spot * 2 + low) * width, (par * half + side) * LANE
+                row, col = (spot * 2 + low) * width, (par * NC + side) * LANE
                 left[row : row + width, col : col + LANE] = rows.astype(left.dtype)
-    deep = chunks * width
-    occ = amps_ref.shape[3]
-    step = 256
-    for col in range(0, occ, step):
+    wide = 256
+    for col in range(0, occ, wide):
         total = None
         for par in range(2):
-            right = amps_ref[:, par, :, col : col + step].reshape(deep, step)
-            term = jnp.dot(left[:, par * deep : (par + 1) * deep], right, preferred_element_type=jnp.float32)
-            total = term if total is None else total + term
-        out_ref[:, :, col : col + step] = total.reshape(NX, 2 * width, step).astype(out_ref.dtype)
+            for side, amps in enumerate((own_ref, other_ref)):
+                right = amps[:, par, :, col : col + wide].reshape(LANE, wide)
+                at = (par * NC + side) * LANE
+                term = jnp.dot(left[:, at : at + LANE], right, preferred_element_type=jnp.float32)
+                total = term if total is None else total + term
+        out_ref[:, :, col : col + wide] = total.reshape(NX, 2 * width, wide).astype(out_ref.dtype)
+
+
+def moved(block, dz, dcore=0):
+    pairs = [
+        (owner_index(z, x, core), owner_index((z + dz) % NZ, x, (core + dcore) % NC))
+        for z in range(NZ)
+        for x in range(NX)
+        for core in range(NC)
+    ]
+    return lax.ppermute(block, "owner", pairs)
 
 
 def shards(amplitudes, integrals, cd_tiles, cd_count, ab_tiles, ab_count):
     tile_dev, width, occ = amplitudes.shape
     owners, pieces = lax.axis_size("owner"), lax.axis_size("blk")
     tasks = cd_tiles.shape[0]
-    side_groups = [[owner_index(z, x, core) for z in range(NZ) for core in range(NC)] for x in range(NX)]
     x_groups = [[owner_index(z, x, core) for x in range(NX)] for z in range(NZ) for core in range(NC)]
     bf16, f32 = jnp.bfloat16, jnp.float32
-
-    gathered = lax.all_gather(amplitudes, "owner", axis=0, tiled=True, axis_index_groups=side_groups)
-    gathered = gathered.reshape(NZ * NC, tile_dev, width, occ)
 
     ordered = pl.pallas_call(
         order_columns,
@@ -155,33 +166,37 @@
     )(cd_tiles, cd_count, integrals[0])
     ordered = ordered.reshape(pieces, SUB, LANE)
     mine = lax.all_to_all(ordered, "blk", split_axis=0, concat_axis=0, tiled=True)
+    below, above = moved(amplitudes, 1), moved(amplitudes, NZ - 1)
     outgoing = pl.pallas_call(
         route,
         out_shape=jax.ShapeDtypeStruct((owners, SUB, LANE), bf16),
-        in_specs=[SMEM, SMEM, VMEM],
+        in_specs=[SMEM, SMEM, VMEM, ANY, ANY],
         out_specs=VMEM,
         scratch_shapes=[pltpu.VMEM((owners, SUB, LANE), f32)],
         name="route",
-    )(ab_tiles, ab_count, mine)
+    )(ab_tiles, ab_count, mine, below, above)
     arrived = lax.all_to_all(outgoing, "owner", split_axis=0, concat_axis=0, tiled=True)
+    far = (moved(above[:1], NZ - 1), moved(below[1:], 1))
     spread = pl.pallas_call(
         accumulate,
         out_shape=jax.ShapeDtypeStruct((pieces, 4, SUB, LANE), bf16),
-        in_specs=[VMEM] * 5,
+        in_specs=[VMEM] * 5 + [ANY] * 2,
         out_specs=VMEM,
         scratch_shapes=[pltpu.VMEM((4, tasks, LANE), f32)],
         name="accumulate",
-    )(ab_tiles, ab_count[:, None], cd_tiles, cd_count[:, None], arrived)
+    )(ab_tiles, ab_count[:, None], cd_tiles, cd_count[:, None], arrived, *far)
     weights = lax.all_to_all(spread, "blk", split_axis=0, concat_axis=0, tiled=True)
+    own_side = jnp.concatenate([amplitudes, below, above, *far], axis=0).reshape(NZ, tile_dev, width, occ)
+    other_side = moved(own_side, 0, 1)
     partial = pl.pallas_call(
         multiply,
         out_shape=jax.ShapeDtypeStruct((NX, tile_dev * width, occ), f32),
-        in_specs=[VMEM, VMEM],
+        in_specs=[VMEM, VMEM, VMEM],
         out_specs=VMEM,
         scratch_shapes=[pltpu.VMEM((NX * tile_dev * width, NZ * NC * tile_dev * width), bf16)],
         compiler_params=pltpu.CompilerParams(vmem_limit_bytes=32 * 1024 * 1024),
         name="multiply",
-    )(weights, gathered)
+    )(weights, own_side, other_side)
     parts = lax.all_to_all(
         partial, "owner", split_axis=0, concat_axis=0, tiled=True, axis_index_groups=x_groups
     )

time: 120 us -> 125 us (1.042)
  starting transfers between devices: 19.1 us -> 64.4 us
  blocking collectives: 61.1 us -> 16.3 us
  waiting for transfers between devices: 12.3 us -> 28.3 us
  between operations: 13.4 us -> 0.18 us
  local copies, waits for them, and re-layouts: 4.53 us -> 6.23 us
    all_to_all x2 -> x0, blocking collectives: 44.1 us -> none  [the longest x1 23.3 us: shards(): lax.all_to_all(ordered, 'blk', split_axis=0, concat_axis=0, tiled=True)]
    ppermute x0 -> x5, starting transfers between devices: none -> 29.1 us  [moved(): return lax.ppermute(block, 'owner', pairs)]
    ppermute x0 -> x5, waiting for transfers between devices: none -> 21.7 us  [moved(): return lax.ppermute(block, 'owner', pairs)]
    all_to_all x0 -> x2, starting transfers between devices: none -> 20.2 us  [the longest x1 12.9 us: shards(): lax.all_to_all(ordered, 'blk', split_axis=0, concat_axis=0, tiled=True)]
    all_to_all x1, waiting for transfers between devices: 11.6 us -> 0.01 us  [shards(): lax.all_to_all(outgoing, 'owner', split_axis=0, concat_axis=0, tiled=True)]
    all_to_all x0 -> x2, waiting for transfers between devices: none -> 6.63 us  [the longest x1 6.63 us: shards(): lax.all_to_all(spread, 'blk', split_axis=0, concat_axis=0, tiled=True)]
    all_to_all x1, starting transfers between devices: 19.1 us -> 15.2 us  [shards(): lax.all_to_all(outgoing, 'owner', split_axis=0, concat_axis=0, tiled=True)]
    unnamed x8 -> x30, local copies, waits for them, and re-layouts: 3.15 us -> 4.84 us
  transfers between devices with their start and end apart: 2 -> 8, of which waited for: 1 -> 6; matrix products, arithmetic and copies ran while one was open for 1% -> 1% of each run, Pallas kernels for 5% -> 0%
where the time goes in v3:
time: 125 us; the launch traced here: 123 us
  starting transfers between devices  64.4 us (52%)
  waiting for transfers between devices  28.3 us (23%)
  blocking collectives  16.3 us (13%)
  Pallas kernels  6.91 us (6%)
  local copies, waits for them, and re-layouts  6.23 us (5%)
    ppermute x5, starting transfers between devices, moved(): return lax.ppermute(block, 'owner', pairs)  29.1 us
    ppermute x5, waiting for transfers between devices, moved(): return lax.ppermute(block, 'owner', pairs)  21.7 us
    all_to_all x1, blocking collectives, shards(): lax.all_to_all(partial, 'owner', split_axis=0, concat_axis=0, tiled=True,...  16.3 us
    all_to_all x1, starting transfers between devices, shards(): lax.all_to_all(outgoing, 'owner', split_axis=0, concat_axis=0, tiled=True)  15.2 us
    all_to_all x1, starting transfers between devices, shards(): lax.all_to_all(ordered, 'blk', split_axis=0, concat_axis=0, tiled=True)  12.9 us
    all_to_all x1, starting transfers between devices, shards(): lax.all_to_all(spread, 'blk', split_axis=0, concat_axis=0, tiled=True)  7.27 us
    all_to_all x1, waiting for transfers between devices, shards(): lax.all_to_all(spread, 'blk', split_axis=0, concat_axis=0, tiled=True)  6.63 us
    unnamed x30, local copies, waits for them, and re-layouts  4.84 us
  transfers between devices with their start and end apart: 8, of which 6 were waited for; matrix products, arithmetic and copies ran while one was open for 1% of the time, Pallas kernels for 0%

profile of v3, /device:TPU:6, one launch (start us, length us, event | category | flops | bytes accessed | tf_op | source)
XLA Modules:
  0.0 123.1 jit_solution(17230262848755820789)
XLA Ops:
  0.0 0.0 copy-start.10
  0.0 2.4 %order_columns.1 = bf16[4,8,8,128]{3,2,1,0:T(8,128)(2,1)} custom-call(s32[32,32]{1,0:T(8,128)} %cd_ref.1, s32[32]{0:T(128)} %count_ref.2, bf16[32,1024]{1,0:T(8,128)(2,1)} %bitcast.9), custom_call_target="tpu_custom_call" | custom-call | tf_op jit(solution)/shard_map/order_columns/pallas_call | solution.py:159
  2.4 12.9 %all-to-all-start = ((bf16[32,8,128]{2,1,0:T(8,128)(2,1)}), bf16[32,8,128]{2,1,0:T(8,128)(2,1)S(1)}, u32[]{:S(2)}, u32[]{:S(2)}) async-start(bf16[32,8,128]{2,1,0:T(8,128)(2,1)} %bitcast.8), calls=%async_computation | async-start | bytes 131072 | tf_op jit(solution)/shard_map/all_to_all | solution.py:168
  15.3 0.0 copy-done.10
  15.3 10.9 %collective-permute-start = (bf16[2,32,1024]{2,1,0:T(8,128)(2,1)S(1)}, bf16[2,32,1024]{2,1,0:T(8,128)(2,1)S(1)}, u32[]{:S(2)}, u32[]{:S(2)}) collective-permute-start(bf16[2,32,1024]{2,1,0:T(8,128)(2,1)S(1)} %copy-done.10), channel_id=1, source_target_pairs={{0,8},{1,9},{2,10},{3,11},{4,12},{5,13},{6,14},{7,15},{8,16},{9,17... | collective-permute-start | bytes 393224 | tf_op jit(solution)/shard_map/ppermute | solution.py:149
  26.3 6.5 %collective-permute-start.1 = (bf16[2,32,1024]{2,1,0:T(8,128)(2,1)S(1)}, bf16[2,32,1024]{2,1,0:T(8,128)(2,1)S(1)}, u32[]{:S(2)}, u32[]{:S(2)}) collective-permute-start(bf16[2,32,1024]{2,1,0:T(8,128)(2,1)S(1)} %copy-done.10), channel_id=1, source_target_pairs={{0,24},{1,25},{2,26},{3,27},{4,28},{5,29},{6,30},{7,31},{8,0},{9,1... | collective-permute-start | bytes 393224 | tf_op jit(solution)/shard_map/ppermute | solution.py:149
  32.8 1.4 %collective-permute-done.rest_0_ = bf16[2,32,1024]{2,1,0:T(8,128)(2,1)S(1)} collective-permute-done((bf16[2,32,1024]{2,1,0:T(8,128)(2,1)S(1)}, bf16[2,32,1024]{2,1,0:T(8,128)(2,1)S(1)}, u32[]{:S(2)}, u32[]{:S(2)}) %collective-permute-start) | collective-permute-done | bytes 131104 | tf_op jit(solution)/shard_map/ppermute | solution.py:149
  34.1 0.0 copy-start
  34.1 10.5 %collective-permute-done.1.rest_1_ = bf16[2,32,1024]{2,1,0:T(8,128)(2,1)S(1)} collective-permute-done((bf16[2,32,1024]{2,1,0:T(8,128)(2,1)S(1)}, bf16[2,32,1024]{2,1,0:T(8,128)(2,1)S(1)}, u32[]{:S(2)}, u32[]{:S(2)}) %collective-permute-start.1) | collective-permute-done | bytes 131104 | tf_op jit(solution)/shard_map/ppermute | solution.py:149
  44.6 0.0 copy-start.2
  44.6 0.0 all-to-all-done.rows_ref
  44.6 0.0 copy-done
  44.6 0.6 copy-done.2
  45.2 0.0 copy-start.4
  45.2 0.6 copy-done.4
  45.9 1.9 %route.1 = bf16[32,8,128]{2,1,0:T(8,128)(2,1)} custom-call(s32[32,32]{1,0:T(8,128)} %ab_ref.1, s32[32]{0:T(128)} %count_ref.3, bf16[32,8,128]{2,1,0:T(8,128)(2,1)} %copy-done.4, bf16[2,32,1024]{2,1,0:T(8,128)(2,1)} %copy-done, bf16[2,32,1024]{2,1,0:T(8,128)(2,1)} %copy-done.2), custom_call_target="tpu_custom_call" | custom-call | tf_op jit(solution)/shard_map/route/pallas_call | solution.py:170
  47.7 0.0 copy-start.1
  47.7 0.0 copy-start.3
  47.7 15.2 %all-to-all-start.1 = ((bf16[32,8,128]{2,1,0:T(8,128)(2,1)}), bf16[32,8,128]{2,1,0:T(8,128)(2,1)S(1)}, u32[]{:S(2)}, u32[]{:S(2)}) async-start(bf16[32,8,128]{2,1,0:T(8,128)(2,1)} %route.1), calls=%async_computation.1 | async-start | bytes 131072 | tf_op jit(solution)/shard_map/all_to_all | solution.py:178
  62.9 0.0 copy-done.1
  62.9 7.3 %collective-permute-start.3 = (bf16[1,32,1024]{2,1,0:T(8,128)(2,1)S(1)}, bf16[1,32,1024]{2,1,0:T(8,128)(2,1)S(1)}, u32[]{:S(2)}, u32[]{:S(2)}) collective-permute-start(bf16[1,32,1024]{2,1,0:T(8,128)(2,1)S(1)} %slice.9), channel_id=1, source_target_pairs={{0,8},{1,9},{2,10},{3,11},{4,12},{5,13},{6,14},{7,15},{8,16},{9,17... | collective-permute-start | bytes 196616 | tf_op jit(solution)/shard_map/ppermute | solution.py:149
  70.2 0.0 copy-done.3
  70.2 0.0 copy-start.11
  70.3 2.5 %collective-permute-start.2 = (bf16[1,32,1024]{2,1,0:T(8,128)(2,1)S(1)}, bf16[1,32,1024]{2,1,0:T(8,128)(2,1)S(1)}, u32[]{:S(2)}, u32[]{:S(2)}) collective-permute-start(bf16[1,32,1024]{2,1,0:T(8,128)(2,1)S(1)} %slice.8), channel_id=1, source_target_pairs={{0,24},{1,25},{2,26},{3,27},{4,28},{5,29},{6,30},{7,31},{8,0},{9,1... | collective-permute-start | bytes 196616 | tf_op jit(solution)/shard_map/ppermute | solution.py:149
  72.7 0.0 copy-done.11
  72.7 0.7 copy.7.ab_count_ref
  73.4 0.0 copy-start.12
  73.4 0.7 copy-done.12
  74.1 0.7 copy.8.cd_count_ref
  74.8 2.3 %collective-permute-done.3.rest_1_ = bf16[1,32,1024]{2,1,0:T(8,128)(2,1)S(1)} collective-permute-done((bf16[1,32,1024]{2,1,0:T(8,128)(2,1)S(1)}, bf16[1,32,1024]{2,1,0:T(8,128)(2,1)S(1)}, u32[]{:S(2)}, u32[]{:S(2)}) %collective-permute-start.3) | collective-permute-done | bytes 65568 | tf_op jit(solution)/shard_map/ppermute | solution.py:149
  77.0 0.0 copy-start.5
  77.0 5.7 %collective-permute-done.2.rest_0_ = bf16[1,32,1024]{2,1,0:T(8,128)(2,1)S(1)} collective-permute-done((bf16[1,32,1024]{2,1,0:T(8,128)(2,1)S(1)}, bf16[1,32,1024]{2,1,0:T(8,128)(2,1)S(1)}, u32[]{:S(2)}, u32[]{:S(2)}) %collective-permute-start.2) | collective-permute-done | bytes 65568 | tf_op jit(solution)/shard_map/ppermute | solution.py:149
  82.8 0.0 copy-start.7
  82.8 0.0 all-to-all-done.1.rows_ref
  82.8 0.0 copy-done.5
  82.8 0.6 copy-done.7
  83.4 0.0 copy-start.9
  83.4 0.6 copy-done.9
  84.0 1.9 %accumulate.1 = bf16[32,4,8,128]{3,2,1,0:T(8,128)(2,1)} custom-call(s32[32,32]{1,0:T(8,128)} %ab_ref.1, s32[32,1]{1,0:T(8,128)} %copy.7.ab_count_ref, s32[32,32]{1,0:T(8,128)} %cd_ref.1, s32[32,1]{1,0:T(8,128)} %copy.8.cd_count_ref, bf16[32,8,128]{2,1,0:T(8,128)(2,1)} %copy-done.9, bf16[1,32,1024]{2,1,0:T(8,128)(2,1)} %copy-done.7, ...), custom_call_target="tpu_custom_call" | custom-call | tf_op jit(solution)/shard_map/accumulate/pallas_call | solution.py:180
  85.8 7.3 %all-to-all-start.2 = ((bf16[32,4,8,128]{3,2,1,0:T(8,128)(2,1)}), bf16[32,4,8,128]{3,2,1,0:T(8,128)(2,1)S(1)}, u32[]{:S(2)}, u32[]{:S(2)}) async-start(bf16[32,4,8,128]{3,2,1,0:T(8,128)(2,1)} %accumulate.1), calls=%async_computation.2 | async-start | bytes 524288 | tf_op jit(solution)/shard_map/all_to_all | solution.py:188
  93.2 0.0 copy-start.8
  93.2 0.8 copy-done.8
  94.0 0.0 copy-start.6
  94.0 0.8 copy-done.6
  94.8 1.9 %collective-permute-start.4 = (bf16[4,2,32,1024]{3,2,1,0:T(8,128)(2,1)S(1)}, bf16[4,2,32,1024]{3,2,1,0:T(8,128)(2,1)S(1)}, u32[]{:S(2)}, u32[]{:S(2)}) collective-permute-start(bf16[4,2,32,1024]{3,2,1,0:T(8,128)(2,1)S(1)} %bitcast.6), channel_id=1, source_target_pairs={{0,1},{1,0},{2,3},{3,2},{4,5},{5,4},{6,7},{7,6},{8,9},{9,8},{10,11... | collective-permute-start | bytes 1572872 | tf_op jit(solution)/shard_map/ppermute | solution.py:149
  96.8 1.9 %collective-permute-done.4.other_ref = bf16[4,2,32,1024]{3,2,1,0:T(8,128)(2,1)S(1)} collective-permute-done((bf16[4,2,32,1024]{3,2,1,0:T(8,128)(2,1)S(1)}, bf16[4,2,32,1024]{3,2,1,0:T(8,128)(2,1)S(1)}, u32[]{:S(2)}, u32[]{:S(2)}) %collective-permute-start.4) | collective-permute-done | bytes 524320 | tf_op jit(solution)/shard_map/ppermute | solution.py:149
  98.6 6.6 %all-to-all-done.2.weights_ref = bf16[32,4,8,128]{3,2,1,0:T(8,128)(2,1)S(1)} async-done(((bf16[32,4,8,128]{3,2,1,0:T(8,128)(2,1)}), bf16[32,4,8,128]{3,2,1,0:T(8,128)(2,1)S(1)}, u32[]{:S(2)}, u32[]{:S(2)}) %all-to-all-start.2) | async-done | bytes 262176 | tf_op jit(solution)/shard_map/all_to_all | solution.py:188
  105.3 0.8 multiply.1
  106.1 16.3 %all_to_all.20 = f32[4,64,1024]{2,1,0:T(8,128)S(1)} all-to-all(f32[4,64,1024]{2,1,0:T(8,128)S(1)} %multiply.1), channel_id=1, replica_groups={{0,2,4,6},{1,3,5,7},{8,10,12,14},{9,11,13,15},{16,18,20,22},{17,19,21,2..., dimensions={0} | all-to-all | bytes 2097152 | tf_op jit(solution)/shard_map/all_to_all | solution.py:200
  122.4 0.8 reduce_sum.9
  (7 shorter events, 0.1 us)
Async XLA Ops:
  0.0 15.3 %copy-start.10 = (bf16[2,32,1024]{2,1,0:T(8,128)(2,1)S(1)}, bf16[2,32,1024]{2,1,0:T(8,128)(2,1)}, u32[]{:S(2)}) copy-start(bf16[2,32,1024]{2,1,0:T(8,128)(2,1)} %param.6) | copy-start | bytes 393220
  2.4 42.2 %all-to-all-start = ((bf16[32,8,128]{2,1,0:T(8,128)(2,1)}), bf16[32,8,128]{2,1,0:T(8,128)(2,1)S(1)}, u32[]{:S(2)}, u32[]{:S(2)}) async-start(bf16[32,8,128]{2,1,0:T(8,128)(2,1)} %bitcast.8), calls=%async_computation | async-start | bytes 131072 | tf_op jit(solution)/shard_map/all_to_all | solution.py:168
  15.3 18.8 %collective-permute-start = (bf16[2,32,1024]{2,1,0:T(8,128)(2,1)S(1)}, bf16[2,32,1024]{2,1,0:T(8,128)(2,1)S(1)}, u32[]{:S(2)}, u32[]{:S(2)}) collective-permute-start(bf16[2,32,1024]{2,1,0:T(8,128)(2,1)S(1)} %copy-done.10), channel_id=1, source_target_pairs={{0,8},{1,9},{2,10},{3,11},{4,12},{5,13},{6,14},{7,15},{8,16},{9,17... | collective-permute-start | bytes 393224 | tf_op jit(solution)/shard_map/ppermute | solution.py:149
  26.3 18.3 %collective-permute-start.1 = (bf16[2,32,1024]{2,1,0:T(8,128)(2,1)S(1)}, bf16[2,32,1024]{2,1,0:T(8,128)(2,1)S(1)}, u32[]{:S(2)}, u32[]{:S(2)}) collective-permute-start(bf16[2,32,1024]{2,1,0:T(8,128)(2,1)S(1)} %copy-done.10), channel_id=1, source_target_pairs={{0,24},{1,25},{2,26},{3,27},{4,28},{5,29},{6,30},{7,31},{8,0},{9,1... | collective-permute-start | bytes 393224 | tf_op jit(solution)/shard_map/ppermute | solution.py:149
  34.1 10.5 %copy-start = (bf16[2,32,1024]{2,1,0:T(8,128)(2,1)}, bf16[2,32,1024]{2,1,0:T(8,128)(2,1)S(1)}, u32[]{:S(2)}) copy-start(bf16[2,32,1024]{2,1,0:T(8,128)(2,1)S(1)} %collective-permute-done.rest_0_) | copy-start | bytes 393220
  44.6 0.6 copy-start.2
  45.2 0.6 copy-start.4
  47.7 15.2 %copy-start.1 = (bf16[2,32,1024]{2,1,0:T(8,128)(2,1)S(1)}, bf16[2,32,1024]{2,1,0:T(8,128)(2,1)}, u32[]{:S(2)}) copy-start(bf16[2,32,1024]{2,1,0:T(8,128)(2,1)} %copy-done) | copy-start | bytes 393220
  47.7 22.5 %copy-start.3 = (bf16[2,32,1024]{2,1,0:T(8,128)(2,1)S(1)}, bf16[2,32,1024]{2,1,0:T(8,128)(2,1)}, u32[]{:S(2)}) copy-start(bf16[2,32,1024]{2,1,0:T(8,128)(2,1)} %copy-done.2) | copy-start | bytes 393220
  47.7 35.0 %all-to-all-start.1 = ((bf16[32,8,128]{2,1,0:T(8,128)(2,1)}), bf16[32,8,128]{2,1,0:T(8,128)(2,1)S(1)}, u32[]{:S(2)}, u32[]{:S(2)}) async-start(bf16[32,8,128]{2,1,0:T(8,128)(2,1)} %route.1), calls=%async_computation.1 | async-start | bytes 131072 | tf_op jit(solution)/shard_map/all_to_all | solution.py:178
  62.9 14.1 %collective-permute-start.3 = (bf16[1,32,1024]{2,1,0:T(8,128)(2,1)S(1)}, bf16[1,32,1024]{2,1,0:T(8,128)(2,1)S(1)}, u32[]{:S(2)}, u32[]{:S(2)}) collective-permute-start(bf16[1,32,1024]{2,1,0:T(8,128)(2,1)S(1)} %slice.9), channel_id=1, source_target_pairs={{0,8},{1,9},{2,10},{3,11},{4,12},{5,13},{6,14},{7,15},{8,16},{9,17... | collective-permute-start | bytes 196616 | tf_op jit(solution)/shard_map/ppermute | solution.py:149
  70.2 2.5 %copy-start.11 = (s32[32]{0:T(128)S(1)}, s32[32]{0:T(128)}, u32[]{:S(2)}) copy-start(s32[32]{0:T(128)} %count_ref.3) | copy-start | bytes 388
  70.3 12.5 %collective-permute-start.2 = (bf16[1,32,1024]{2,1,0:T(8,128)(2,1)S(1)}, bf16[1,32,1024]{2,1,0:T(8,128)(2,1)S(1)}, u32[]{:S(2)}, u32[]{:S(2)}) collective-permute-start(bf16[1,32,1024]{2,1,0:T(8,128)(2,1)S(1)} %slice.8), channel_id=1, source_target_pairs={{0,24},{1,25},{2,26},{3,27},{4,28},{5,29},{6,30},{7,31},{8,0},{9,1... | collective-permute-start | bytes 196616 | tf_op jit(solution)/shard_map/ppermute | solution.py:149
  73.4 0.7 copy-start.12
  77.0 5.7 %copy-start.5 = (bf16[1,32,1024]{2,1,0:T(8,128)(2,1)}, bf16[1,32,1024]{2,1,0:T(8,128)(2,1)S(1)}, u32[]{:S(2)}) copy-start(bf16[1,32,1024]{2,1,0:T(8,128)(2,1)S(1)} %collective-permute-done.3.rest_1_) | copy-start | bytes 196612
  82.8 0.6 copy-start.7
  83.4 0.6 copy-start.9
  85.8 19.4 %all-to-all-start.2 = ((bf16[32,4,8,128]{3,2,1,0:T(8,128)(2,1)}), bf16[32,4,8,128]{3,2,1,0:T(8,128)(2,1)S(1)}, u32[]{:S(2)}, u32[]{:S(2)}) async-start(bf16[32,4,8,128]{3,2,1,0:T(8,128)(2,1)} %accumulate.1), calls=%async_computation.2 | async-start | bytes 524288 | tf_op jit(solution)/shard_map/all_to_all | solution.py:188
  93.2 0.8 copy-start.8
  94.0 0.8 copy-start.6
  94.8 3.8 %collective-permute-start.4 = (bf16[4,2,32,1024]{3,2,1,0:T(8,128)(2,1)S(1)}, bf16[4,2,32,1024]{3,2,1,0:T(8,128)(2,1)S(1)}, u32[]{:S(2)}, u32[]{:S(2)}) collective-permute-start(bf16[4,2,32,1024]{3,2,1,0:T(8,128)(2,1)S(1)} %bitcast.6), channel_id=1, source_target_pairs={{0,1},{1,0},{2,3},{3,2},{4,5},{5,4},{6,7},{7,6},{8,9},{9,8},{10,11... | collective-permute-start | bytes 1572872 | tf_op jit(solution)/shard_map/ppermute | solution.py:149

commit v4 on v3

--- a/solution.py
+++ b/solution.py
@@ -12,7 +12,8 @@
 SMEM = pl.BlockSpec(memory_space=pltpu.SMEM)
 VMEM = pl.BlockSpec(memory_space=pltpu.VMEM)
 ANY = pl.BlockSpec(memory_space=pl.ANY)
-STEPS = (0, -1, 1, 2)
+SMALL = pltpu.CompilerParams(vmem_limit_bytes=4 * 1024 * 1024)
+STEPS = (0, 1, 3, 2)
 
 
 def owner_index(z, x, core):
@@ -82,8 +83,15 @@
     z, x, core = own // (NX * NC), (own // NC) % NX, own % NC
     tasks, list_len = ab_ref.shape
     place = lax.broadcasted_iota(jnp.int32, (tasks, list_len), 1)
-    ab_list = jnp.where(place < ab_count_ref[...], ab_ref[...], -1)
-    cd_list = jnp.where(place < cd_count_ref[...], cd_ref[...], -1)
+    task = lax.broadcasted_iota(jnp.int32, (tasks, tasks), 0)
+    same = task == lax.broadcasted_iota(jnp.int32, (tasks, tasks), 1)
+
+    def live(list_ref, count_ref):
+        counts = jnp.where(same, count_ref[...].astype(jnp.float32), 0.0)
+        counts = jnp.sum(counts, axis=1, keepdims=True)
+        return jnp.where(place.astype(jnp.float32) < counts, list_ref[...], -1)
+
+    ab_list, cd_list = live(ab_ref, ab_count_ref), live(cd_ref, cd_count_ref)
     cd_owner = owner_index(chunk // NC, x, chunk % NC)
     group = lane_group((tasks, LANE), LANE // NX)
     cd_hit = [
@@ -108,6 +116,15 @@
             out_ref[target, kind] = rounded
 
 
+def settle(first_ref, second_ref, out_ref):
+    pass
+
+
+def collect(*refs):
+    for place, ref in enumerate(refs[:-1]):
+        refs[-1][place] = ref[...]
+
+
 def multiply(weights_ref, own_ref, other_ref, out_ref, left):
     own = lax.axis_index("owner")
     z, core = own // (NX * NC), own % NC
@@ -120,7 +137,7 @@
             for part in range(width // SUB):
                 tiles = []
                 for step in STEPS:
-                    chunk = (z + step + NZ) % NZ * NC + (core + side) % NC
+                    chunk = (z ^ step) * NC + (core + side) % NC
                     tiles.append(weights_ref[part * chunks + chunk, kind].astype(jnp.float32))
                 parts.append(regroup(tiles, width))
             for spot in range(NX):
@@ -141,7 +158,7 @@
 
 def moved(block, dz, dcore=0):
     pairs = [
-        (owner_index(z, x, core), owner_index((z + dz) % NZ, x, (core + dcore) % NC))
+        (owner_index(z, x, core), owner_index(z ^ dz, x, core ^ dcore))
         for z in range(NZ)
         for x in range(NX)
         for core in range(NC)
@@ -156,6 +173,29 @@
     x_groups = [[owner_index(z, x, core) for x in range(NX)] for z in range(NZ) for core in range(NC)]
     bf16, f32 = jnp.bfloat16, jnp.float32
 
+    first, second = moved(amplitudes, 1), moved(amplitudes, 3)
+    second = pl.pallas_call(
+        settle,
+        out_shape=jax.ShapeDtypeStruct(second.shape, second.dtype),
+        in_specs=[ANY, ANY],
+        out_specs=ANY,
+        input_output_aliases={1: 0},
+        cost_estimate=pl.CostEstimate(flops=10**10, bytes_accessed=second.size * 4, transcendentals=0),
+        compiler_params=SMALL,
+        name="settle",
+    )(first, second)
+    blocks = [amplitudes, first, second, moved(second, 1)]
+    own_side = pl.pallas_call(
+        collect,
+        out_shape=jax.ShapeDtypeStruct((NZ, tile_dev, width, occ), bf16),
+        in_specs=[VMEM] * NZ,
+        out_specs=VMEM,
+        cost_estimate=pl.CostEstimate(flops=10000000000, bytes_accessed=NZ * amplitudes.size * 4, transcendentals=0),
+        compiler_params=SMALL,
+        name="collect",
+    )(*blocks)
+    other_side = moved(own_side, 0, 1)
+
     ordered = pl.pallas_call(
         order_columns,
         out_shape=jax.ShapeDtypeStruct((width // SUB, NZ * NC, SUB, LANE), bf16),
@@ -166,35 +206,33 @@
     )(cd_tiles, cd_count, integrals[0])
     ordered = ordered.reshape(pieces, SUB, LANE)
     mine = lax.all_to_all(ordered, "blk", split_axis=0, concat_axis=0, tiled=True)
-    below, above = moved(amplitudes, 1), moved(amplitudes, NZ - 1)
     outgoing = pl.pallas_call(
         route,
         out_shape=jax.ShapeDtypeStruct((owners, SUB, LANE), bf16),
-        in_specs=[SMEM, SMEM, VMEM, ANY, ANY],
+        in_specs=[SMEM, SMEM, VMEM],
         out_specs=VMEM,
         scratch_shapes=[pltpu.VMEM((owners, SUB, LANE), f32)],
+        compiler_params=SMALL,
         name="route",
-    )(ab_tiles, ab_count, mine, below, above)
+    )(ab_tiles, ab_count, mine)
     arrived = lax.all_to_all(outgoing, "owner", split_axis=0, concat_axis=0, tiled=True)
-    far = (moved(above[:1], NZ - 1), moved(below[1:], 1))
     spread = pl.pallas_call(
         accumulate,
         out_shape=jax.ShapeDtypeStruct((pieces, 4, SUB, LANE), bf16),
-        in_specs=[VMEM] * 5 + [ANY] * 2,
+        in_specs=[VMEM] * 5,
         out_specs=VMEM,
         scratch_shapes=[pltpu.VMEM((4, tasks, LANE), f32)],
+        compiler_params=SMALL,
         name="accumulate",
-    )(ab_tiles, ab_count[:, None], cd_tiles, cd_count[:, None], arrived, *far)
+    )(ab_tiles, ab_count[None, :], cd_tiles, cd_count[None, :], arrived)
     weights = lax.all_to_all(spread, "blk", split_axis=0, concat_axis=0, tiled=True)
-    own_side = jnp.concatenate([amplitudes, below, above, *far], axis=0).reshape(NZ, tile_dev, width, occ)
-    other_side = moved(own_side, 0, 1)
     partial = pl.pallas_call(
         multiply,
         out_shape=jax.ShapeDtypeStruct((NX, tile_dev * width, occ), f32),
         in_specs=[VMEM, VMEM, VMEM],
         out_specs=VMEM,
         scratch_shapes=[pltpu.VMEM((NX * tile_dev * width, NZ * NC * tile_dev * width), bf16)],
-        compiler_params=pltpu.CompilerParams(vmem_limit_bytes=32 * 1024 * 1024),
+        compiler_params=pltpu.CompilerParams(vmem_limit_bytes=16 * 1024 * 1024),
         name="multiply",
     )(weights, own_side, other_side)
     parts = lax.all_to_all(

time: 125 us -> 106 us (0.85)
  waiting for transfers between devices: 28.3 us -> 14.9 us
  local copies, waits for them, and re-layouts: 6.23 us -> 0.67 us
  starting transfers between devices: 64.4 us -> 65.9 us
    ppermute x5 -> x4, waiting for transfers between devices: 21.7 us -> 1.88 us  [moved(): return lax.ppermute(block, 'owner', pairs)]
    all_to_all x1, starting transfers between devices: 7.27 us -> 14.2 us  [shards(): lax.all_to_all(spread, 'blk', split_axis=0, concat_axis=0, tiled=True)]
    all_to_all x1, waiting for transfers between devices: 0.01 us -> 5.68 us  [shards(): lax.all_to_all(outgoing, 'owner', split_axis=0, concat_axis=0, tiled=True)]
    all_to_all x1, starting transfers between devices: 15.2 us -> 10.2 us  [shards(): lax.all_to_all(outgoing, 'owner', split_axis=0, concat_axis=0, tiled=True)]
    unnamed x30 -> x10, local copies, waits for them, and re-layouts: 4.84 us -> 0.67 us
    broadcast_in_dim x2 -> x0, local copies, waits for them, and re-layouts: 1.38 us -> none  [the longest x1 0.69 us: shards(): ab_count[:, None]]
    ppermute x5 -> x4, starting transfers between devices: 29.1 us -> 28.3 us  [moved(): return lax.ppermute(block, 'owner', pairs)]
  transfers between devices with their start and end apart: 8 -> 7, of which waited for: 6 -> 3; matrix products, arithmetic and copies ran while one was open for 1% -> 0% of each run, Pallas kernels for 0% -> 3%
where the time goes in v4:
time: 106 us; the launch traced here: 105 us
  starting transfers between devices  65.9 us (62%)
  blocking collectives  16.7 us (16%)
  waiting for transfers between devices  14.9 us (14%)
  Pallas kernels  5.97 us (6%)
    ppermute x4, starting transfers between devices, moved(): return lax.ppermute(block, 'owner', pairs)  28.3 us
    all_to_all x1, blocking collectives, shards(): lax.all_to_all(partial, 'owner', split_axis=0, concat_axis=0, tiled=True,...  16.7 us
    all_to_all x1, starting transfers between devices, shards(): lax.all_to_all(spread, 'blk', split_axis=0, concat_axis=0, tiled=True)  14.2 us
    all_to_all x1, starting transfers between devices, shards(): lax.all_to_all(ordered, 'blk', split_axis=0, concat_axis=0, tiled=True)  13 us
    all_to_all x1, starting transfers between devices, shards(): lax.all_to_all(outgoing, 'owner', split_axis=0, concat_axis=0, tiled=True)  10.2 us
    all_to_all x1, waiting for transfers between devices, shards(): lax.all_to_all(spread, 'blk', split_axis=0, concat_axis=0, tiled=True)  7.37 us
    all_to_all x1, waiting for transfers between devices, shards(): lax.all_to_all(outgoing, 'owner', split_axis=0, concat_axis=0, tiled=True)  5.68 us
    pallas_call x1, Pallas kernels, shards(): pl.pallas_call(order_columns, out_shape=jax.ShapeDtypeStruct((width // SU...  2.41 us
  transfers between devices with their start and end apart: 7, of which 3 were waited for; matrix products, arithmetic and copies ran while one was open for 0% of the time, Pallas kernels for 3%

profile of v4, /device:TPU:6, one launch (start us, length us, event | category | flops | bytes accessed | tf_op | source)
XLA Modules:
  0.0 105.1 jit_solution(3721667987079217692)
XLA Ops:
  0.0 0.0 copy-start.4
  0.0 2.4 %order_columns.1 = bf16[4,8,8,128]{3,2,1,0:T(8,128)(2,1)} custom-call(s32[32,32]{1,0:T(8,128)} %cd_ref.1, s32[32]{0:T(128)} %count_ref.2, bf16[32,1024]{1,0:T(8,128)(2,1)} %bitcast.8), custom_call_target="tpu_custom_call" | custom-call | tf_op jit(solution)/shard_map/order_columns/pallas_call | solution.py:199
  2.4 0.0 copy-start
  2.4 0.0 copy-start.2
  2.4 13.0 %all-to-all-start = ((bf16[32,8,128]{2,1,0:T(8,128)(2,1)}), bf16[32,8,128]{2,1,0:T(8,128)(2,1)S(1)}, u32[]{:S(2)}, u32[]{:S(2)}) async-start(bf16[32,8,128]{2,1,0:T(8,128)(2,1)} %bitcast.7), calls=%async_computation | async-start | bytes 131072 | tf_op jit(solution)/shard_map/all_to_all | solution.py:208
  15.5 0.0 copy-done.4
  15.5 10.9 %collective-permute-start = (bf16[2,32,1024]{2,1,0:T(8,128)(2,1)S(1)}, bf16[2,32,1024]{2,1,0:T(8,128)(2,1)S(1)}, u32[]{:S(2)}, u32[]{:S(2)}) collective-permute-start(bf16[2,32,1024]{2,1,0:T(8,128)(2,1)S(1)} %copy-done.4), channel_id=1, source_target_pairs={{0,8},{1,9},{2,10},{3,11},{4,12},{5,13},{6,14},{7,15},{8,0},{9,1},... | collective-permute-start | bytes 393224 | tf_op jit(solution)/shard_map/ppermute | solution.py:166
  26.4 8.2 %collective-permute-start.1 = (bf16[2,32,1024]{2,1,0:T(8,128)(2,1)S(1)}, bf16[2,32,1024]{2,1,0:T(8,128)(2,1)S(1)}, u32[]{:S(2)}, u32[]{:S(2)}) collective-permute-start(bf16[2,32,1024]{2,1,0:T(8,128)(2,1)S(1)} %copy-done.4), channel_id=1, source_target_pairs={{0,24},{1,25},{2,26},{3,27},{4,28},{5,29},{6,30},{7,31},{8,16},{9,... | collective-permute-start | bytes 393224 | tf_op jit(solution)/shard_map/ppermute | solution.py:166
  34.6 0.0 all-to-all-done.rows_ref
  34.6 0.0 copy-done
  34.7 0.0 copy-done.2
  34.7 1.8 %route.1 = bf16[32,8,128]{2,1,0:T(8,128)(2,1)} custom-call(s32[32,32]{1,0:T(8,128)S(1)} %copy-done, s32[32]{0:T(128)S(1)} %copy-done.2, bf16[32,8,128]{2,1,0:T(8,128)(2,1)S(1)} %all-to-all-done.rows_ref), custom_call_target="tpu_custom_call" | custom-call | tf_op jit(solution)/shard_map/route/pallas_call | solution.py:209
  36.4 10.2 %all-to-all-start.1 = ((bf16[32,8,128]{2,1,0:T(8,128)(2,1)}), bf16[32,8,128]{2,1,0:T(8,128)(2,1)S(1)}, u32[]{:S(2)}, u32[]{:S(2)}) async-start(bf16[32,8,128]{2,1,0:T(8,128)(2,1)} %route.1), calls=%async_computation.1 | async-start | bytes 131072 | tf_op jit(solution)/shard_map/all_to_all | solution.py:218
  46.7 0.0 copy-start.1
  46.7 0.0 collective-permute-done.first_ref.refs_1_
  46.7 0.0 collective-permute-done.1.second_ref
  46.7 7.3 %collective-permute-start.2 = (bf16[2,32,1024]{2,1,0:T(8,128)(2,1)S(1)}, bf16[2,32,1024]{2,1,0:T(8,128)(2,1)S(1)}, u32[]{:S(2)}, u32[]{:S(2)}) collective-permute-start(bf16[2,32,1024]{2,1,0:T(8,128)(2,1)S(1)} %settle.1.refs_2_), channel_id=1, source_target_pairs={{0,8},{1,9},{2,10},{3,11},{4,12},{5,13},{6,14},{7,15},{8,0},{9,1},... | collective-permute-start | bytes 393224 | tf_op jit(solution)/shard_map/ppermute | solution.py:166
  54.0 5.7 %all-to-all-done.1.rows_ref = bf16[32,8,128]{2,1,0:T(8,128)(2,1)S(1)} async-done(((bf16[32,8,128]{2,1,0:T(8,128)(2,1)}), bf16[32,8,128]{2,1,0:T(8,128)(2,1)S(1)}, u32[]{:S(2)}, u32[]{:S(2)}) %all-to-all-start.1) | async-done | bytes 65568 | tf_op jit(solution)/shard_map/all_to_all | solution.py:218
  59.7 0.0 copy-start.3
  59.7 0.0 copy-done.1
  59.7 0.7 copy-done.3
  60.4 1.0 accumulate.1
  61.3 14.2 %all-to-all-start.2 = ((bf16[32,4,8,128]{3,2,1,0:T(8,128)(2,1)}), bf16[32,4,8,128]{3,2,1,0:T(8,128)(2,1)S(1)}, u32[]{:S(2)}, u32[]{:S(2)}) async-start(bf16[32,4,8,128]{3,2,1,0:T(8,128)(2,1)} %accumulate.1), calls=%async_computation.2 | async-start | bytes 524288 | tf_op jit(solution)/shard_map/all_to_all | solution.py:228
  75.6 0.0 collective-permute-done.2.refs_3_
  75.6 1.9 %collective-permute-start.3 = (bf16[4,2,32,1024]{3,2,1,0:T(8,128)(2,1)S(1)}, bf16[4,2,32,1024]{3,2,1,0:T(8,128)(2,1)S(1)}, u32[]{:S(2)}, u32[]{:S(2)}) collective-permute-start(bf16[4,2,32,1024]{3,2,1,0:T(8,128)(2,1)S(1)} %collect.1.own_ref), channel_id=1, source_target_pairs={{0,1},{1,0},{2,3},{3,2},{4,5},{5,4},{6,7},{7,6},{8,9},{9,8},{10,11... | collective-permute-start | bytes 1572872 | tf_op jit(solution)/shard_map/ppermute | solution.py:166
  77.6 1.9 %collective-permute-done.3.other_ref = bf16[4,2,32,1024]{3,2,1,0:T(8,128)(2,1)S(1)} collective-permute-done((bf16[4,2,32,1024]{3,2,1,0:T(8,128)(2,1)S(1)}, bf16[4,2,32,1024]{3,2,1,0:T(8,128)(2,1)S(1)}, u32[]{:S(2)}, u32[]{:S(2)}) %collective-permute-start.3) | collective-permute-done | bytes 524320 | tf_op jit(solution)/shard_map/ppermute | solution.py:166
  79.4 7.4 %all-to-all-done.2.weights_ref = bf16[32,4,8,128]{3,2,1,0:T(8,128)(2,1)S(1)} async-done(((bf16[32,4,8,128]{3,2,1,0:T(8,128)(2,1)}), bf16[32,4,8,128]{3,2,1,0:T(8,128)(2,1)S(1)}, u32[]{:S(2)}, u32[]{:S(2)}) %all-to-all-start.2) | async-done | bytes 262176 | tf_op jit(solution)/shard_map/all_to_all | solution.py:228
  86.8 0.8 multiply.1
  87.6 16.7 %all_to_all.20 = f32[4,64,1024]{2,1,0:T(8,128)S(1)} all-to-all(f32[4,64,1024]{2,1,0:T(8,128)S(1)} %multiply.1), channel_id=1, replica_groups={{0,2,4,6},{1,3,5,7},{8,10,12,14},{9,11,13,15},{16,18,20,22},{17,19,21,2..., dimensions={0} | all-to-all | bytes 2097152 | tf_op jit(solution)/shard_map/all_to_all | solution.py:238
  104.3 0.8 reduce_sum.9
  (2 shorter events, 0.0 us)
Async XLA Ops:
  0.0 15.5 %copy-start.4 = (bf16[2,32,1024]{2,1,0:T(8,128)(2,1)S(1)}, bf16[2,32,1024]{2,1,0:T(8,128)(2,1)}, u32[]{:S(2)}) copy-start(bf16[2,32,1024]{2,1,0:T(8,128)(2,1)} %refs_0_.1) | copy-start | bytes 393220
  2.4 32.2 %copy-start = (s32[32,32]{1,0:T(8,128)S(1)}, s32[32,32]{1,0:T(8,128)}, u32[]{:S(2)}) copy-start(s32[32,32]{1,0:T(8,128)} %ab_ref.1) | copy-start | bytes 12292
  2.4 32.2 %copy-start.2 = (s32[32]{0:T(128)S(1)}, s32[32]{0:T(128)}, u32[]{:S(2)}) copy-start(s32[32]{0:T(128)} %count_ref.3) | copy-start | bytes 388
  2.4 32.2 %all-to-all-start = ((bf16[32,8,128]{2,1,0:T(8,128)(2,1)}), bf16[32,8,128]{2,1,0:T(8,128)(2,1)S(1)}, u32[]{:S(2)}, u32[]{:S(2)}) async-start(bf16[32,8,128]{2,1,0:T(8,128)(2,1)} %bitcast.7), calls=%async_computation | async-start | bytes 131072 | tf_op jit(solution)/shard_map/all_to_all | solution.py:208
  15.5 31.2 %collective-permute-start = (bf16[2,32,1024]{2,1,0:T(8,128)(2,1)S(1)}, bf16[2,32,1024]{2,1,0:T(8,128)(2,1)S(1)}, u32[]{:S(2)}, u32[]{:S(2)}) collective-permute-start(bf16[2,32,1024]{2,1,0:T(8,128)(2,1)S(1)} %copy-done.4), channel_id=1, source_target_pairs={{0,8},{1,9},{2,10},{3,11},{4,12},{5,13},{6,14},{7,15},{8,0},{9,1},... | collective-permute-start | bytes 393224 | tf_op jit(solution)/shard_map/ppermute | solution.py:166
  26.4 20.3 %collective-permute-start.1 = (bf16[2,32,1024]{2,1,0:T(8,128)(2,1)S(1)}, bf16[2,32,1024]{2,1,0:T(8,128)(2,1)S(1)}, u32[]{:S(2)}, u32[]{:S(2)}) collective-permute-start(bf16[2,32,1024]{2,1,0:T(8,128)(2,1)S(1)} %copy-done.4), channel_id=1, source_target_pairs={{0,24},{1,25},{2,26},{3,27},{4,28},{5,29},{6,30},{7,31},{8,16},{9,... | collective-permute-start | bytes 393224 | tf_op jit(solution)/shard_map/ppermute | solution.py:166
  36.4 23.3 %all-to-all-start.1 = ((bf16[32,8,128]{2,1,0:T(8,128)(2,1)}), bf16[32,8,128]{2,1,0:T(8,128)(2,1)S(1)}, u32[]{:S(2)}, u32[]{:S(2)}) async-start(bf16[32,8,128]{2,1,0:T(8,128)(2,1)} %route.1), calls=%async_computation.1 | async-start | bytes 131072 | tf_op jit(solution)/shard_map/all_to_all | solution.py:218
  46.7 13.0 %copy-start.1 = (s32[32,32]{1,0:T(8,128)S(1)}, s32[32,32]{1,0:T(8,128)}, u32[]{:S(2)}) copy-start(s32[32,32]{1,0:T(8,128)} %cd_ref.1) | copy-start | bytes 12292
  46.7 28.8 %collective-permute-start.2 = (bf16[2,32,1024]{2,1,0:T(8,128)(2,1)S(1)}, bf16[2,32,1024]{2,1,0:T(8,128)(2,1)S(1)}, u32[]{:S(2)}, u32[]{:S(2)}) collective-permute-start(bf16[2,32,1024]{2,1,0:T(8,128)(2,1)S(1)} %settle.1.refs_2_), channel_id=1, source_target_pairs={{0,8},{1,9},{2,10},{3,11},{4,12},{5,13},{6,14},{7,15},{8,0},{9,1},... | collective-permute-start | bytes 393224 | tf_op jit(solution)/shard_map/ppermute | solution.py:166
  59.7 0.7 copy-start.3
  61.3 25.5 %all-to-all-start.2 = ((bf16[32,4,8,128]{3,2,1,0:T(8,128)(2,1)}), bf16[32,4,8,128]{3,2,1,0:T(8,128)(2,1)S(1)}, u32[]{:S(2)}, u32[]{:S(2)}) async-start(bf16[32,4,8,128]{3,2,1,0:T(8,128)(2,1)} %accumulate.1), calls=%async_computation.2 | async-start | bytes 524288 | tf_op jit(solution)/shard_map/all_to_all | solution.py:228
  75.6 3.8 %collective-permute-start.3 = (bf16[4,2,32,1024]{3,2,1,0:T(8,128)(2,1)S(1)}, bf16[4,2,32,1024]{3,2,1,0:T(8,128)(2,1)S(1)}, u32[]{:S(2)}, u32[]{:S(2)}) collective-permute-start(bf16[4,2,32,1024]{3,2,1,0:T(8,128)(2,1)S(1)} %collect.1.own_ref), channel_id=1, source_target_pairs={{0,1},{1,0},{2,3},{3,2},{4,5},{5,4},{6,7},{7,6},{8,9},{9,8},{10,11... | collective-permute-start | bytes 1572872 | tf_op jit(solution)/shard_map/ppermute | solution.py:166

commit v5 on v4

--- a/solution.py
+++ b/solution.py
@@ -69,11 +69,19 @@
     for place in range(list_len):
         owner = tiles_ref[own, place] // 2
         held[owner] += jnp.where(place < count, rows_ref[place].astype(jnp.float32), 0.0)
+    width = LANE // NX
+    group = lane_group((SUB, LANE), width)
     for z in range(NZ):
         for core in range(NC):
-            moved = regroup([held[owner_index(z, x, core)] for x in range(NX)], LANE // NX)
+            tiles = [held[owner_index(z, x, core)] for x in range(NX)]
             for x in range(NX):
-                out_ref[owner_index(z, x, core)] = moved[x].astype(out_ref.dtype)
+                wanted = [(tiles[x ^ (3 * a)], x ^ d) for a in range(2) for d in range(2)]
+                merged = None
+                for place, (tile, spot) in enumerate(wanted):
+                    shift = (place - spot) % NX * width
+                    turned = pltpu.roll(tile, shift, 1) if shift else tile
+                    merged = turned if merged is None else jnp.where(group == place, turned, merged)
+                out_ref[owner_index(z, x, core)] = merged.astype(out_ref.dtype)
 
 
 def accumulate(ab_ref, ab_count_ref, cd_ref, cd_count_ref, rows_ref, *rest):
@@ -92,19 +100,26 @@
         return jnp.where(place.astype(jnp.float32) < counts, list_ref[...], -1)
 
     ab_list, cd_list = live(ab_ref, ab_count_ref), live(cd_ref, cd_count_ref)
-    cd_owner = owner_index(chunk // NC, x, chunk % NC)
     group = lane_group((tasks, LANE), LANE // NX)
-    cd_hit = [
-        jnp.max((cd_list == cd_owner * 2 + par).astype(jnp.float32), axis=1, keepdims=True) for par in range(2)
-    ]
+
+    def hit(tile_list, tile):
+        return jnp.max((tile_list == tile).astype(jnp.float32), axis=1, keepdims=True)
+
+    def ab_hit(low):
+        mine, theirs = (hit(ab_list, owner_index(z, spot, core) * 2 + low) for spot in (x, x ^ 3))
+        return jnp.where(group < 2, mine, theirs)
+
+    def cd_hit(par):
+        mine, theirs = (
+            hit(cd_list, owner_index(chunk // NC, spot, chunk % NC) * 2 + par) for spot in (x, x ^ 1)
+        )
+        return jnp.where(group % 2 == 0, mine, theirs)
+
+    cd_hits = [cd_hit(par) for par in range(2)]
     for low in range(2):
-        ab_hit = jnp.zeros((tasks, LANE), jnp.float32)
-        for spot in range(NX):
-            tile = owner_index(z, spot, core) * 2 + low
-            hit = jnp.max((ab_list == tile).astype(jnp.float32), axis=1, keepdims=True)
-            ab_hit = jnp.where(group == spot, hit, ab_hit)
+        rows_hit = ab_hit(low)
         for par in range(2):
-            mask[low * 2 + par] = ab_hit * cd_hit[par]
+            mask[low * 2 + par] = rows_hit * cd_hits[par]
     totals = [jnp.zeros((SUB, LANE), jnp.float32) for _ in range(4)]
     for task in range(tasks):
         rows = rows_ref[task].astype(jnp.float32)
@@ -116,20 +131,28 @@
             out_ref[target, kind] = rounded
 
 
-def settle(first_ref, second_ref, out_ref):
+def collect_near(own_ref, first_ref, second_ref, near_ref, relay_ref):
+    for place, ref in enumerate((own_ref, first_ref, second_ref)):
+        near_ref[place] = ref[...]
+    relay_ref[...] = first_ref[...]
+
+
+def settle(*refs):
     pass
 
 
-def collect(*refs):
-    for place, ref in enumerate(refs[:-1]):
-        refs[-1][place] = ref[...]
-
-
-def multiply(weights_ref, own_ref, other_ref, out_ref, left):
+def collect_all(near_ref, far_ref, out_ref):
+    out_ref[: NZ - 1] = near_ref[...]
+    out_ref[NZ - 1] = far_ref[...]
+
+
+def multiply(weights_ref, *rest):
+    amps_refs, (mine_ref, theirs_ref, left) = rest[:4], rest[4:]
     own = lax.axis_index("owner")
     z, core = own // (NX * NC), own % NC
-    width, occ = own_ref.shape[2:]
+    width, occ = amps_refs[0].shape[2:]
     chunks = NZ * NC
+    blocks = [(par, d, side) for par in range(2) for d in range(2) for side in range(NC)]
     for kind in range(4):
         low, par = kind // 2, kind % 2
         for side in range(NC):
@@ -140,25 +163,25 @@
                     chunk = (z ^ step) * NC + (core + side) % NC
                     tiles.append(weights_ref[part * chunks + chunk, kind].astype(jnp.float32))
                 parts.append(regroup(tiles, width))
-            for spot in range(NX):
-                rows = jnp.concatenate([p[spot] for p in parts], axis=0)
-                row, col = (spot * 2 + low) * width, (par * NC + side) * LANE
-                left[row : row + width, col : col + LANE] = rows.astype(left.dtype)
+            for a in range(2):
+                for d in range(2):
+                    rows = jnp.concatenate([p[2 * a + d] for p in parts], axis=0)
+                    row, col = (a * 2 + low) * width, blocks.index((par, d, side)) * LANE
+                    left[row : row + width, col : col + LANE] = rows.astype(left.dtype)
     wide = 256
     for col in range(0, occ, wide):
         total = None
-        for par in range(2):
-            for side, amps in enumerate((own_ref, other_ref)):
-                right = amps[:, par, :, col : col + wide].reshape(LANE, wide)
-                at = (par * NC + side) * LANE
-                term = jnp.dot(left[:, at : at + LANE], right, preferred_element_type=jnp.float32)
-                total = term if total is None else total + term
-        out_ref[:, :, col : col + wide] = total.reshape(NX, 2 * width, wide).astype(out_ref.dtype)
-
-
-def moved(block, dz, dcore=0):
+        for at, (par, d, side) in enumerate(blocks):
+            right = amps_refs[2 * side + d][:, par, :, col : col + wide].reshape(LANE, wide)
+            term = jnp.dot(left[:, at * LANE : (at + 1) * LANE], right, preferred_element_type=jnp.float32)
+            total = term if total is None else total + term
+        mine_ref[:, col : col + wide] = total[: 2 * width]
+        theirs_ref[:, col : col + wide] = total[2 * width :]
+
+
+def moved(block, dz=0, dx=0, dcore=0):
     pairs = [
-        (owner_index(z, x, core), owner_index(z ^ dz, x, core ^ dcore))
+        (owner_index(z, x, core), owner_index(z ^ dz, x ^ dx, core ^ dcore))
         for z in range(NZ)
         for x in range(NX)
         for core in range(NC)
@@ -166,36 +189,25 @@
     return lax.ppermute(block, "owner", pairs)
 
 
+def joined(near, far, flops):
+    return pl.pallas_call(
+        collect_all,
+        out_shape=jax.ShapeDtypeStruct((near.shape[0] + 1, *near.shape[1:]), near.dtype),
+        in_specs=[VMEM] * 2,
+        out_specs=VMEM,
+        cost_estimate=pl.CostEstimate(flops=flops, bytes_accessed=near.size * 6, transcendentals=0),
+        compiler_params=SMALL,
+        name="collect_all",
+    )(near, far)
+
+
 def shards(amplitudes, integrals, cd_tiles, cd_count, ab_tiles, ab_count):
     tile_dev, width, occ = amplitudes.shape
     owners, pieces = lax.axis_size("owner"), lax.axis_size("blk")
     tasks = cd_tiles.shape[0]
-    x_groups = [[owner_index(z, x, core) for x in range(NX)] for z in range(NZ) for core in range(NC)]
     bf16, f32 = jnp.bfloat16, jnp.float32
 
     first, second = moved(amplitudes, 1), moved(amplitudes, 3)
-    second = pl.pallas_call(
-        settle,
-        out_shape=jax.ShapeDtypeStruct(second.shape, second.dtype),
-        in_specs=[ANY, ANY],
-        out_specs=ANY,
-        input_output_aliases={1: 0},
-        cost_estimate=pl.CostEstimate(flops=10**10, bytes_accessed=second.size * 4, transcendentals=0),
-        compiler_params=SMALL,
-        name="settle",
-    )(first, second)
-    blocks = [amplitudes, first, second, moved(second, 1)]
-    own_side = pl.pallas_call(
-        collect,
-        out_shape=jax.ShapeDtypeStruct((NZ, tile_dev, width, occ), bf16),
-        in_specs=[VMEM] * NZ,
-        out_specs=VMEM,
-        cost_estimate=pl.CostEstimate(flops=10000000000, bytes_accessed=NZ * amplitudes.size * 4, transcendentals=0),
-        compiler_params=SMALL,
-        name="collect",
-    )(*blocks)
-    other_side = moved(own_side, 0, 1)
-
     ordered = pl.pallas_call(
         order_columns,
         out_shape=jax.ShapeDtypeStruct((width // SUB, NZ * NC, SUB, LANE), bf16),
@@ -215,6 +227,20 @@
         compiler_params=SMALL,
         name="route",
     )(ab_tiles, ab_count, mine)
+    near, relay = pl.pallas_call(
+        collect_near,
+        out_shape=(
+            jax.ShapeDtypeStruct((NZ - 1, tile_dev, width, occ), bf16),
+            jax.ShapeDtypeStruct(second.shape, bf16),
+        ),
+        in_specs=[VMEM] * 3,
+        out_specs=(VMEM, VMEM),
+        cost_estimate=pl.CostEstimate(flops=10000000000, bytes_accessed=amplitudes.size * 16, transcendentals=0),
+        compiler_params=SMALL,
+        name="collect_near",
+    )(amplitudes, first, second)
+    near_pair = moved(near, dx=1)
+    far = moved(relay, 3)
     arrived = lax.all_to_all(outgoing, "owner", split_axis=0, concat_axis=0, tiled=True)
     spread = pl.pallas_call(
         accumulate,
@@ -225,20 +251,32 @@
         compiler_params=SMALL,
         name="accumulate",
     )(ab_tiles, ab_count[None, :], cd_tiles, cd_count[None, :], arrived)
+    far = pl.pallas_call(
+        settle,
+        out_shape=jax.ShapeDtypeStruct(far.shape, far.dtype),
+        in_specs=[ANY, ANY],
+        out_specs=ANY,
+        input_output_aliases={0: 0},
+        cost_estimate=pl.CostEstimate(flops=1000000, bytes_accessed=far.size * 4, transcendentals=0),
+        compiler_params=SMALL,
+        name="settle",
+    )(far, spread)
+    far_pair = moved(far, dx=1)
+    sides = [joined(near, far, 2000000000), joined(near_pair, far_pair, 5000000000)]
+    sides += [moved(side, dcore=1) for side in sides]
+
     weights = lax.all_to_all(spread, "blk", split_axis=0, concat_axis=0, tiled=True)
-    partial = pl.pallas_call(
+    half = jax.ShapeDtypeStruct((tile_dev * width, occ), f32)
+    mine, theirs = pl.pallas_call(
         multiply,
-        out_shape=jax.ShapeDtypeStruct((NX, tile_dev * width, occ), f32),
-        in_specs=[VMEM, VMEM, VMEM],
-        out_specs=VMEM,
-        scratch_shapes=[pltpu.VMEM((NX * tile_dev * width, NZ * NC * tile_dev * width), bf16)],
+        out_shape=(half, half),
+        in_specs=[VMEM] * 5,
+        out_specs=(VMEM, VMEM),
+        scratch_shapes=[pltpu.VMEM((2 * tile_dev * width, 2 * NZ * NC * tile_dev * width), bf16)],
         compiler_params=pltpu.CompilerParams(vmem_limit_bytes=16 * 1024 * 1024),
         name="multiply",
-    )(weights, own_side, other_side)
-    parts = lax.all_to_all(
-        partial, "owner", split_axis=0, concat_axis=0, tiled=True, axis_index_groups=x_groups
-    )
-    return jnp.sum(parts, axis=0).reshape(tile_dev, width, occ)
+    )(weights, *sides)
+    return (mine + moved(theirs, dx=3)).reshape(tile_dev, width, occ)
 
 
 def solution(mesh):

time: 106 us -> 96.5 us (0.910)
  blocking collectives: 16.7 us -> 0 us
  starting transfers between devices: 65.9 us -> 71.6 us
    all_to_all x1 -> x0, blocking collectives: 16.7 us -> none  [shards(): lax.all_to_all(partial, 'owner', split_axis=0, concat_axis=0, tiled=True,...]
    ppermute x4 -> x8, starting transfers between devices: 28.3 us -> 39.6 us  [moved(): return lax.ppermute(block, 'owner', pairs)]
    ppermute x4 -> x8, waiting for transfers between devices: 1.88 us -> 11.4 us  [moved(): return lax.ppermute(block, 'owner', pairs)]
    all_to_all x1, waiting for transfers between devices: 7.37 us -> 1.2 us  [shards(): lax.all_to_all(spread, 'blk', split_axis=0, concat_axis=0, tiled=True)]
    all_to_all x1, starting transfers between devices: 14.2 us -> 8.68 us  [shards(): lax.all_to_all(spread, 'blk', split_axis=0, concat_axis=0, tiled=True)]
    all_to_all x1, waiting for transfers between devices: 5.68 us -> 2.82 us  [shards(): lax.all_to_all(outgoing, 'owner', split_axis=0, concat_axis=0, tiled=True)]
  transfers between devices with their start and end apart: 7 -> 11, of which waited for: 3 -> 5; matrix products, arithmetic and copies ran while one was open for 0% -> 0% of each run, Pallas kernels for 3% -> 3%
where the time goes in v5:
time: 96.5 us; the launch traced here: 94.7 us
  starting transfers between devices  71.6 us (74%)
  waiting for transfers between devices  15.4 us (16%)
  Pallas kernels  6.03 us (6%)
    ppermute x8, starting transfers between devices, moved(): return lax.ppermute(block, 'owner', pairs)  39.6 us
    all_to_all x1, starting transfers between devices, shards(): lax.all_to_all(ordered, 'blk', split_axis=0, concat_axis=0, tiled=True)  13 us
    ppermute x8, waiting for transfers between devices, moved(): return lax.ppermute(block, 'owner', pairs)  11.4 us
    all_to_all x1, starting transfers between devices, shards(): lax.all_to_all(outgoing, 'owner', split_axis=0, concat_axis=0, tiled=True)  10.2 us
    all_to_all x1, starting transfers between devices, shards(): lax.all_to_all(spread, 'blk', split_axis=0, concat_axis=0, tiled=True)  8.68 us
    all_to_all x1, waiting for transfers between devices, shards(): lax.all_to_all(outgoing, 'owner', split_axis=0, concat_axis=0, tiled=True)  2.82 us
    pallas_call x1, Pallas kernels, shards(): pl.pallas_call(order_columns, out_shape=jax.ShapeDtypeStruct((width // SU...  2.41 us
  transfers between devices with their start and end apart: 11, of which 5 were waited for; matrix products, arithmetic and copies ran while one was open for 0% of the time, Pallas kernels for 3%

profile of v5, /device:TPU:6, one launch (start us, length us, event | category | flops | bytes accessed | tf_op | source)
XLA Modules:
  0.0 94.7 jit_solution(6632991833484717825)
XLA Ops:
  0.0 0.0 copy-start.4
  0.0 2.4 %order_columns.1 = bf16[4,8,8,128]{3,2,1,0:T(8,128)(2,1)} custom-call(s32[32,32]{1,0:T(8,128)} %cd_ref.1, s32[32]{0:T(128)} %count_ref.2, bf16[32,1024]{1,0:T(8,128)(2,1)} %bitcast.8), custom_call_target="tpu_custom_call" | custom-call | tf_op jit(solution)/shard_map/order_columns/pallas_call | solution.py:211
  2.4 0.0 copy-start
  2.4 0.0 copy-start.2
  2.4 13.0 %all-to-all-start = ((bf16[32,8,128]{2,1,0:T(8,128)(2,1)}), bf16[32,8,128]{2,1,0:T(8,128)(2,1)S(1)}, u32[]{:S(2)}, u32[]{:S(2)}) async-start(bf16[32,8,128]{2,1,0:T(8,128)(2,1)} %bitcast.7), calls=%async_computation | async-start | bytes 131072 | tf_op jit(solution)/shard_map/all_to_all | solution.py:220
  15.5 0.0 copy-done.4
  15.5 10.9 %collective-permute-start = (bf16[2,32,1024]{2,1,0:T(8,128)(2,1)S(1)}, bf16[2,32,1024]{2,1,0:T(8,128)(2,1)S(1)}, u32[]{:S(2)}, u32[]{:S(2)}) collective-permute-start(bf16[2,32,1024]{2,1,0:T(8,128)(2,1)S(1)} %copy-done.4), channel_id=1, source_target_pairs={{0,8},{1,9},{2,10},{3,11},{4,12},{5,13},{6,14},{7,15},{8,0},{9,1},... | collective-permute-start | bytes 393224 | tf_op jit(solution)/shard_map/ppermute | solution.py:189
  26.4 8.2 %collective-permute-start.1 = (bf16[2,32,1024]{2,1,0:T(8,128)(2,1)S(1)}, bf16[2,32,1024]{2,1,0:T(8,128)(2,1)S(1)}, u32[]{:S(2)}, u32[]{:S(2)}) collective-permute-start(bf16[2,32,1024]{2,1,0:T(8,128)(2,1)S(1)} %copy-done.4), channel_id=1, source_target_pairs={{0,24},{1,25},{2,26},{3,27},{4,28},{5,29},{6,30},{7,31},{8,16},{9,... | collective-permute-start | bytes 393224 | tf_op jit(solution)/shard_map/ppermute | solution.py:189
  34.6 0.0 all-to-all-done.rows_ref
  34.6 0.0 copy-done
  34.7 0.0 copy-done.2
  34.7 1.8 %route.1 = bf16[32,8,128]{2,1,0:T(8,128)(2,1)} custom-call(s32[32,32]{1,0:T(8,128)S(1)} %copy-done, s32[32]{0:T(128)S(1)} %copy-done.2, bf16[32,8,128]{2,1,0:T(8,128)(2,1)S(1)} %all-to-all-done.rows_ref), custom_call_target="tpu_custom_call" | custom-call | tf_op jit(solution)/shard_map/route/pallas_call | solution.py:221
  36.4 10.2 %all-to-all-start.1 = ((bf16[32,8,128]{2,1,0:T(8,128)(2,1)}), bf16[32,8,128]{2,1,0:T(8,128)(2,1)S(1)}, u32[]{:S(2)}, u32[]{:S(2)}) async-start(bf16[32,8,128]{2,1,0:T(8,128)(2,1)} %route.1), calls=%async_computation.1 | async-start | bytes 131072 | tf_op jit(solution)/shard_map/all_to_all | solution.py:244
  46.7 0.0 collective-permute-done.first_ref
  46.7 0.0 collective-permute-done.1.second_ref
  46.7 0.0 copy-start.1
  46.7 2.8 %collective-permute-start.3 = (bf16[3,2,32,1024]{3,2,1,0:T(8,128)(2,1)S(1)}, bf16[3,2,32,1024]{3,2,1,0:T(8,128)(2,1)S(1)}, u32[]{:S(2)}, u32[]{:S(2)}) collective-permute-start(bf16[3,2,32,1024]{3,2,1,0:T(8,128)(2,1)S(1)} %get-tuple-element.9.near_ref), channel_id=1, source_target_pairs={{0,2},{1,3},{2,0},{3,1},{4,6},{5,7},{6,4},{7,5},{8,10},{9,11},{10,... | collective-permute-start | bytes 1179656 | tf_op jit(solution)/shard_map/ppermute | solution.py:189
  49.5 7.3 %collective-permute-start.2 = (bf16[2,32,1024]{2,1,0:T(8,128)(2,1)S(1)}, bf16[2,32,1024]{2,1,0:T(8,128)(2,1)S(1)}, u32[]{:S(2)}, u32[]{:S(2)}) collective-permute-start(bf16[2,32,1024]{2,1,0:T(8,128)(2,1)S(1)} %get-tuple-element.10), channel_id=1, source_target_pairs={{0,24},{1,25},{2,26},{3,27},{4,28},{5,29},{6,30},{7,31},{8,16},{9,... | collective-permute-start | bytes 393224 | tf_op jit(solution)/shard_map/ppermute | solution.py:189
  56.9 2.8 %all-to-all-done.1.rows_ref = bf16[32,8,128]{2,1,0:T(8,128)(2,1)S(1)} async-done(((bf16[32,8,128]{2,1,0:T(8,128)(2,1)}), bf16[32,8,128]{2,1,0:T(8,128)(2,1)S(1)}, u32[]{:S(2)}, u32[]{:S(2)}) %all-to-all-start.1) | async-done | bytes 65568 | tf_op jit(solution)/shard_map/all_to_all | solution.py:244
  59.7 0.0 copy-start.3
  59.7 0.0 copy-done.1
  59.7 0.7 copy-done.3
  60.3 1.0 %accumulate.1.refs_1_ = bf16[32,4,8,128]{3,2,1,0:T(8,128)(2,1)} custom-call(s32[32,32]{1,0:T(8,128)S(1)} %copy-done, s32[1,32]{1,0:T(1,128)S(1)} %bitcast.5, s32[32,32]{1,0:T(8,128)S(1)} %copy-done.1, s32[1,32]{1,0:T(1,128)S(1)} %bitcast.6, bf16[32,8,128]{2,1,0:T(8,128)(2,1)S(1)} %all-to-all-done.1.rows_ref), custom_call_target="tpu_custom_call" | custom-call | tf_op jit(solution)/shard_map/accumulate/pallas_call | solution.py:245
  61.3 8.7 %all-to-all-start.2 = ((bf16[32,4,8,128]{3,2,1,0:T(8,128)(2,1)}), bf16[32,4,8,128]{3,2,1,0:T(8,128)(2,1)S(1)}, u32[]{:S(2)}, u32[]{:S(2)}) async-start(bf16[32,4,8,128]{3,2,1,0:T(8,128)(2,1)} %accumulate.1.refs_1_), calls=%async_computation.2 | async-start | bytes 524288 | tf_op jit(solution)/shard_map/all_to_all | solution.py:268
  70.0 0.0 collective-permute-done.2.refs_0_
  70.0 2.6 %collective-permute-start.4 = (bf16[2,32,1024]{2,1,0:T(8,128)(2,1)S(1)}, bf16[2,32,1024]{2,1,0:T(8,128)(2,1)S(1)}, u32[]{:S(2)}, u32[]{:S(2)}) collective-permute-start(bf16[2,32,1024]{2,1,0:T(8,128)(2,1)S(1)} %settle.1.far_ref), channel_id=1, source_target_pairs={{0,2},{1,3},{2,0},{3,1},{4,6},{5,7},{6,4},{7,5},{8,10},{9,11},{10,... | collective-permute-start | bytes 393224 | tf_op jit(solution)/shard_map/ppermute | solution.py:189
  72.7 1.9 %collective-permute-start.5 = (bf16[4,2,32,1024]{3,2,1,0:T(8,128)(2,1)S(1)}, bf16[4,2,32,1024]{3,2,1,0:T(8,128)(2,1)S(1)}, u32[]{:S(2)}, u32[]{:S(2)}) collective-permute-start(bf16[4,2,32,1024]{3,2,1,0:T(8,128)(2,1)S(1)} %collect_all.2.rest_0_), channel_id=1, source_target_pairs={{0,1},{1,0},{2,3},{3,2},{4,5},{5,4},{6,7},{7,6},{8,9},{9,8},{10,11... | collective-permute-start | bytes 1572872 | tf_op jit(solution)/shard_map/ppermute | solution.py:189
  74.6 0.0 collective-permute-done.3.near_ref
  74.6 2.9 %collective-permute-done.4.far_ref = bf16[2,32,1024]{2,1,0:T(8,128)(2,1)S(1)} collective-permute-done((bf16[2,32,1024]{2,1,0:T(8,128)(2,1)S(1)}, bf16[2,32,1024]{2,1,0:T(8,128)(2,1)S(1)}, u32[]{:S(2)}, u32[]{:S(2)}) %collective-permute-start.4) | collective-permute-done | bytes 131104 | tf_op jit(solution)/shard_map/ppermute | solution.py:189
  77.6 1.9 %collective-permute-start.6 = (bf16[4,2,32,1024]{3,2,1,0:T(8,128)(2,1)S(1)}, bf16[4,2,32,1024]{3,2,1,0:T(8,128)(2,1)S(1)}, u32[]{:S(2)}, u32[]{:S(2)}) collective-permute-start(bf16[4,2,32,1024]{3,2,1,0:T(8,128)(2,1)S(1)} %collect_all.3.rest_1_), channel_id=1, source_target_pairs={{0,1},{1,0},{2,3},{3,2},{4,5},{5,4},{6,7},{7,6},{8,9},{9,8},{10,11... | collective-permute-start | bytes 1572872 | tf_op jit(solution)/shard_map/ppermute | solution.py:189
  79.5 0.0 collective-permute-done.5.rest_2_
  79.5 1.9 %collective-permute-done.6.rest_3_ = bf16[4,2,32,1024]{3,2,1,0:T(8,128)(2,1)S(1)} collective-permute-done((bf16[4,2,32,1024]{3,2,1,0:T(8,128)(2,1)S(1)}, bf16[4,2,32,1024]{3,2,1,0:T(8,128)(2,1)S(1)}, u32[]{:S(2)}, u32[]{:S(2)}) %collective-permute-start.6) | collective-permute-done | bytes 524320 | tf_op jit(solution)/shard_map/ppermute | solution.py:189
  81.4 1.2 %all-to-all-done.2.weights_ref = bf16[32,4,8,128]{3,2,1,0:T(8,128)(2,1)S(1)} async-done(((bf16[32,4,8,128]{3,2,1,0:T(8,128)(2,1)}), bf16[32,4,8,128]{3,2,1,0:T(8,128)(2,1)S(1)}, u32[]{:S(2)}, u32[]{:S(2)}) %all-to-all-start.2) | async-done | bytes 262176 | tf_op jit(solution)/shard_map/all_to_all | solution.py:268
  82.6 0.8 multiply.1
  83.4 3.9 %collective-permute-start.7 = (f32[64,1024]{1,0:T(8,128)S(1)}, f32[64,1024]{1,0:T(8,128)S(1)}, u32[]{:S(2)}, u32[]{:S(2)}) collective-permute-start(f32[64,1024]{1,0:T(8,128)S(1)} %get-tuple-element.12), channel_id=1, source_target_pairs={{0,6},{1,7},{2,4},{3,5},{4,2},{5,3},{6,0},{7,1},{8,14},{9,15},{10,... | collective-permute-start | bytes 786440 | tf_op jit(solution)/shard_map/ppermute | solution.py:189
  87.3 6.6 %collective-permute-done.7 = f32[64,1024]{1,0:T(8,128)S(1)} collective-permute-done((f32[64,1024]{1,0:T(8,128)S(1)}, f32[64,1024]{1,0:T(8,128)S(1)}, u32[]{:S(2)}, u32[]{:S(2)}) %collective-permute-start.7) | collective-permute-done | bytes 262176 | tf_op jit(solution)/shard_map/ppermute | solution.py:189
  93.9 0.7 add.3
  (4 shorter events, 0.1 us)
Async XLA Ops:
  0.0 15.5 %copy-start.4 = (bf16[2,32,1024]{2,1,0:T(8,128)(2,1)S(1)}, bf16[2,32,1024]{2,1,0:T(8,128)(2,1)}, u32[]{:S(2)}) copy-start(bf16[2,32,1024]{2,1,0:T(8,128)(2,1)} %own_ref.1) | copy-start | bytes 393220
  2.4 32.2 %copy-start = (s32[32,32]{1,0:T(8,128)S(1)}, s32[32,32]{1,0:T(8,128)}, u32[]{:S(2)}) copy-start(s32[32,32]{1,0:T(8,128)} %ab_ref.1) | copy-start | bytes 12292
  2.4 32.2 %copy-start.2 = (s32[32]{0:T(128)S(1)}, s32[32]{0:T(128)}, u32[]{:S(2)}) copy-start(s32[32]{0:T(128)} %count_ref.3) | copy-start | bytes 388
  2.4 32.2 %all-to-all-start = ((bf16[32,8,128]{2,1,0:T(8,128)(2,1)}), bf16[32,8,128]{2,1,0:T(8,128)(2,1)S(1)}, u32[]{:S(2)}, u32[]{:S(2)}) async-start(bf16[32,8,128]{2,1,0:T(8,128)(2,1)} %bitcast.7), calls=%async_computation | async-start | bytes 131072 | tf_op jit(solution)/shard_map/all_to_all | solution.py:220
  15.5 31.2 %collective-permute-start = (bf16[2,32,1024]{2,1,0:T(8,128)(2,1)S(1)}, bf16[2,32,1024]{2,1,0:T(8,128)(2,1)S(1)}, u32[]{:S(2)}, u32[]{:S(2)}) collective-permute-start(bf16[2,32,1024]{2,1,0:T(8,128)(2,1)S(1)} %copy-done.4), channel_id=1, source_target_pairs={{0,8},{1,9},{2,10},{3,11},{4,12},{5,13},{6,14},{7,15},{8,0},{9,1},... | collective-permute-start | bytes 393224 | tf_op jit(solution)/shard_map/ppermute | solution.py:189
  26.4 20.3 %collective-permute-start.1 = (bf16[2,32,1024]{2,1,0:T(8,128)(2,1)S(1)}, bf16[2,32,1024]{2,1,0:T(8,128)(2,1)S(1)}, u32[]{:S(2)}, u32[]{:S(2)}) collective-permute-start(bf16[2,32,1024]{2,1,0:T(8,128)(2,1)S(1)} %copy-done.4), channel_id=1, source_target_pairs={{0,24},{1,25},{2,26},{3,27},{4,28},{5,29},{6,30},{7,31},{8,16},{9,... | collective-permute-start | bytes 393224 | tf_op jit(solution)/shard_map/ppermute | solution.py:189
  36.4 23.3 %all-to-all-start.1 = ((bf16[32,8,128]{2,1,0:T(8,128)(2,1)}), bf16[32,8,128]{2,1,0:T(8,128)(2,1)S(1)}, u32[]{:S(2)}, u32[]{:S(2)}) async-start(bf16[32,8,128]{2,1,0:T(8,128)(2,1)} %route.1), calls=%async_computation.1 | async-start | bytes 131072 | tf_op jit(solution)/shard_map/all_to_all | solution.py:244
  46.7 13.0 %copy-start.1 = (s32[32,32]{1,0:T(8,128)S(1)}, s32[32,32]{1,0:T(8,128)}, u32[]{:S(2)}) copy-start(s32[32,32]{1,0:T(8,128)} %cd_ref.1) | copy-start | bytes 12292
  46.7 27.9 %collective-permute-start.3 = (bf16[3,2,32,1024]{3,2,1,0:T(8,128)(2,1)S(1)}, bf16[3,2,32,1024]{3,2,1,0:T(8,128)(2,1)S(1)}, u32[]{:S(2)}, u32[]{:S(2)}) collective-permute-start(bf16[3,2,32,1024]{3,2,1,0:T(8,128)(2,1)S(1)} %get-tuple-element.9.near_ref), channel_id=1, source_target_pairs={{0,2},{1,3},{2,0},{3,1},{4,6},{5,7},{6,4},{7,5},{8,10},{9,11},{10,... | collective-permute-start | bytes 1179656 | tf_op jit(solution)/shard_map/ppermute | solution.py:189
  49.5 20.5 %collective-permute-start.2 = (bf16[2,32,1024]{2,1,0:T(8,128)(2,1)S(1)}, bf16[2,32,1024]{2,1,0:T(8,128)(2,1)S(1)}, u32[]{:S(2)}, u32[]{:S(2)}) collective-permute-start(bf16[2,32,1024]{2,1,0:T(8,128)(2,1)S(1)} %get-tuple-element.10), channel_id=1, source_target_pairs={{0,24},{1,25},{2,26},{3,27},{4,28},{5,29},{6,30},{7,31},{8,16},{9,... | collective-permute-start | bytes 393224 | tf_op jit(solution)/shard_map/ppermute | solution.py:189
  59.7 0.7 copy-start.3
  61.3 21.3 %all-to-all-start.2 = ((bf16[32,4,8,128]{3,2,1,0:T(8,128)(2,1)}), bf16[32,4,8,128]{3,2,1,0:T(8,128)(2,1)S(1)}, u32[]{:S(2)}, u32[]{:S(2)}) async-start(bf16[32,4,8,128]{3,2,1,0:T(8,128)(2,1)} %accumulate.1.refs_1_), calls=%async_computation.2 | async-start | bytes 524288 | tf_op jit(solution)/shard_map/all_to_all | solution.py:268
  70.0 7.5 %collective-permute-start.4 = (bf16[2,32,1024]{2,1,0:T(8,128)(2,1)S(1)}, bf16[2,32,1024]{2,1,0:T(8,128)(2,1)S(1)}, u32[]{:S(2)}, u32[]{:S(2)}) collective-permute-start(bf16[2,32,1024]{2,1,0:T(8,128)(2,1)S(1)} %settle.1.far_ref), channel_id=1, source_target_pairs={{0,2},{1,3},{2,0},{3,1},{4,6},{5,7},{6,4},{7,5},{8,10},{9,11},{10,... | collective-permute-start | bytes 393224 | tf_op jit(solution)/shard_map/ppermute | solution.py:189
  72.7 6.8 %collective-permute-start.5 = (bf16[4,2,32,1024]{3,2,1,0:T(8,128)(2,1)S(1)}, bf16[4,2,32,1024]{3,2,1,0:T(8,128)(2,1)S(1)}, u32[]{:S(2)}, u32[]{:S(2)}) collective-permute-start(bf16[4,2,32,1024]{3,2,1,0:T(8,128)(2,1)S(1)} %collect_all.2.rest_0_), channel_id=1, source_target_pairs={{0,1},{1,0},{2,3},{3,2},{4,5},{5,4},{6,7},{7,6},{8,9},{9,8},{10,11... | collective-permute-start | bytes 1572872 | tf_op jit(solution)/shard_map/ppermute | solution.py:189
  77.6 3.8 %collective-permute-start.6 = (bf16[4,2,32,1024]{3,2,1,0:T(8,128)(2,1)S(1)}, bf16[4,2,32,1024]{3,2,1,0:T(8,128)(2,1)S(1)}, u32[]{:S(2)}, u32[]{:S(2)}) collective-permute-start(bf16[4,2,32,1024]{3,2,1,0:T(8,128)(2,1)S(1)} %collect_all.3.rest_1_), channel_id=1, source_target_pairs={{0,1},{1,0},{2,3},{3,2},{4,5},{5,4},{6,7},{7,6},{8,9},{9,8},{10,11... | collective-permute-start | bytes 1572872 | tf_op jit(solution)/shard_map/ppermute | solution.py:189
  83.4 10.6 %collective-permute-start.7 = (f32[64,1024]{1,0:T(8,128)S(1)}, f32[64,1024]{1,0:T(8,128)S(1)}, u32[]{:S(2)}, u32[]{:S(2)}) collective-permute-start(f32[64,1024]{1,0:T(8,128)S(1)} %get-tuple-element.12), channel_id=1, source_target_pairs={{0,6},{1,7},{2,4},{3,5},{4,2},{5,3},{6,0},{7,1},{8,14},{9,15},{10,... | collective-permute-start | bytes 786440 | tf_op jit(solution)/shard_map/ppermute | solution.py:189

commit v6 on v5

--- a/solution.py
+++ b/solution.py
@@ -176,7 +176,7 @@
             term = jnp.dot(left[:, at * LANE : (at + 1) * LANE], right, preferred_element_type=jnp.float32)
             total = term if total is None else total + term
         mine_ref[:, col : col + wide] = total[: 2 * width]
-        theirs_ref[:, col : col + wide] = total[2 * width :]
+        theirs_ref[:, col : col + wide] = total[2 * width :].astype(theirs_ref.dtype)
 
 
 def moved(block, dz=0, dx=0, dcore=0):
@@ -266,17 +266,17 @@
     sides += [moved(side, dcore=1) for side in sides]
 
     weights = lax.all_to_all(spread, "blk", split_axis=0, concat_axis=0, tiled=True)
-    half = jax.ShapeDtypeStruct((tile_dev * width, occ), f32)
+    shape = (tile_dev * width, occ)
     mine, theirs = pl.pallas_call(
         multiply,
-        out_shape=(half, half),
+        out_shape=(jax.ShapeDtypeStruct(shape, f32), jax.ShapeDtypeStruct(shape, bf16)),
         in_specs=[VMEM] * 5,
         out_specs=(VMEM, VMEM),
         scratch_shapes=[pltpu.VMEM((2 * tile_dev * width, 2 * NZ * NC * tile_dev * width), bf16)],
         compiler_params=pltpu.CompilerParams(vmem_limit_bytes=16 * 1024 * 1024),
         name="multiply",
     )(weights, *sides)
-    return (mine + moved(theirs, dx=3)).reshape(tile_dev, width, occ)
+    return (mine + moved(theirs, dx=3).astype(f32)).reshape(tile_dev, width, occ)
 
 
 def solution(mesh):

time: 96.5 us -> 94.6 us (0.980)
  the two profiles are of different devices: /device:TPU:6 before, /device:TPU:8 now
where the time goes in v6:
time: 94.6 us; the launch traced here: 94 us
  starting transfers between devices  71 us (75%)
  waiting for transfers between devices  15.4 us (16%)
  Pallas kernels  6.03 us (6%)
    ppermute x8, starting transfers between devices, moved(): return lax.ppermute(block, 'owner', pairs)  35.9 us
    all_to_all x1, starting transfers between devices, shards(): lax.all_to_all(ordered, 'blk', split_axis=0, concat_axis=0, tiled=True)  16.7 us
    ppermute x8, waiting for transfers between devices, moved(): return lax.ppermute(block, 'owner', pairs)  9.85 us
    all_to_all x1, starting transfers between devices, shards(): lax.all_to_all(spread, 'blk', split_axis=0, concat_axis=0, tiled=True)  9.38 us
    all_to_all x1, starting transfers between devices, shards(): lax.all_to_all(outgoing, 'owner', split_axis=0, concat_axis=0, tiled=True)  8.97 us
    all_to_all x1, waiting for transfers between devices, shards(): lax.all_to_all(outgoing, 'owner', split_axis=0, concat_axis=0, tiled=True)  4.01 us
    pallas_call x1, Pallas kernels, shards(): pl.pallas_call(order_columns, out_shape=jax.ShapeDtypeStruct((width // SU...  2.41 us
  transfers between devices with their start and end apart: 11, of which 5 were waited for; matrix products, arithmetic and copies ran while one was open for 0% of the time, Pallas kernels for 3%

profile of v6, /device:TPU:8, one launch (start us, length us, event | category | flops | bytes accessed | tf_op | source)
XLA Modules:
  0.0 94.0 jit_solution(14473656309270773851)
XLA Ops:
  0.0 0.0 copy-start.4
  0.0 2.4 %order_columns.1 = bf16[4,8,8,128]{3,2,1,0:T(8,128)(2,1)} custom-call(s32[32,32]{1,0:T(8,128)} %cd_ref.1, s32[32]{0:T(128)} %count_ref.2, bf16[32,1024]{1,0:T(8,128)(2,1)} %bitcast.8), custom_call_target="tpu_custom_call" | custom-call | tf_op jit(solution)/shard_map/order_columns/pallas_call | solution.py:211
  2.4 0.0 copy-start
  2.4 0.0 copy-start.2
  2.4 16.7 %all-to-all-start = ((bf16[32,8,128]{2,1,0:T(8,128)(2,1)}), bf16[32,8,128]{2,1,0:T(8,128)(2,1)S(1)}, u32[]{:S(2)}, u32[]{:S(2)}) async-start(bf16[32,8,128]{2,1,0:T(8,128)(2,1)} %bitcast.7), calls=%async_computation | async-start | bytes 131072 | tf_op jit(solution)/shard_map/all_to_all | solution.py:220
  19.2 0.0 copy-done.4
  19.2 7.4 %collective-permute-start = (bf16[2,32,1024]{2,1,0:T(8,128)(2,1)S(1)}, bf16[2,32,1024]{2,1,0:T(8,128)(2,1)S(1)}, u32[]{:S(2)}, u32[]{:S(2)}) collective-permute-start(bf16[2,32,1024]{2,1,0:T(8,128)(2,1)S(1)} %copy-done.4), channel_id=1, source_target_pairs={{0,8},{1,9},{2,10},{3,11},{4,12},{5,13},{6,14},{7,15},{8,0},{9,1},... | collective-permute-start | bytes 393224 | tf_op jit(solution)/shard_map/ppermute | solution.py:189
  26.6 8.2 %collective-permute-start.1 = (bf16[2,32,1024]{2,1,0:T(8,128)(2,1)S(1)}, bf16[2,32,1024]{2,1,0:T(8,128)(2,1)S(1)}, u32[]{:S(2)}, u32[]{:S(2)}) collective-permute-start(bf16[2,32,1024]{2,1,0:T(8,128)(2,1)S(1)} %copy-done.4), channel_id=1, source_target_pairs={{0,24},{1,25},{2,26},{3,27},{4,28},{5,29},{6,30},{7,31},{8,16},{9,... | collective-permute-start | bytes 393224 | tf_op jit(solution)/shard_map/ppermute | solution.py:189
  34.9 0.0 all-to-all-done.rows_ref
  34.9 0.0 copy-done
  34.9 0.0 copy-done.2
  34.9 1.8 %route.1 = bf16[32,8,128]{2,1,0:T(8,128)(2,1)} custom-call(s32[32,32]{1,0:T(8,128)S(1)} %copy-done, s32[32]{0:T(128)S(1)} %copy-done.2, bf16[32,8,128]{2,1,0:T(8,128)(2,1)S(1)} %all-to-all-done.rows_ref), custom_call_target="tpu_custom_call" | custom-call | tf_op jit(solution)/shard_map/route/pallas_call | solution.py:221
  36.6 9.0 %all-to-all-start.1 = ((bf16[32,8,128]{2,1,0:T(8,128)(2,1)}), bf16[32,8,128]{2,1,0:T(8,128)(2,1)S(1)}, u32[]{:S(2)}, u32[]{:S(2)}) async-start(bf16[32,8,128]{2,1,0:T(8,128)(2,1)} %route.1), calls=%async_computation.1 | async-start | bytes 131072 | tf_op jit(solution)/shard_map/all_to_all | solution.py:244
  45.6 0.0 collective-permute-done.first_ref
  45.6 0.0 collective-permute-done.1.second_ref
  45.6 0.0 copy-start.1
  45.7 3.7 %collective-permute-start.3 = (bf16[3,2,32,1024]{3,2,1,0:T(8,128)(2,1)S(1)}, bf16[3,2,32,1024]{3,2,1,0:T(8,128)(2,1)S(1)}, u32[]{:S(2)}, u32[]{:S(2)}) collective-permute-start(bf16[3,2,32,1024]{3,2,1,0:T(8,128)(2,1)S(1)} %get-tuple-element.9.near_ref), channel_id=1, source_target_pairs={{0,2},{1,3},{2,0},{3,1},{4,6},{5,7},{6,4},{7,5},{8,10},{9,11},{10,... | collective-permute-start | bytes 1179656 | tf_op jit(solution)/shard_map/ppermute | solution.py:189
  49.4 7.5 %collective-permute-start.2 = (bf16[2,32,1024]{2,1,0:T(8,128)(2,1)S(1)}, bf16[2,32,1024]{2,1,0:T(8,128)(2,1)S(1)}, u32[]{:S(2)}, u32[]{:S(2)}) collective-permute-start(bf16[2,32,1024]{2,1,0:T(8,128)(2,1)S(1)} %get-tuple-element.10), channel_id=1, source_target_pairs={{0,24},{1,25},{2,26},{3,27},{4,28},{5,29},{6,30},{7,31},{8,16},{9,... | collective-permute-start | bytes 393224 | tf_op jit(solution)/shard_map/ppermute | solution.py:189
  56.9 4.0 %all-to-all-done.1.rows_ref = bf16[32,8,128]{2,1,0:T(8,128)(2,1)S(1)} async-done(((bf16[32,8,128]{2,1,0:T(8,128)(2,1)}), bf16[32,8,128]{2,1,0:T(8,128)(2,1)S(1)}, u32[]{:S(2)}, u32[]{:S(2)}) %all-to-all-start.1) | async-done | bytes 65568 | tf_op jit(solution)/shard_map/all_to_all | solution.py:244
  60.9 0.0 copy-start.3
  60.9 0.0 copy-done.1
  60.9 0.7 copy-done.3
  61.6 1.0 %accumulate.1.refs_1_ = bf16[32,4,8,128]{3,2,1,0:T(8,128)(2,1)} custom-call(s32[32,32]{1,0:T(8,128)S(1)} %copy-done, s32[1,32]{1,0:T(1,128)S(1)} %bitcast.5, s32[32,32]{1,0:T(8,128)S(1)} %copy-done.1, s32[1,32]{1,0:T(1,128)S(1)} %bitcast.6, bf16[32,8,128]{2,1,0:T(8,128)(2,1)S(1)} %all-to-all-done.1.rows_ref), custom_call_target="tpu_custom_call" | custom-call | tf_op jit(solution)/shard_map/accumulate/pallas_call | solution.py:245
  62.5 9.4 %all-to-all-start.2 = ((bf16[32,4,8,128]{3,2,1,0:T(8,128)(2,1)}), bf16[32,4,8,128]{3,2,1,0:T(8,128)(2,1)S(1)}, u32[]{:S(2)}, u32[]{:S(2)}) async-start(bf16[32,4,8,128]{3,2,1,0:T(8,128)(2,1)} %accumulate.1.refs_1_), calls=%async_computation.2 | async-start | bytes 524288 | tf_op jit(solution)/shard_map/all_to_all | solution.py:268
  71.9 0.0 collective-permute-done.2.refs_0_
  71.9 2.0 %collective-permute-start.4 = (bf16[2,32,1024]{2,1,0:T(8,128)(2,1)S(1)}, bf16[2,32,1024]{2,1,0:T(8,128)(2,1)S(1)}, u32[]{:S(2)}, u32[]{:S(2)}) collective-permute-start(bf16[2,32,1024]{2,1,0:T(8,128)(2,1)S(1)} %settle.1.far_ref), channel_id=1, source_target_pairs={{0,2},{1,3},{2,0},{3,1},{4,6},{5,7},{6,4},{7,5},{8,10},{9,11},{10,... | collective-permute-start | bytes 393224 | tf_op jit(solution)/shard_map/ppermute | solution.py:189
  74.0 1.9 %collective-permute-start.5 = (bf16[4,2,32,1024]{3,2,1,0:T(8,128)(2,1)S(1)}, bf16[4,2,32,1024]{3,2,1,0:T(8,128)(2,1)S(1)}, u32[]{:S(2)}, u32[]{:S(2)}) collective-permute-start(bf16[4,2,32,1024]{3,2,1,0:T(8,128)(2,1)S(1)} %collect_all.2.rest_0_), channel_id=1, source_target_pairs={{0,1},{1,0},{2,3},{3,2},{4,5},{5,4},{6,7},{7,6},{8,9},{9,8},{10,11... | collective-permute-start | bytes 1572872 | tf_op jit(solution)/shard_map/ppermute | solution.py:189
  76.0 0.0 collective-permute-done.3.near_ref
  76.0 3.0 %collective-permute-done.4.far_ref = bf16[2,32,1024]{2,1,0:T(8,128)(2,1)S(1)} collective-permute-done((bf16[2,32,1024]{2,1,0:T(8,128)(2,1)S(1)}, bf16[2,32,1024]{2,1,0:T(8,128)(2,1)S(1)}, u32[]{:S(2)}, u32[]{:S(2)}) %collective-permute-start.4) | collective-permute-done | bytes 131104 | tf_op jit(solution)/shard_map/ppermute | solution.py:189
  79.0 1.9 %collective-permute-start.6 = (bf16[4,2,32,1024]{3,2,1,0:T(8,128)(2,1)S(1)}, bf16[4,2,32,1024]{3,2,1,0:T(8,128)(2,1)S(1)}, u32[]{:S(2)}, u32[]{:S(2)}) collective-permute-start(bf16[4,2,32,1024]{3,2,1,0:T(8,128)(2,1)S(1)} %collect_all.3.rest_1_), channel_id=1, source_target_pairs={{0,1},{1,0},{2,3},{3,2},{4,5},{5,4},{6,7},{7,6},{8,9},{9,8},{10,11... | collective-permute-start | bytes 1572872 | tf_op jit(solution)/shard_map/ppermute | solution.py:189
  81.0 0.0 collective-permute-done.5.rest_2_
  81.0 1.9 %collective-permute-done.6.rest_3_ = bf16[4,2,32,1024]{3,2,1,0:T(8,128)(2,1)S(1)} collective-permute-done((bf16[4,2,32,1024]{3,2,1,0:T(8,128)(2,1)S(1)}, bf16[4,2,32,1024]{3,2,1,0:T(8,128)(2,1)S(1)}, u32[]{:S(2)}, u32[]{:S(2)}) %collective-permute-start.6) | collective-permute-done | bytes 524320 | tf_op jit(solution)/shard_map/ppermute | solution.py:189
  82.9 1.5 %all-to-all-done.2.weights_ref = bf16[32,4,8,128]{3,2,1,0:T(8,128)(2,1)S(1)} async-done(((bf16[32,4,8,128]{3,2,1,0:T(8,128)(2,1)}), bf16[32,4,8,128]{3,2,1,0:T(8,128)(2,1)S(1)}, u32[]{:S(2)}, u32[]{:S(2)}) %all-to-all-start.2) | async-done | bytes 262176 | tf_op jit(solution)/shard_map/all_to_all | solution.py:268
  84.4 0.8 multiply.1
  85.2 3.1 %collective-permute-start.7 = (bf16[64,1024]{1,0:T(8,128)(2,1)S(1)}, bf16[64,1024]{1,0:T(8,128)(2,1)S(1)}, u32[]{:S(2)}, u32[]{:S(2)}) collective-permute-start(bf16[64,1024]{1,0:T(8,128)(2,1)S(1)} %get-tuple-element.12), channel_id=1, source_target_pairs={{0,6},{1,7},{2,4},{3,5},{4,2},{5,3},{6,0},{7,1},{8,14},{9,15},{10,... | collective-permute-start | bytes 393224 | tf_op jit(solution)/shard_map/ppermute | solution.py:189
  88.3 4.9 %collective-permute-done.7 = bf16[64,1024]{1,0:T(8,128)(2,1)S(1)} collective-permute-done((bf16[64,1024]{1,0:T(8,128)(2,1)S(1)}, bf16[64,1024]{1,0:T(8,128)(2,1)S(1)}, u32[]{:S(2)}, u32[]{:S(2)}) %collective-permute-start.7) | collective-permute-done | bytes 131104 | tf_op jit(solution)/shard_map/ppermute | solution.py:189
  93.2 0.7 convert_add_fusion
  (4 shorter events, 0.1 us)
Async XLA Ops:
  0.0 19.2 %copy-start.4 = (bf16[2,32,1024]{2,1,0:T(8,128)(2,1)S(1)}, bf16[2,32,1024]{2,1,0:T(8,128)(2,1)}, u32[]{:S(2)}) copy-start(bf16[2,32,1024]{2,1,0:T(8,128)(2,1)} %own_ref.1) | copy-start | bytes 393220
  2.4 32.4 %copy-start = (s32[32,32]{1,0:T(8,128)S(1)}, s32[32,32]{1,0:T(8,128)}, u32[]{:S(2)}) copy-start(s32[32,32]{1,0:T(8,128)} %ab_ref.1) | copy-start | bytes 12292
  2.4 32.5 %copy-start.2 = (s32[32]{0:T(128)S(1)}, s32[32]{0:T(128)}, u32[]{:S(2)}) copy-start(s32[32]{0:T(128)} %count_ref.3) | copy-start | bytes 388
  2.4 32.4 %all-to-all-start = ((bf16[32,8,128]{2,1,0:T(8,128)(2,1)}), bf16[32,8,128]{2,1,0:T(8,128)(2,1)S(1)}, u32[]{:S(2)}, u32[]{:S(2)}) async-start(bf16[32,8,128]{2,1,0:T(8,128)(2,1)} %bitcast.7), calls=%async_computation | async-start | bytes 131072 | tf_op jit(solution)/shard_map/all_to_all | solution.py:220
  19.2 26.4 %collective-permute-start = (bf16[2,32,1024]{2,1,0:T(8,128)(2,1)S(1)}, bf16[2,32,1024]{2,1,0:T(8,128)(2,1)S(1)}, u32[]{:S(2)}, u32[]{:S(2)}) collective-permute-start(bf16[2,32,1024]{2,1,0:T(8,128)(2,1)S(1)} %copy-done.4), channel_id=1, source_target_pairs={{0,8},{1,9},{2,10},{3,11},{4,12},{5,13},{6,14},{7,15},{8,0},{9,1},... | collective-permute-start | bytes 393224 | tf_op jit(solution)/shard_map/ppermute | solution.py:189
  26.6 19.0 %collective-permute-start.1 = (bf16[2,32,1024]{2,1,0:T(8,128)(2,1)S(1)}, bf16[2,32,1024]{2,1,0:T(8,128)(2,1)S(1)}, u32[]{:S(2)}, u32[]{:S(2)}) collective-permute-start(bf16[2,32,1024]{2,1,0:T(8,128)(2,1)S(1)} %copy-done.4), channel_id=1, source_target_pairs={{0,24},{1,25},{2,26},{3,27},{4,28},{5,29},{6,30},{7,31},{8,16},{9,... | collective-permute-start | bytes 393224 | tf_op jit(solution)/shard_map/ppermute | solution.py:189
  36.6 24.3 %all-to-all-start.1 = ((bf16[32,8,128]{2,1,0:T(8,128)(2,1)}), bf16[32,8,128]{2,1,0:T(8,128)(2,1)S(1)}, u32[]{:S(2)}, u32[]{:S(2)}) async-start(bf16[32,8,128]{2,1,0:T(8,128)(2,1)} %route.1), calls=%async_computation.1 | async-start | bytes 131072 | tf_op jit(solution)/shard_map/all_to_all | solution.py:244
  45.6 15.3 %copy-start.1 = (s32[32,32]{1,0:T(8,128)S(1)}, s32[32,32]{1,0:T(8,128)}, u32[]{:S(2)}) copy-start(s32[32,32]{1,0:T(8,128)} %cd_ref.1) | copy-start | bytes 12292
  45.7 30.3 %collective-permute-start.3 = (bf16[3,2,32,1024]{3,2,1,0:T(8,128)(2,1)S(1)}, bf16[3,2,32,1024]{3,2,1,0:T(8,128)(2,1)S(1)}, u32[]{:S(2)}, u32[]{:S(2)}) collective-permute-start(bf16[3,2,32,1024]{3,2,1,0:T(8,128)(2,1)S(1)} %get-tuple-element.9.near_ref), channel_id=1, source_target_pairs={{0,2},{1,3},{2,0},{3,1},{4,6},{5,7},{6,4},{7,5},{8,10},{9,11},{10,... | collective-permute-start | bytes 1179656 | tf_op jit(solution)/shard_map/ppermute | solution.py:189
  49.4 22.5 %collective-permute-start.2 = (bf16[2,32,1024]{2,1,0:T(8,128)(2,1)S(1)}, bf16[2,32,1024]{2,1,0:T(8,128)(2,1)S(1)}, u32[]{:S(2)}, u32[]{:S(2)}) collective-permute-start(bf16[2,32,1024]{2,1,0:T(8,128)(2,1)S(1)} %get-tuple-element.10), channel_id=1, source_target_pairs={{0,24},{1,25},{2,26},{3,27},{4,28},{5,29},{6,30},{7,31},{8,16},{9,... | collective-permute-start | bytes 393224 | tf_op jit(solution)/shard_map/ppermute | solution.py:189
  60.9 0.7 copy-start.3
  62.5 21.8 %all-to-all-start.2 = ((bf16[32,4,8,128]{3,2,1,0:T(8,128)(2,1)}), bf16[32,4,8,128]{3,2,1,0:T(8,128)(2,1)S(1)}, u32[]{:S(2)}, u32[]{:S(2)}) async-start(bf16[32,4,8,128]{3,2,1,0:T(8,128)(2,1)} %accumulate.1.refs_1_), calls=%async_computation.2 | async-start | bytes 524288 | tf_op jit(solution)/shard_map/all_to_all | solution.py:268
  71.9 7.1 %collective-permute-start.4 = (bf16[2,32,1024]{2,1,0:T(8,128)(2,1)S(1)}, bf16[2,32,1024]{2,1,0:T(8,128)(2,1)S(1)}, u32[]{:S(2)}, u32[]{:S(2)}) collective-permute-start(bf16[2,32,1024]{2,1,0:T(8,128)(2,1)S(1)} %settle.1.far_ref), channel_id=1, source_target_pairs={{0,2},{1,3},{2,0},{3,1},{4,6},{5,7},{6,4},{7,5},{8,10},{9,11},{10,... | collective-permute-start | bytes 393224 | tf_op jit(solution)/shard_map/ppermute | solution.py:189
  74.0 6.9 %collective-permute-start.5 = (bf16[4,2,32,1024]{3,2,1,0:T(8,128)(2,1)S(1)}, bf16[4,2,32,1024]{3,2,1,0:T(8,128)(2,1)S(1)}, u32[]{:S(2)}, u32[]{:S(2)}) collective-permute-start(bf16[4,2,32,1024]{3,2,1,0:T(8,128)(2,1)S(1)} %collect_all.2.rest_0_), channel_id=1, source_target_pairs={{0,1},{1,0},{2,3},{3,2},{4,5},{5,4},{6,7},{7,6},{8,9},{9,8},{10,11... | collective-permute-start | bytes 1572872 | tf_op jit(solution)/shard_map/ppermute | solution.py:189
  79.0 3.8 %collective-permute-start.6 = (bf16[4,2,32,1024]{3,2,1,0:T(8,128)(2,1)S(1)}, bf16[4,2,32,1024]{3,2,1,0:T(8,128)(2,1)S(1)}, u32[]{:S(2)}, u32[]{:S(2)}) collective-permute-start(bf16[4,2,32,1024]{3,2,1,0:T(8,128)(2,1)S(1)} %collect_all.3.rest_1_), channel_id=1, source_target_pairs={{0,1},{1,0},{2,3},{3,2},{4,5},{5,4},{6,7},{7,6},{8,9},{9,8},{10,11... | collective-permute-start | bytes 1572872 | tf_op jit(solution)/shard_map/ppermute | solution.py:189
  85.2 8.1 %collective-permute-start.7 = (bf16[64,1024]{1,0:T(8,128)(2,1)S(1)}, bf16[64,1024]{1,0:T(8,128)(2,1)S(1)}, u32[]{:S(2)}, u32[]{:S(2)}) collective-permute-start(bf16[64,1024]{1,0:T(8,128)(2,1)S(1)} %get-tuple-element.12), channel_id=1, source_target_pairs={{0,6},{1,7},{2,4},{3,5},{4,2},{5,3},{6,0},{7,1},{8,14},{9,15},{10,... | collective-permute-start | bytes 393224 | tf_op jit(solution)/shard_map/ppermute | solution.py:189

commit v7 on v6

--- a/solution.py
+++ b/solution.py
@@ -84,8 +84,7 @@
                 out_ref[owner_index(z, x, core)] = merged.astype(out_ref.dtype)
 
 
-def accumulate(ab_ref, ab_count_ref, cd_ref, cd_count_ref, rows_ref, *rest):
-    out_ref, mask = rest[-2:]
+def make_masks(ab_ref, ab_count_ref, cd_ref, cd_count_ref, mask):
     own, piece = lax.axis_index("owner"), lax.axis_index("blk")
     chunk = piece % (NZ * NC)
     z, x, core = own // (NX * NC), (own // NC) % NX, own % NC
@@ -120,8 +119,11 @@
         rows_hit = ab_hit(low)
         for par in range(2):
             mask[low * 2 + par] = rows_hit * cd_hits[par]
+
+
+def accumulate(mask, rows_ref, out_ref):
     totals = [jnp.zeros((SUB, LANE), jnp.float32) for _ in range(4)]
-    for task in range(tasks):
+    for task in range(rows_ref.shape[0]):
         rows = rows_ref[task].astype(jnp.float32)
         for kind in range(4):
             totals[kind] += rows * mask[kind, task : task + 1, :]
@@ -131,7 +133,10 @@
             out_ref[target, kind] = rounded
 
 
-def collect_near(own_ref, first_ref, second_ref, near_ref, relay_ref):
+def collect_near(*refs):
+    own_ref, first_ref, second_ref, _ = refs[:4]
+    near_ref, relay_ref, mask = refs[8:]
+    make_masks(*refs[4:8], mask)
     for place, ref in enumerate((own_ref, first_ref, second_ref)):
         near_ref[place] = ref[...]
     relay_ref[...] = first_ref[...]
@@ -141,16 +146,18 @@
     pass
 
 
-def collect_all(near_ref, far_ref, out_ref):
-    out_ref[: NZ - 1] = near_ref[...]
+def collect_rest(near_pair_ref, far_ref, far_pair_ref, _, out_ref):
+    out_ref[: NZ - 1] = near_pair_ref[...]
     out_ref[NZ - 1] = far_ref[...]
+    out_ref[NZ] = far_pair_ref[...]
 
 
 def multiply(weights_ref, *rest):
-    amps_refs, (mine_ref, theirs_ref, left) = rest[:4], rest[4:]
+    mine_ref, theirs_ref, left = rest[4:]
+    amps = [((near, more, NZ - 1), (more, more, NZ)) for near, more in (rest[:2], rest[2:4])]
     own = lax.axis_index("owner")
     z, core = own // (NX * NC), own % NC
-    width, occ = amps_refs[0].shape[2:]
+    width, occ = rest[0].shape[2:]
     chunks = NZ * NC
     blocks = [(par, d, side) for par in range(2) for d in range(2) for side in range(NC)]
     for kind in range(4):
@@ -172,7 +179,9 @@
     for col in range(0, occ, wide):
         total = None
         for at, (par, d, side) in enumerate(blocks):
-            right = amps_refs[2 * side + d][:, par, :, col : col + wide].reshape(LANE, wide)
+            near, far, last = amps[side][d]
+            right = [ref[place, par, :, col : col + wide] for ref, place in ((near, 0), (near, 1), (near, 2), (far, last))]
+            right = jnp.concatenate(right, axis=0)
             term = jnp.dot(left[:, at * LANE : (at + 1) * LANE], right, preferred_element_type=jnp.float32)
             total = term if total is None else total + term
         mine_ref[:, col : col + wide] = total[: 2 * width]
@@ -187,18 +196,6 @@
         for core in range(NC)
     ]
     return lax.ppermute(block, "owner", pairs)
-
-
-def joined(near, far, flops):
-    return pl.pallas_call(
-        collect_all,
-        out_shape=jax.ShapeDtypeStruct((near.shape[0] + 1, *near.shape[1:]), near.dtype),
-        in_specs=[VMEM] * 2,
-        out_specs=VMEM,
-        cost_estimate=pl.CostEstimate(flops=flops, bytes_accessed=near.size * 6, transcendentals=0),
-        compiler_params=SMALL,
-        name="collect_all",
-    )(near, far)
 
 
 def shards(amplitudes, integrals, cd_tiles, cd_count, ab_tiles, ab_count):
@@ -227,43 +224,52 @@
         compiler_params=SMALL,
         name="route",
     )(ab_tiles, ab_count, mine)
-    near, relay = pl.pallas_call(
+    near, relay, mask = pl.pallas_call(
         collect_near,
         out_shape=(
             jax.ShapeDtypeStruct((NZ - 1, tile_dev, width, occ), bf16),
             jax.ShapeDtypeStruct(second.shape, bf16),
+            jax.ShapeDtypeStruct((4, tasks, LANE), f32),
         ),
-        in_specs=[VMEM] * 3,
-        out_specs=(VMEM, VMEM),
+        in_specs=[VMEM] * 3 + [ANY] + [VMEM] * 4,
+        out_specs=(VMEM, VMEM, VMEM),
         cost_estimate=pl.CostEstimate(flops=10000000000, bytes_accessed=amplitudes.size * 16, transcendentals=0),
         compiler_params=SMALL,
         name="collect_near",
-    )(amplitudes, first, second)
+    )(amplitudes, first, second, mine, ab_tiles, ab_count[None, :], cd_tiles, cd_count[None, :])
     near_pair = moved(near, dx=1)
+    near_other = moved(near, dcore=1)
     far = moved(relay, 3)
     arrived = lax.all_to_all(outgoing, "owner", split_axis=0, concat_axis=0, tiled=True)
     spread = pl.pallas_call(
         accumulate,
         out_shape=jax.ShapeDtypeStruct((pieces, 4, SUB, LANE), bf16),
-        in_specs=[VMEM] * 5,
-        out_specs=VMEM,
-        scratch_shapes=[pltpu.VMEM((4, tasks, LANE), f32)],
+        in_specs=[VMEM] * 2,
+        out_specs=VMEM,
         compiler_params=SMALL,
         name="accumulate",
-    )(ab_tiles, ab_count[None, :], cd_tiles, cd_count[None, :], arrived)
+    )(mask, arrived)
     far = pl.pallas_call(
         settle,
         out_shape=jax.ShapeDtypeStruct(far.shape, far.dtype),
         in_specs=[ANY, ANY],
         out_specs=ANY,
         input_output_aliases={0: 0},
-        cost_estimate=pl.CostEstimate(flops=1000000, bytes_accessed=far.size * 4, transcendentals=0),
+        cost_estimate=pl.CostEstimate(flops=2000000000, bytes_accessed=far.size * 4, transcendentals=0),
         compiler_params=SMALL,
         name="settle",
     )(far, spread)
     far_pair = moved(far, dx=1)
-    sides = [joined(near, far, 2000000000), joined(near_pair, far_pair, 5000000000)]
-    sides += [moved(side, dcore=1) for side in sides]
+    rest = pl.pallas_call(
+        collect_rest,
+        out_shape=jax.ShapeDtypeStruct((NZ + 1, tile_dev, width, occ), bf16),
+        in_specs=[VMEM] * 3 + [ANY],
+        out_specs=VMEM,
+        cost_estimate=pl.CostEstimate(flops=2000000000, bytes_accessed=amplitudes.size * 20, transcendentals=0),
+        compiler_params=SMALL,
+        name="collect_rest",
+    )(near_pair, far, far_pair, near_other)
+    sides = [near, rest, near_other, moved(rest, dcore=1)]
 
     weights = lax.all_to_all(spread, "blk", split_axis=0, concat_axis=0, tiled=True)
     shape = (tile_dev * width, occ)

time: 94.6 us -> 93.9 us (level)
    all_to_all x1, waiting for transfers between devices: 4.01 us -> 1.4 us  [shards(): lax.all_to_all(outgoing, 'owner', split_axis=0, concat_axis=0, tiled=True)]
    ppermute x8, waiting for transfers between devices: 9.85 us -> 12 us  [moved(): return lax.ppermute(block, 'owner', pairs)]
where the time goes in v7:
time: 93.9 us; the launch traced here: 93.3 us
  starting transfers between devices  71 us (76%)
  waiting for transfers between devices  14.7 us (16%)
  Pallas kernels  5.96 us (6%)
    ppermute x8, starting transfers between devices, moved(): return lax.ppermute(block, 'owner', pairs)  35.8 us
    all_to_all x1, starting transfers between devices, shards(): lax.all_to_all(ordered, 'blk', split_axis=0, concat_axis=0, tiled=True)  16.7 us
    ppermute x8, waiting for transfers between devices, moved(): return lax.ppermute(block, 'owner', pairs)  12 us
    all_to_all x1, starting transfers between devices, shards(): lax.all_to_all(spread, 'blk', split_axis=0, concat_axis=0, tiled=True)  9.38 us
    all_to_all x1, starting transfers between devices, shards(): lax.all_to_all(outgoing, 'owner', split_axis=0, concat_axis=0, tiled=True)  9.11 us
    pallas_call x1, Pallas kernels, shards(): pl.pallas_call(order_columns, out_shape=jax.ShapeDtypeStruct((width // SU...  2.41 us
  transfers between devices with their start and end apart: 11, of which 5 were waited for; matrix products, arithmetic and copies ran while one was open for 0% of the time, Pallas kernels for 3%

profile of v7, /device:TPU:8, one launch (start us, length us, event | category | flops | bytes accessed | tf_op | source)
XLA Modules:
  0.0 93.3 jit_solution(9840061068080428721)
XLA Ops:
  0.0 0.0 copy-start.4
  0.0 2.4 %order_columns.1 = bf16[4,8,8,128]{3,2,1,0:T(8,128)(2,1)} custom-call(s32[32,32]{1,0:T(8,128)} %refs_6_.1, s32[32]{0:T(128)} %count_ref.2, bf16[32,1024]{1,0:T(8,128)(2,1)} %bitcast.8), custom_call_target="tpu_custom_call" | custom-call | tf_op jit(solution)/shard_map/order_columns/pallas_call | solution.py:208
  2.4 0.0 copy-start.1
  2.4 0.0 copy-start.3
  2.4 16.7 %all-to-all-start = ((bf16[32,8,128]{2,1,0:T(8,128)(2,1)}), bf16[32,8,128]{2,1,0:T(8,128)(2,1)S(1)}, u32[]{:S(2)}, u32[]{:S(2)}) async-start(bf16[32,8,128]{2,1,0:T(8,128)(2,1)} %bitcast.7), calls=%async_computation | async-start | bytes 131072 | tf_op jit(solution)/shard_map/all_to_all | solution.py:217
  19.2 0.0 copy-done.4
  19.2 7.4 %collective-permute-start = (bf16[2,32,1024]{2,1,0:T(8,128)(2,1)S(1)}, bf16[2,32,1024]{2,1,0:T(8,128)(2,1)S(1)}, u32[]{:S(2)}, u32[]{:S(2)}) collective-permute-start(bf16[2,32,1024]{2,1,0:T(8,128)(2,1)S(1)} %copy-done.4), channel_id=1, source_target_pairs={{0,8},{1,9},{2,10},{3,11},{4,12},{5,13},{6,14},{7,15},{8,0},{9,1},... | collective-permute-start | bytes 393224 | tf_op jit(solution)/shard_map/ppermute | solution.py:198
  26.6 8.2 %collective-permute-start.1 = (bf16[2,32,1024]{2,1,0:T(8,128)(2,1)S(1)}, bf16[2,32,1024]{2,1,0:T(8,128)(2,1)S(1)}, u32[]{:S(2)}, u32[]{:S(2)}) collective-permute-start(bf16[2,32,1024]{2,1,0:T(8,128)(2,1)S(1)} %copy-done.4), channel_id=1, source_target_pairs={{0,24},{1,25},{2,26},{3,27},{4,28},{5,29},{6,30},{7,31},{8,16},{9,... | collective-permute-start | bytes 393224 | tf_op jit(solution)/shard_map/ppermute | solution.py:198
  34.8 0.0 all-to-all-done.refs_3_.rows_ref
  34.9 0.0 copy-done.1
  34.9 0.0 copy-done.3
  34.9 1.8 %route.1 = bf16[32,8,128]{2,1,0:T(8,128)(2,1)} custom-call(s32[32,32]{1,0:T(8,128)S(1)} %copy-done.1, s32[32]{0:T(128)S(1)} %copy-done.3, bf16[32,8,128]{2,1,0:T(8,128)(2,1)S(1)} %all-to-all-done.refs_3_.rows_ref), custom_call_target="tpu_custom_call" | custom-call | tf_op jit(solution)/shard_map/route/pallas_call | solution.py:218
  36.6 0.0 copy-start
  36.6 9.1 %all-to-all-start.1 = ((bf16[32,8,128]{2,1,0:T(8,128)(2,1)}), bf16[32,8,128]{2,1,0:T(8,128)(2,1)S(1)}, u32[]{:S(2)}, u32[]{:S(2)}) async-start(bf16[32,8,128]{2,1,0:T(8,128)(2,1)} %route.1), calls=%async_computation.1 | async-start | bytes 131072 | tf_op jit(solution)/shard_map/all_to_all | solution.py:243
  45.8 0.0 collective-permute-done.refs_1_
  45.8 0.0 collective-permute-done.1.refs_2_
  45.8 0.0 copy-start.2
  45.8 0.0 copy-done
  45.8 0.6 copy-done.2
  46.4 0.2 collect_near.1
  46.6 7.7 %collective-permute-start.3 = (bf16[2,32,1024]{2,1,0:T(8,128)(2,1)S(1)}, bf16[2,32,1024]{2,1,0:T(8,128)(2,1)S(1)}, u32[]{:S(2)}, u32[]{:S(2)}) collective-permute-start(bf16[2,32,1024]{2,1,0:T(8,128)(2,1)S(1)} %get-tuple-element.12), channel_id=1, source_target_pairs={{0,24},{1,25},{2,26},{3,27},{4,28},{5,29},{6,30},{7,31},{8,16},{9,... | collective-permute-start | bytes 393224 | tf_op jit(solution)/shard_map/ppermute | solution.py:198
  54.3 1.9 %collective-permute-start.5 = (bf16[3,2,32,1024]{3,2,1,0:T(8,128)(2,1)S(1)}, bf16[3,2,32,1024]{3,2,1,0:T(8,128)(2,1)S(1)}, u32[]{:S(2)}, u32[]{:S(2)}) collective-permute-start(bf16[3,2,32,1024]{3,2,1,0:T(8,128)(2,1)S(1)} %get-tuple-element.11.rest_0_), channel_id=1, source_target_pairs={{0,1},{1,0},{2,3},{3,2},{4,5},{5,4},{6,7},{7,6},{8,9},{9,8},{10,11... | collective-permute-start | bytes 1179656 | tf_op jit(solution)/shard_map/ppermute | solution.py:198
  56.3 3.4 %collective-permute-start.2 = (bf16[3,2,32,1024]{3,2,1,0:T(8,128)(2,1)S(1)}, bf16[3,2,32,1024]{3,2,1,0:T(8,128)(2,1)S(1)}, u32[]{:S(2)}, u32[]{:S(2)}) collective-permute-start(bf16[3,2,32,1024]{3,2,1,0:T(8,128)(2,1)S(1)} %get-tuple-element.11.rest_0_), channel_id=1, source_target_pairs={{0,2},{1,3},{2,0},{3,1},{4,6},{5,7},{6,4},{7,5},{8,10},{9,11},{10,... | collective-permute-start | bytes 1179656 | tf_op jit(solution)/shard_map/ppermute | solution.py:198
  59.7 1.4 %all-to-all-done.1.rows_ref = bf16[32,8,128]{2,1,0:T(8,128)(2,1)S(1)} async-done(((bf16[32,8,128]{2,1,0:T(8,128)(2,1)}), bf16[32,8,128]{2,1,0:T(8,128)(2,1)S(1)}, u32[]{:S(2)}, u32[]{:S(2)}) %all-to-all-start.1) | async-done | bytes 65568 | tf_op jit(solution)/shard_map/all_to_all | solution.py:243
  61.1 0.8 accumulate.1.refs_1_
  61.9 9.4 %all-to-all-start.2 = ((bf16[32,4,8,128]{3,2,1,0:T(8,128)(2,1)}), bf16[32,4,8,128]{3,2,1,0:T(8,128)(2,1)S(1)}, u32[]{:S(2)}, u32[]{:S(2)}) async-start(bf16[32,4,8,128]{3,2,1,0:T(8,128)(2,1)} %accumulate.1.refs_1_), calls=%async_computation.2 | async-start | bytes 524288 | tf_op jit(solution)/shard_map/all_to_all | solution.py:274
  71.2 0.0 collective-permute-done.3.refs_0_
  71.3 2.1 %collective-permute-start.4 = (bf16[2,32,1024]{2,1,0:T(8,128)(2,1)S(1)}, bf16[2,32,1024]{2,1,0:T(8,128)(2,1)S(1)}, u32[]{:S(2)}, u32[]{:S(2)}) collective-permute-start(bf16[2,32,1024]{2,1,0:T(8,128)(2,1)S(1)} %settle.1.far_ref), channel_id=1, source_target_pairs={{0,2},{1,3},{2,0},{3,1},{4,6},{5,7},{6,4},{7,5},{8,10},{9,11},{10,... | collective-permute-start | bytes 393224 | tf_op jit(solution)/shard_map/ppermute | solution.py:198
  73.3 5.0 %collective-permute-done.4.far_pair_ref = bf16[2,32,1024]{2,1,0:T(8,128)(2,1)S(1)} collective-permute-done((bf16[2,32,1024]{2,1,0:T(8,128)(2,1)S(1)}, bf16[2,32,1024]{2,1,0:T(8,128)(2,1)S(1)}, u32[]{:S(2)}, u32[]{:S(2)}) %collective-permute-start.4) | collective-permute-done | bytes 131104 | tf_op jit(solution)/shard_map/ppermute | solution.py:198
  78.3 0.0 collective-permute-done.5._.rest_2_
  78.3 0.0 collective-permute-done.2.near_pair_ref
  78.4 1.9 %collective-permute-start.6 = (bf16[5,2,32,1024]{3,2,1,0:T(8,128)(2,1)S(1)}, bf16[5,2,32,1024]{3,2,1,0:T(8,128)(2,1)S(1)}, u32[]{:S(2)}, u32[]{:S(2)}) collective-permute-start(bf16[5,2,32,1024]{3,2,1,0:T(8,128)(2,1)S(1)} %collect_rest.1.rest_1_), channel_id=1, source_target_pairs={{0,1},{1,0},{2,3},{3,2},{4,5},{5,4},{6,7},{7,6},{8,9},{9,8},{10,11... | collective-permute-start | bytes 1966088 | tf_op jit(solution)/shard_map/ppermute | solution.py:198
  80.3 2.1 %collective-permute-done.6.rest_3_ = bf16[5,2,32,1024]{3,2,1,0:T(8,128)(2,1)S(1)} collective-permute-done((bf16[5,2,32,1024]{3,2,1,0:T(8,128)(2,1)S(1)}, bf16[5,2,32,1024]{3,2,1,0:T(8,128)(2,1)S(1)}, u32[]{:S(2)}, u32[]{:S(2)}) %collective-permute-start.6) | collective-permute-done | bytes 655392 | tf_op jit(solution)/shard_map/ppermute | solution.py:198
  82.4 1.3 %all-to-all-done.2.weights_ref = bf16[32,4,8,128]{3,2,1,0:T(8,128)(2,1)S(1)} async-done(((bf16[32,4,8,128]{3,2,1,0:T(8,128)(2,1)}), bf16[32,4,8,128]{3,2,1,0:T(8,128)(2,1)S(1)}, u32[]{:S(2)}, u32[]{:S(2)}) %all-to-all-start.2) | async-done | bytes 262176 | tf_op jit(solution)/shard_map/all_to_all | solution.py:274
  83.7 0.8 multiply.1
  84.4 3.1 %collective-permute-start.7 = (bf16[64,1024]{1,0:T(8,128)(2,1)S(1)}, bf16[64,1024]{1,0:T(8,128)(2,1)S(1)}, u32[]{:S(2)}, u32[]{:S(2)}) collective-permute-start(bf16[64,1024]{1,0:T(8,128)(2,1)S(1)} %get-tuple-element.14), channel_id=1, source_target_pairs={{0,6},{1,7},{2,4},{3,5},{4,2},{5,3},{6,0},{7,1},{8,14},{9,15},{10,... | collective-permute-start | bytes 393224 | tf_op jit(solution)/shard_map/ppermute | solution.py:198
  87.6 4.9 %collective-permute-done.7 = bf16[64,1024]{1,0:T(8,128)(2,1)S(1)} collective-permute-done((bf16[64,1024]{1,0:T(8,128)(2,1)S(1)}, bf16[64,1024]{1,0:T(8,128)(2,1)S(1)}, u32[]{:S(2)}, u32[]{:S(2)}) %collective-permute-start.7) | collective-permute-done | bytes 131104 | tf_op jit(solution)/shard_map/ppermute | solution.py:198
  92.5 0.7 convert_add_fusion
  (2 shorter events, 0.0 us)
Async XLA Ops:
  0.0 19.2 %copy-start.4 = (bf16[2,32,1024]{2,1,0:T(8,128)(2,1)S(1)}, bf16[2,32,1024]{2,1,0:T(8,128)(2,1)}, u32[]{:S(2)}) copy-start(bf16[2,32,1024]{2,1,0:T(8,128)(2,1)} %refs_0_.1) | copy-start | bytes 393220
  2.4 32.4 %copy-start.1 = (s32[32,32]{1,0:T(8,128)S(1)}, s32[32,32]{1,0:T(8,128)}, u32[]{:S(2)}) copy-start(s32[32,32]{1,0:T(8,128)} %tiles_ref.3) | copy-start | bytes 12292
  2.4 32.5 %copy-start.3 = (s32[32]{0:T(128)S(1)}, s32[32]{0:T(128)}, u32[]{:S(2)}) copy-start(s32[32]{0:T(128)} %count_ref.3) | copy-start | bytes 388
  2.4 32.4 %all-to-all-start = ((bf16[32,8,128]{2,1,0:T(8,128)(2,1)}), bf16[32,8,128]{2,1,0:T(8,128)(2,1)S(1)}, u32[]{:S(2)}, u32[]{:S(2)}) async-start(bf16[32,8,128]{2,1,0:T(8,128)(2,1)} %bitcast.7), calls=%async_computation | async-start | bytes 131072 | tf_op jit(solution)/shard_map/all_to_all | solution.py:217
  19.2 26.6 %collective-permute-start = (bf16[2,32,1024]{2,1,0:T(8,128)(2,1)S(1)}, bf16[2,32,1024]{2,1,0:T(8,128)(2,1)S(1)}, u32[]{:S(2)}, u32[]{:S(2)}) collective-permute-start(bf16[2,32,1024]{2,1,0:T(8,128)(2,1)S(1)} %copy-done.4), channel_id=1, source_target_pairs={{0,8},{1,9},{2,10},{3,11},{4,12},{5,13},{6,14},{7,15},{8,0},{9,1},... | collective-permute-start | bytes 393224 | tf_op jit(solution)/shard_map/ppermute | solution.py:198
  26.6 19.1 %collective-permute-start.1 = (bf16[2,32,1024]{2,1,0:T(8,128)(2,1)S(1)}, bf16[2,32,1024]{2,1,0:T(8,128)(2,1)S(1)}, u32[]{:S(2)}, u32[]{:S(2)}) collective-permute-start(bf16[2,32,1024]{2,1,0:T(8,128)(2,1)S(1)} %copy-done.4), channel_id=1, source_target_pairs={{0,24},{1,25},{2,26},{3,27},{4,28},{5,29},{6,30},{7,31},{8,16},{9,... | collective-permute-start | bytes 393224 | tf_op jit(solution)/shard_map/ppermute | solution.py:198
  36.6 9.2 %copy-start = (s32[32,32]{1,0:T(8,128)S(1)}, s32[32,32]{1,0:T(8,128)}, u32[]{:S(2)}) copy-start(s32[32,32]{1,0:T(8,128)} %refs_6_.1) | copy-start | bytes 12292
  36.6 24.4 %all-to-all-start.1 = ((bf16[32,8,128]{2,1,0:T(8,128)(2,1)}), bf16[32,8,128]{2,1,0:T(8,128)(2,1)S(1)}, u32[]{:S(2)}, u32[]{:S(2)}) async-start(bf16[32,8,128]{2,1,0:T(8,128)(2,1)} %route.1), calls=%async_computation.1 | async-start | bytes 131072 | tf_op jit(solution)/shard_map/all_to_all | solution.py:243
  45.8 0.7 copy-start.2
  46.6 24.6 %collective-permute-start.3 = (bf16[2,32,1024]{2,1,0:T(8,128)(2,1)S(1)}, bf16[2,32,1024]{2,1,0:T(8,128)(2,1)S(1)}, u32[]{:S(2)}, u32[]{:S(2)}) collective-permute-start(bf16[2,32,1024]{2,1,0:T(8,128)(2,1)S(1)} %get-tuple-element.12), channel_id=1, source_target_pairs={{0,24},{1,25},{2,26},{3,27},{4,28},{5,29},{6,30},{7,31},{8,16},{9,... | collective-permute-start | bytes 393224 | tf_op jit(solution)/shard_map/ppermute | solution.py:198
  54.3 24.0 %collective-permute-start.5 = (bf16[3,2,32,1024]{3,2,1,0:T(8,128)(2,1)S(1)}, bf16[3,2,32,1024]{3,2,1,0:T(8,128)(2,1)S(1)}, u32[]{:S(2)}, u32[]{:S(2)}) collective-permute-start(bf16[3,2,32,1024]{3,2,1,0:T(8,128)(2,1)S(1)} %get-tuple-element.11.rest_0_), channel_id=1, source_target_pairs={{0,1},{1,0},{2,3},{3,2},{4,5},{5,4},{6,7},{7,6},{8,9},{9,8},{10,11... | collective-permute-start | bytes 1179656 | tf_op jit(solution)/shard_map/ppermute | solution.py:198
  56.3 22.1 %collective-permute-start.2 = (bf16[3,2,32,1024]{3,2,1,0:T(8,128)(2,1)S(1)}, bf16[3,2,32,1024]{3,2,1,0:T(8,128)(2,1)S(1)}, u32[]{:S(2)}, u32[]{:S(2)}) collective-permute-start(bf16[3,2,32,1024]{3,2,1,0:T(8,128)(2,1)S(1)} %get-tuple-element.11.rest_0_), channel_id=1, source_target_pairs={{0,2},{1,3},{2,0},{3,1},{4,6},{5,7},{6,4},{7,5},{8,10},{9,11},{10,... | collective-permute-start | bytes 1179656 | tf_op jit(solution)/shard_map/ppermute | solution.py:198
  61.9 21.8 %all-to-all-start.2 = ((bf16[32,4,8,128]{3,2,1,0:T(8,128)(2,1)}), bf16[32,4,8,128]{3,2,1,0:T(8,128)(2,1)S(1)}, u32[]{:S(2)}, u32[]{:S(2)}) async-start(bf16[32,4,8,128]{3,2,1,0:T(8,128)(2,1)} %accumulate.1.refs_1_), calls=%async_computation.2 | async-start | bytes 524288 | tf_op jit(solution)/shard_map/all_to_all | solution.py:274
  71.3 7.1 %collective-permute-start.4 = (bf16[2,32,1024]{2,1,0:T(8,128)(2,1)S(1)}, bf16[2,32,1024]{2,1,0:T(8,128)(2,1)S(1)}, u32[]{:S(2)}, u32[]{:S(2)}) collective-permute-start(bf16[2,32,1024]{2,1,0:T(8,128)(2,1)S(1)} %settle.1.far_ref), channel_id=1, source_target_pairs={{0,2},{1,3},{2,0},{3,1},{4,6},{5,7},{6,4},{7,5},{8,10},{9,11},{10,... | collective-permute-start | bytes 393224 | tf_op jit(solution)/shard_map/ppermute | solution.py:198
  78.4 4.0 %collective-permute-start.6 = (bf16[5,2,32,1024]{3,2,1,0:T(8,128)(2,1)S(1)}, bf16[5,2,32,1024]{3,2,1,0:T(8,128)(2,1)S(1)}, u32[]{:S(2)}, u32[]{:S(2)}) collective-permute-start(bf16[5,2,32,1024]{3,2,1,0:T(8,128)(2,1)S(1)} %collect_rest.1.rest_1_), channel_id=1, source_target_pairs={{0,1},{1,0},{2,3},{3,2},{4,5},{5,4},{6,7},{7,6},{8,9},{9,8},{10,11... | collective-permute-start | bytes 1966088 | tf_op jit(solution)/shard_map/ppermute | solution.py:198
  84.4 8.1 %collective-permute-start.7 = (bf16[64,1024]{1,0:T(8,128)(2,1)S(1)}, bf16[64,1024]{1,0:T(8,128)(2,1)S(1)}, u32[]{:S(2)}, u32[]{:S(2)}) collective-permute-start(bf16[64,1024]{1,0:T(8,128)(2,1)S(1)} %get-tuple-element.14), channel_id=1, source_target_pairs={{0,6},{1,7},{2,4},{3,5},{4,2},{5,3},{6,0},{7,1},{8,14},{9,15},{10,... | collective-permute-start | bytes 393224 | tf_op jit(solution)/shard_map/ppermute | solution.py:198

commit v8 on v7

--- a/solution.py
+++ b/solution.py
@@ -24,26 +24,36 @@
     return lax.broadcasted_iota(jnp.int32, shape, len(shape) - 1) // width
 
 
-def order_columns(tiles_ref, count_ref, rows_ref, out_ref, total):
+def invert(tiles_ref, count_ref, where_ref):
     own = lax.axis_index("owner")
-    width, columns = rows_ref.shape
-    list_len = tiles_ref.shape[1]
+    for owner in range(where_ref.shape[0]):
+        where_ref[owner] = -1
+    count = count_ref[own]
+    for place in range(tiles_ref.shape[1]):
+        owner = tiles_ref[own, place] // 2
+
+        @pl.when(place < count)
+        def _():
+            where_ref[owner] = place
+
+
+def order_columns(tiles_ref, count_ref, rows_ref, out_ref, where_ref):
+    width = rows_ref.shape[0]
     groups = LANE // width
-    total[...] = jnp.zeros_like(total)
-    count = count_ref[own]
+    invert(tiles_ref, count_ref, where_ref)
     group = lane_group((width, LANE), width)
-    for place in range(list_len):
-        if place % groups == 0:
-            chunk = rows_ref[:, place // groups * LANE : (place // groups + 1) * LANE].astype(jnp.float32)
-        owner = tiles_ref[own, place] // 2
-        spot = (owner // NC) % NX
-        target = owner // (NX * NC) * NC + owner % NC
-        turned = pltpu.roll(chunk, (spot - place % groups + groups) % groups * width, 1)
-        keep = (group == spot) & (place < count)
-        total[target] += jnp.where(keep, turned, 0.0)
-    for part in range(width // SUB):
-        for target in range(NZ * NC):
-            out_ref[part, target] = total[target, part * SUB : (part + 1) * SUB, :].astype(out_ref.dtype)
+    for z in range(NZ):
+        for core in range(NC):
+            merged = jnp.zeros((width, LANE), jnp.float32)
+            for spot in range(NX):
+                found = where_ref[owner_index(z, spot, core)]
+                place = jnp.maximum(found, 0)
+                start = pl.multiple_of(place // groups * LANE, LANE)
+                chunk = rows_ref[:, pl.ds(start, LANE)].astype(jnp.float32)
+                turned = pltpu.roll(chunk, (spot - place % groups + groups) % groups * width, 1)
+                merged = jnp.where((group == spot) & (found >= 0), turned, merged)
+            for part in range(width // SUB):
+                out_ref[part, z * NC + core] = merged[part * SUB : (part + 1) * SUB].astype(out_ref.dtype)
 
 
 def regroup(tiles, width):
@@ -60,20 +70,18 @@
     return results
 
 
-def route(tiles_ref, count_ref, rows_ref, *rest):
-    out_ref, held = rest[-2:]
-    own = lax.axis_index("owner")
-    list_len = tiles_ref.shape[1]
-    held[...] = jnp.zeros_like(held)
-    count = count_ref[own]
-    for place in range(list_len):
-        owner = tiles_ref[own, place] // 2
-        held[owner] += jnp.where(place < count, rows_ref[place].astype(jnp.float32), 0.0)
+def route(tiles_ref, count_ref, rows_ref, out_ref, where_ref):
+    invert(tiles_ref, count_ref, where_ref)
+
+    def held(owner):
+        found = where_ref[owner]
+        return jnp.where(found >= 0, rows_ref[jnp.maximum(found, 0)].astype(jnp.float32), 0.0)
+
     width = LANE // NX
     group = lane_group((SUB, LANE), width)
     for z in range(NZ):
         for core in range(NC):
-            tiles = [held[owner_index(z, x, core)] for x in range(NX)]
+            tiles = [held(owner_index(z, x, core)) for x in range(NX)]
             for x in range(NX):
                 wanted = [(tiles[x ^ (3 * a)], x ^ d) for a in range(2) for d in range(2)]
                 merged = None
@@ -210,7 +218,7 @@
         out_shape=jax.ShapeDtypeStruct((width // SUB, NZ * NC, SUB, LANE), bf16),
         in_specs=[SMEM, SMEM, VMEM],
         out_specs=VMEM,
-        scratch_shapes=[pltpu.VMEM((NZ * NC, width, LANE), f32)],
+        scratch_shapes=[pltpu.SMEM((owners,), jnp.int32)],
         name="order_columns",
     )(cd_tiles, cd_count, integrals[0])
     ordered = ordered.reshape(pieces, SUB, LANE)
@@ -220,7 +228,7 @@
         out_shape=jax.ShapeDtypeStruct((owners, SUB, LANE), bf16),
         in_specs=[SMEM, SMEM, VMEM],
         out_specs=VMEM,
-        scratch_shapes=[pltpu.VMEM((owners, SUB, LANE), f32)],
+        scratch_shapes=[pltpu.SMEM((owners,), jnp.int32)],
         compiler_params=SMALL,
         name="route",
     )(ab_tiles, ab_count, mine)

time: 93.9 us -> 93.7 us (level)
  no operation moved by 1% of the time
where the time goes in v8:
time: 93.7 us; the launch traced here: 93.1 us
  starting transfers between devices  71 us (76%)
  waiting for transfers between devices  14.7 us (16%)
  Pallas kernels  5.77 us (6%)
    ppermute x8, starting transfers between devices, moved(): return lax.ppermute(block, 'owner', pairs)  35.7 us
    all_to_all x1, starting transfers between devices, shards(): lax.all_to_all(ordered, 'blk', split_axis=0, concat_axis=0, tiled=True)  16.7 us
    ppermute x8, waiting for transfers between devices, moved(): return lax.ppermute(block, 'owner', pairs)  12 us
    all_to_all x1, starting transfers between devices, shards(): lax.all_to_all(spread, 'blk', split_axis=0, concat_axis=0, tiled=True)  9.38 us
    all_to_all x1, starting transfers between devices, shards(): lax.all_to_all(outgoing, 'owner', split_axis=0, concat_axis=0, tiled=True)  9.11 us
    pallas_call x1, Pallas kernels, shards(): pl.pallas_call(order_columns, out_shape=jax.ShapeDtypeStruct((width // SU...  2.19 us
  transfers between devices with their start and end apart: 11, of which 5 were waited for; matrix products, arithmetic and copies ran while one was open for 0% of the time, Pallas kernels for 3%

profile of v8, /device:TPU:8, one launch (start us, length us, event | category | flops | bytes accessed | tf_op | source)
XLA Modules:
  0.0 93.1 jit_solution(5972844753454612861)
XLA Ops:
  0.0 0.0 copy-start.4
  0.0 2.2 %order_columns.1 = bf16[4,8,8,128]{3,2,1,0:T(8,128)(2,1)} custom-call(s32[32,32]{1,0:T(8,128)} %refs_6_.1, s32[32]{0:T(128)} %count_ref.2, bf16[32,1024]{1,0:T(8,128)(2,1)} %bitcast.8), custom_call_target="tpu_custom_call" | custom-call | tf_op jit(solution)/shard_map/order_columns/pallas_call | solution.py:216
  2.2 0.0 copy-start.1
  2.2 0.0 copy-start.3
  2.2 16.7 %all-to-all-start = ((bf16[32,8,128]{2,1,0:T(8,128)(2,1)}), bf16[32,8,128]{2,1,0:T(8,128)(2,1)S(1)}, u32[]{:S(2)}, u32[]{:S(2)}) async-start(bf16[32,8,128]{2,1,0:T(8,128)(2,1)} %bitcast.7), calls=%async_computation | async-start | bytes 131072 | tf_op jit(solution)/shard_map/all_to_all | solution.py:225
  18.9 0.0 copy-done.4
  19.0 7.4 %collective-permute-start = (bf16[2,32,1024]{2,1,0:T(8,128)(2,1)S(1)}, bf16[2,32,1024]{2,1,0:T(8,128)(2,1)S(1)}, u32[]{:S(2)}, u32[]{:S(2)}) collective-permute-start(bf16[2,32,1024]{2,1,0:T(8,128)(2,1)S(1)} %copy-done.4), channel_id=1, source_target_pairs={{0,8},{1,9},{2,10},{3,11},{4,12},{5,13},{6,14},{7,15},{8,0},{9,1},... | collective-permute-start | bytes 393224 | tf_op jit(solution)/shard_map/ppermute | solution.py:206
  26.4 8.2 %collective-permute-start.1 = (bf16[2,32,1024]{2,1,0:T(8,128)(2,1)S(1)}, bf16[2,32,1024]{2,1,0:T(8,128)(2,1)S(1)}, u32[]{:S(2)}, u32[]{:S(2)}) collective-permute-start(bf16[2,32,1024]{2,1,0:T(8,128)(2,1)S(1)} %copy-done.4), channel_id=1, source_target_pairs={{0,24},{1,25},{2,26},{3,27},{4,28},{5,29},{6,30},{7,31},{8,16},{9,... | collective-permute-start | bytes 393224 | tf_op jit(solution)/shard_map/ppermute | solution.py:206
  34.6 0.0 all-to-all-done.refs_3_.rows_ref
  34.6 0.0 copy-done.1
  34.7 0.0 copy-done.3
  34.7 1.8 %route.1 = bf16[32,8,128]{2,1,0:T(8,128)(2,1)} custom-call(s32[32,32]{1,0:T(8,128)S(1)} %copy-done.1, s32[32]{0:T(128)S(1)} %copy-done.3, bf16[32,8,128]{2,1,0:T(8,128)(2,1)S(1)} %all-to-all-done.refs_3_.rows_ref), custom_call_target="tpu_custom_call" | custom-call | tf_op jit(solution)/shard_map/route/pallas_call | solution.py:226
  36.4 0.0 copy-start
  36.4 9.1 %all-to-all-start.1 = ((bf16[32,8,128]{2,1,0:T(8,128)(2,1)}), bf16[32,8,128]{2,1,0:T(8,128)(2,1)S(1)}, u32[]{:S(2)}, u32[]{:S(2)}) async-start(bf16[32,8,128]{2,1,0:T(8,128)(2,1)} %route.1), calls=%async_computation.1 | async-start | bytes 131072 | tf_op jit(solution)/shard_map/all_to_all | solution.py:251
  45.6 0.0 collective-permute-done.refs_1_
  45.6 0.0 collective-permute-done.1.refs_2_
  45.6 0.0 copy-start.2
  45.6 0.0 copy-done
  45.6 0.6 copy-done.2
  46.2 0.2 collect_near.1
  46.4 7.7 %collective-permute-start.3 = (bf16[2,32,1024]{2,1,0:T(8,128)(2,1)S(1)}, bf16[2,32,1024]{2,1,0:T(8,128)(2,1)S(1)}, u32[]{:S(2)}, u32[]{:S(2)}) collective-permute-start(bf16[2,32,1024]{2,1,0:T(8,128)(2,1)S(1)} %get-tuple-element.12), channel_id=1, source_target_pairs={{0,24},{1,25},{2,26},{3,27},{4,28},{5,29},{6,30},{7,31},{8,16},{9,... | collective-permute-start | bytes 393224 | tf_op jit(solution)/shard_map/ppermute | solution.py:206
  54.1 1.9 %collective-permute-start.5 = (bf16[3,2,32,1024]{3,2,1,0:T(8,128)(2,1)S(1)}, bf16[3,2,32,1024]{3,2,1,0:T(8,128)(2,1)S(1)}, u32[]{:S(2)}, u32[]{:S(2)}) collective-permute-start(bf16[3,2,32,1024]{3,2,1,0:T(8,128)(2,1)S(1)} %get-tuple-element.11.rest_0_), channel_id=1, source_target_pairs={{0,1},{1,0},{2,3},{3,2},{4,5},{5,4},{6,7},{7,6},{8,9},{9,8},{10,11... | collective-permute-start | bytes 1179656 | tf_op jit(solution)/shard_map/ppermute | solution.py:206
  56.0 3.4 %collective-permute-start.2 = (bf16[3,2,32,1024]{3,2,1,0:T(8,128)(2,1)S(1)}, bf16[3,2,32,1024]{3,2,1,0:T(8,128)(2,1)S(1)}, u32[]{:S(2)}, u32[]{:S(2)}) collective-permute-start(bf16[3,2,32,1024]{3,2,1,0:T(8,128)(2,1)S(1)} %get-tuple-element.11.rest_0_), channel_id=1, source_target_pairs={{0,2},{1,3},{2,0},{3,1},{4,6},{5,7},{6,4},{7,5},{8,10},{9,11},{10,... | collective-permute-start | bytes 1179656 | tf_op jit(solution)/shard_map/ppermute | solution.py:206
  59.4 1.4 %all-to-all-done.1.rows_ref = bf16[32,8,128]{2,1,0:T(8,128)(2,1)S(1)} async-done(((bf16[32,8,128]{2,1,0:T(8,128)(2,1)}), bf16[32,8,128]{2,1,0:T(8,128)(2,1)S(1)}, u32[]{:S(2)}, u32[]{:S(2)}) %all-to-all-start.1) | async-done | bytes 65568 | tf_op jit(solution)/shard_map/all_to_all | solution.py:251
  60.9 0.8 accumulate.1.refs_1_
  61.7 9.4 %all-to-all-start.2 = ((bf16[32,4,8,128]{3,2,1,0:T(8,128)(2,1)}), bf16[32,4,8,128]{3,2,1,0:T(8,128)(2,1)S(1)}, u32[]{:S(2)}, u32[]{:S(2)}) async-start(bf16[32,4,8,128]{3,2,1,0:T(8,128)(2,1)} %accumulate.1.refs_1_), calls=%async_computation.2 | async-start | bytes 524288 | tf_op jit(solution)/shard_map/all_to_all | solution.py:282
  71.0 0.0 collective-permute-done.3.refs_0_
  71.1 2.1 %collective-permute-start.4 = (bf16[2,32,1024]{2,1,0:T(8,128)(2,1)S(1)}, bf16[2,32,1024]{2,1,0:T(8,128)(2,1)S(1)}, u32[]{:S(2)}, u32[]{:S(2)}) collective-permute-start(bf16[2,32,1024]{2,1,0:T(8,128)(2,1)S(1)} %settle.1.far_ref), channel_id=1, source_target_pairs={{0,2},{1,3},{2,0},{3,1},{4,6},{5,7},{6,4},{7,5},{8,10},{9,11},{10,... | collective-permute-start | bytes 393224 | tf_op jit(solution)/shard_map/ppermute | solution.py:206
  73.1 5.0 %collective-permute-done.4.far_pair_ref = bf16[2,32,1024]{2,1,0:T(8,128)(2,1)S(1)} collective-permute-done((bf16[2,32,1024]{2,1,0:T(8,128)(2,1)S(1)}, bf16[2,32,1024]{2,1,0:T(8,128)(2,1)S(1)}, u32[]{:S(2)}, u32[]{:S(2)}) %collective-permute-start.4) | collective-permute-done | bytes 131104 | tf_op jit(solution)/shard_map/ppermute | solution.py:206
  78.1 0.0 collective-permute-done.5._.rest_2_
  78.1 0.0 collective-permute-done.2.near_pair_ref
  78.2 1.9 %collective-permute-start.6 = (bf16[5,2,32,1024]{3,2,1,0:T(8,128)(2,1)S(1)}, bf16[5,2,32,1024]{3,2,1,0:T(8,128)(2,1)S(1)}, u32[]{:S(2)}, u32[]{:S(2)}) collective-permute-start(bf16[5,2,32,1024]{3,2,1,0:T(8,128)(2,1)S(1)} %collect_rest.1.rest_1_), channel_id=1, source_target_pairs={{0,1},{1,0},{2,3},{3,2},{4,5},{5,4},{6,7},{7,6},{8,9},{9,8},{10,11... | collective-permute-start | bytes 1966088 | tf_op jit(solution)/shard_map/ppermute | solution.py:206
  80.1 2.1 %collective-permute-done.6.rest_3_ = bf16[5,2,32,1024]{3,2,1,0:T(8,128)(2,1)S(1)} collective-permute-done((bf16[5,2,32,1024]{3,2,1,0:T(8,128)(2,1)S(1)}, bf16[5,2,32,1024]{3,2,1,0:T(8,128)(2,1)S(1)}, u32[]{:S(2)}, u32[]{:S(2)}) %collective-permute-start.6) | collective-permute-done | bytes 655392 | tf_op jit(solution)/shard_map/ppermute | solution.py:206
  82.2 1.3 %all-to-all-done.2.weights_ref = bf16[32,4,8,128]{3,2,1,0:T(8,128)(2,1)S(1)} async-done(((bf16[32,4,8,128]{3,2,1,0:T(8,128)(2,1)}), bf16[32,4,8,128]{3,2,1,0:T(8,128)(2,1)S(1)}, u32[]{:S(2)}, u32[]{:S(2)}) %all-to-all-start.2) | async-done | bytes 262176 | tf_op jit(solution)/shard_map/all_to_all | solution.py:282
  83.5 0.8 multiply.1
  84.3 3.1 %collective-permute-start.7 = (bf16[64,1024]{1,0:T(8,128)(2,1)S(1)}, bf16[64,1024]{1,0:T(8,128)(2,1)S(1)}, u32[]{:S(2)}, u32[]{:S(2)}) collective-permute-start(bf16[64,1024]{1,0:T(8,128)(2,1)S(1)} %get-tuple-element.14), channel_id=1, source_target_pairs={{0,6},{1,7},{2,4},{3,5},{4,2},{5,3},{6,0},{7,1},{8,14},{9,15},{10,... | collective-permute-start | bytes 393224 | tf_op jit(solution)/shard_map/ppermute | solution.py:206
  87.4 4.9 %collective-permute-done.7 = bf16[64,1024]{1,0:T(8,128)(2,1)S(1)} collective-permute-done((bf16[64,1024]{1,0:T(8,128)(2,1)S(1)}, bf16[64,1024]{1,0:T(8,128)(2,1)S(1)}, u32[]{:S(2)}, u32[]{:S(2)}) %collective-permute-start.7) | collective-permute-done | bytes 131104 | tf_op jit(solution)/shard_map/ppermute | solution.py:206
  92.3 0.7 convert_add_fusion
  (2 shorter events, 0.0 us)
Async XLA Ops:
  0.0 18.9 %copy-start.4 = (bf16[2,32,1024]{2,1,0:T(8,128)(2,1)S(1)}, bf16[2,32,1024]{2,1,0:T(8,128)(2,1)}, u32[]{:S(2)}) copy-start(bf16[2,32,1024]{2,1,0:T(8,128)(2,1)} %refs_0_.1) | copy-start | bytes 393220
  2.2 32.4 %copy-start.1 = (s32[32,32]{1,0:T(8,128)S(1)}, s32[32,32]{1,0:T(8,128)}, u32[]{:S(2)}) copy-start(s32[32,32]{1,0:T(8,128)} %tiles_ref.3) | copy-start | bytes 12292
  2.2 32.5 %copy-start.3 = (s32[32]{0:T(128)S(1)}, s32[32]{0:T(128)}, u32[]{:S(2)}) copy-start(s32[32]{0:T(128)} %count_ref.3) | copy-start | bytes 388
  2.2 32.4 %all-to-all-start = ((bf16[32,8,128]{2,1,0:T(8,128)(2,1)}), bf16[32,8,128]{2,1,0:T(8,128)(2,1)S(1)}, u32[]{:S(2)}, u32[]{:S(2)}) async-start(bf16[32,8,128]{2,1,0:T(8,128)(2,1)} %bitcast.7), calls=%async_computation | async-start | bytes 131072 | tf_op jit(solution)/shard_map/all_to_all | solution.py:225
  19.0 26.6 %collective-permute-start = (bf16[2,32,1024]{2,1,0:T(8,128)(2,1)S(1)}, bf16[2,32,1024]{2,1,0:T(8,128)(2,1)S(1)}, u32[]{:S(2)}, u32[]{:S(2)}) collective-permute-start(bf16[2,32,1024]{2,1,0:T(8,128)(2,1)S(1)} %copy-done.4), channel_id=1, source_target_pairs={{0,8},{1,9},{2,10},{3,11},{4,12},{5,13},{6,14},{7,15},{8,0},{9,1},... | collective-permute-start | bytes 393224 | tf_op jit(solution)/shard_map/ppermute | solution.py:206
  26.4 19.2 %collective-permute-start.1 = (bf16[2,32,1024]{2,1,0:T(8,128)(2,1)S(1)}, bf16[2,32,1024]{2,1,0:T(8,128)(2,1)S(1)}, u32[]{:S(2)}, u32[]{:S(2)}) collective-permute-start(bf16[2,32,1024]{2,1,0:T(8,128)(2,1)S(1)} %copy-done.4), channel_id=1, source_target_pairs={{0,24},{1,25},{2,26},{3,27},{4,28},{5,29},{6,30},{7,31},{8,16},{9,... | collective-permute-start | bytes 393224 | tf_op jit(solution)/shard_map/ppermute | solution.py:206
  36.4 9.2 %copy-start = (s32[32,32]{1,0:T(8,128)S(1)}, s32[32,32]{1,0:T(8,128)}, u32[]{:S(2)}) copy-start(s32[32,32]{1,0:T(8,128)} %refs_6_.1) | copy-start | bytes 12292
  36.4 24.4 %all-to-all-start.1 = ((bf16[32,8,128]{2,1,0:T(8,128)(2,1)}), bf16[32,8,128]{2,1,0:T(8,128)(2,1)S(1)}, u32[]{:S(2)}, u32[]{:S(2)}) async-start(bf16[32,8,128]{2,1,0:T(8,128)(2,1)} %route.1), calls=%async_computation.1 | async-start | bytes 131072 | tf_op jit(solution)/shard_map/all_to_all | solution.py:251
  45.6 0.7 copy-start.2
  46.4 24.6 %collective-permute-start.3 = (bf16[2,32,1024]{2,1,0:T(8,128)(2,1)S(1)}, bf16[2,32,1024]{2,1,0:T(8,128)(2,1)S(1)}, u32[]{:S(2)}, u32[]{:S(2)}) collective-permute-start(bf16[2,32,1024]{2,1,0:T(8,128)(2,1)S(1)} %get-tuple-element.12), channel_id=1, source_target_pairs={{0,24},{1,25},{2,26},{3,27},{4,28},{5,29},{6,30},{7,31},{8,16},{9,... | collective-permute-start | bytes 393224 | tf_op jit(solution)/shard_map/ppermute | solution.py:206
  54.1 24.0 %collective-permute-start.5 = (bf16[3,2,32,1024]{3,2,1,0:T(8,128)(2,1)S(1)}, bf16[3,2,32,1024]{3,2,1,0:T(8,128)(2,1)S(1)}, u32[]{:S(2)}, u32[]{:S(2)}) collective-permute-start(bf16[3,2,32,1024]{3,2,1,0:T(8,128)(2,1)S(1)} %get-tuple-element.11.rest_0_), channel_id=1, source_target_pairs={{0,1},{1,0},{2,3},{3,2},{4,5},{5,4},{6,7},{7,6},{8,9},{9,8},{10,11... | collective-permute-start | bytes 1179656 | tf_op jit(solution)/shard_map/ppermute | solution.py:206
  56.0 22.1 %collective-permute-start.2 = (bf16[3,2,32,1024]{3,2,1,0:T(8,128)(2,1)S(1)}, bf16[3,2,32,1024]{3,2,1,0:T(8,128)(2,1)S(1)}, u32[]{:S(2)}, u32[]{:S(2)}) collective-permute-start(bf16[3,2,32,1024]{3,2,1,0:T(8,128)(2,1)S(1)} %get-tuple-element.11.rest_0_), channel_id=1, source_target_pairs={{0,2},{1,3},{2,0},{3,1},{4,6},{5,7},{6,4},{7,5},{8,10},{9,11},{10,... | collective-permute-start | bytes 1179656 | tf_op jit(solution)/shard_map/ppermute | solution.py:206
  61.7 21.8 %all-to-all-start.2 = ((bf16[32,4,8,128]{3,2,1,0:T(8,128)(2,1)}), bf16[32,4,8,128]{3,2,1,0:T(8,128)(2,1)S(1)}, u32[]{:S(2)}, u32[]{:S(2)}) async-start(bf16[32,4,8,128]{3,2,1,0:T(8,128)(2,1)} %accumulate.1.refs_1_), calls=%async_computation.2 | async-start | bytes 524288 | tf_op jit(solution)/shard_map/all_to_all | solution.py:282
  71.1 7.1 %collective-permute-start.4 = (bf16[2,32,1024]{2,1,0:T(8,128)(2,1)S(1)}, bf16[2,32,1024]{2,1,0:T(8,128)(2,1)S(1)}, u32[]{:S(2)}, u32[]{:S(2)}) collective-permute-start(bf16[2,32,1024]{2,1,0:T(8,128)(2,1)S(1)} %settle.1.far_ref), channel_id=1, source_target_pairs={{0,2},{1,3},{2,0},{3,1},{4,6},{5,7},{6,4},{7,5},{8,10},{9,11},{10,... | collective-permute-start | bytes 393224 | tf_op jit(solution)/shard_map/ppermute | solution.py:206
  78.2 4.0 %collective-permute-start.6 = (bf16[5,2,32,1024]{3,2,1,0:T(8,128)(2,1)S(1)}, bf16[5,2,32,1024]{3,2,1,0:T(8,128)(2,1)S(1)}, u32[]{:S(2)}, u32[]{:S(2)}) collective-permute-start(bf16[5,2,32,1024]{3,2,1,0:T(8,128)(2,1)S(1)} %collect_rest.1.rest_1_), channel_id=1, source_target_pairs={{0,1},{1,0},{2,3},{3,2},{4,5},{5,4},{6,7},{7,6},{8,9},{9,8},{10,11... | collective-permute-start | bytes 1966088 | tf_op jit(solution)/shard_map/ppermute | solution.py:206
  84.3 8.1 %collective-permute-start.7 = (bf16[64,1024]{1,0:T(8,128)(2,1)S(1)}, bf16[64,1024]{1,0:T(8,128)(2,1)S(1)}, u32[]{:S(2)}, u32[]{:S(2)}) collective-permute-start(bf16[64,1024]{1,0:T(8,128)(2,1)S(1)} %get-tuple-element.14), channel_id=1, source_target_pairs={{0,6},{1,7},{2,4},{3,5},{4,2},{5,3},{6,0},{7,1},{8,14},{9,15},{10,... | collective-permute-start | bytes 393224 | tf_op jit(solution)/shard_map/ppermute | solution.py:206

commit v9 on v8

--- a/solution.py
+++ b/solution.py
@@ -154,15 +154,14 @@
     pass
 
 
-def collect_rest(near_pair_ref, far_ref, far_pair_ref, _, out_ref):
+def collect_rest(near_pair_ref, far_ref, _, out_ref):
     out_ref[: NZ - 1] = near_pair_ref[...]
     out_ref[NZ - 1] = far_ref[...]
-    out_ref[NZ] = far_pair_ref[...]
 
 
 def multiply(weights_ref, *rest):
-    mine_ref, theirs_ref, left = rest[4:]
-    amps = [((near, more, NZ - 1), (more, more, NZ)) for near, more in (rest[:2], rest[2:4])]
+    mine_ref, theirs_ref, left = rest[6:]
+    amps = [((near, more.at[NZ - 1]), (more, last)) for near, more, last in (rest[:3], rest[3:6])]
     own = lax.axis_index("owner")
     z, core = own // (NX * NC), own % NC
     width, occ = rest[0].shape[2:]
@@ -187,8 +186,9 @@
     for col in range(0, occ, wide):
         total = None
         for at, (par, d, side) in enumerate(blocks):
-            near, far, last = amps[side][d]
-            right = [ref[place, par, :, col : col + wide] for ref, place in ((near, 0), (near, 1), (near, 2), (far, last))]
+            near, far = amps[side][d]
+            right = [near[place, par, :, col : col + wide] for place in range(NZ - 1)]
+            right.append(far[par, :, col : col + wide])
             right = jnp.concatenate(right, axis=0)
             term = jnp.dot(left[:, at * LANE : (at + 1) * LANE], right, preferred_element_type=jnp.float32)
             total = term if total is None else total + term
@@ -270,21 +270,21 @@
     far_pair = moved(far, dx=1)
     rest = pl.pallas_call(
         collect_rest,
-        out_shape=jax.ShapeDtypeStruct((NZ + 1, tile_dev, width, occ), bf16),
-        in_specs=[VMEM] * 3 + [ANY],
+        out_shape=jax.ShapeDtypeStruct((NZ, tile_dev, width, occ), bf16),
+        in_specs=[VMEM] * 2 + [ANY],
         out_specs=VMEM,
         cost_estimate=pl.CostEstimate(flops=2000000000, bytes_accessed=amplitudes.size * 20, transcendentals=0),
         compiler_params=SMALL,
         name="collect_rest",
-    )(near_pair, far, far_pair, near_other)
-    sides = [near, rest, near_other, moved(rest, dcore=1)]
+    )(near_pair, far, near_other)
+    sides = [near, rest, far_pair, near_other, moved(rest, dcore=1), moved(far_pair, dcore=1)]
 
     weights = lax.all_to_all(spread, "blk", split_axis=0, concat_axis=0, tiled=True)
     shape = (tile_dev * width, occ)
     mine, theirs = pl.pallas_call(
         multiply,
         out_shape=(jax.ShapeDtypeStruct(shape, f32), jax.ShapeDtypeStruct(shape, bf16)),
-        in_specs=[VMEM] * 5,
+        in_specs=[VMEM] * 7,
         out_specs=(VMEM, VMEM),
         scratch_shapes=[pltpu.VMEM((2 * tile_dev * width, 2 * NZ * NC * tile_dev * width), bf16)],
         compiler_params=pltpu.CompilerParams(vmem_limit_bytes=16 * 1024 * 1024),

time: 93.7 us -> 95.9 us (1.023)
  the two profiles are of different devices: /device:TPU:8 before, /device:TPU:6 now
where the time goes in v9:
time: 95.9 us; the launch traced here: 94.3 us
  starting transfers between devices  73.4 us (77%)
  waiting for transfers between devices  13.6 us (14%)
  Pallas kernels  5.76 us (6%)
    ppermute x9, starting transfers between devices, moved(): return lax.ppermute(block, 'owner', pairs)  41.3 us
    ppermute x9, waiting for transfers between devices, moved(): return lax.ppermute(block, 'owner', pairs)  13.6 us
    all_to_all x1, starting transfers between devices, shards(): lax.all_to_all(ordered, 'blk', split_axis=0, concat_axis=0, tiled=True)  13 us
    all_to_all x1, starting transfers between devices, shards(): lax.all_to_all(outgoing, 'owner', split_axis=0, concat_axis=0, tiled=True)  10.4 us
    all_to_all x1, starting transfers between devices, shards(): lax.all_to_all(spread, 'blk', split_axis=0, concat_axis=0, tiled=True)  8.6 us
    pallas_call x1, Pallas kernels, shards(): pl.pallas_call(order_columns, out_shape=jax.ShapeDtypeStruct((width // SU...  2.19 us
  transfers between devices with their start and end apart: 12, of which 4 were waited for; matrix products, arithmetic and copies ran while one was open for 0% of the time, Pallas kernels for 3%

profile of v9, /device:TPU:6, one launch (start us, length us, event | category | flops | bytes accessed | tf_op | source)
XLA Modules:
  0.0 94.3 jit_solution(17666212694736492397)
XLA Ops:
  0.0 0.0 copy-start.4
  0.0 2.2 %order_columns.1 = bf16[4,8,8,128]{3,2,1,0:T(8,128)(2,1)} custom-call(s32[32,32]{1,0:T(8,128)} %refs_6_.1, s32[32]{0:T(128)} %count_ref.2, bf16[32,1024]{1,0:T(8,128)(2,1)} %bitcast.8), custom_call_target="tpu_custom_call" | custom-call | tf_op jit(solution)/shard_map/order_columns/pallas_call | solution.py:216
  2.2 0.0 copy-start.1
  2.2 0.0 copy-start.3
  2.2 13.0 %all-to-all-start = ((bf16[32,8,128]{2,1,0:T(8,128)(2,1)}), bf16[32,8,128]{2,1,0:T(8,128)(2,1)S(1)}, u32[]{:S(2)}, u32[]{:S(2)}) async-start(bf16[32,8,128]{2,1,0:T(8,128)(2,1)} %bitcast.7), calls=%async_computation | async-start | bytes 131072 | tf_op jit(solution)/shard_map/all_to_all | solution.py:225
  15.3 0.0 copy-done.4
  15.3 10.9 %collective-permute-start = (bf16[2,32,1024]{2,1,0:T(8,128)(2,1)S(1)}, bf16[2,32,1024]{2,1,0:T(8,128)(2,1)S(1)}, u32[]{:S(2)}, u32[]{:S(2)}) collective-permute-start(bf16[2,32,1024]{2,1,0:T(8,128)(2,1)S(1)} %copy-done.4), channel_id=1, source_target_pairs={{0,8},{1,9},{2,10},{3,11},{4,12},{5,13},{6,14},{7,15},{8,0},{9,1},... | collective-permute-start | bytes 393224 | tf_op jit(solution)/shard_map/ppermute | solution.py:206
  26.2 8.2 %collective-permute-start.1 = (bf16[2,32,1024]{2,1,0:T(8,128)(2,1)S(1)}, bf16[2,32,1024]{2,1,0:T(8,128)(2,1)S(1)}, u32[]{:S(2)}, u32[]{:S(2)}) collective-permute-start(bf16[2,32,1024]{2,1,0:T(8,128)(2,1)S(1)} %copy-done.4), channel_id=1, source_target_pairs={{0,24},{1,25},{2,26},{3,27},{4,28},{5,29},{6,30},{7,31},{8,16},{9,... | collective-permute-start | bytes 393224 | tf_op jit(solution)/shard_map/ppermute | solution.py:206
  34.4 0.0 all-to-all-done.refs_3_.rows_ref
  34.4 0.0 copy-done.1
  34.4 0.0 copy-done.3
  34.4 1.8 %route.1 = bf16[32,8,128]{2,1,0:T(8,128)(2,1)} custom-call(s32[32,32]{1,0:T(8,128)S(1)} %copy-done.1, s32[32]{0:T(128)S(1)} %copy-done.3, bf16[32,8,128]{2,1,0:T(8,128)(2,1)S(1)} %all-to-all-done.refs_3_.rows_ref), custom_call_target="tpu_custom_call" | custom-call | tf_op jit(solution)/shard_map/route/pallas_call | solution.py:226
  36.2 0.0 copy-start
  36.2 10.4 %all-to-all-start.1 = ((bf16[32,8,128]{2,1,0:T(8,128)(2,1)}), bf16[32,8,128]{2,1,0:T(8,128)(2,1)S(1)}, u32[]{:S(2)}, u32[]{:S(2)}) async-start(bf16[32,8,128]{2,1,0:T(8,128)(2,1)} %route.1), calls=%async_computation.1 | async-start | bytes 131072 | tf_op jit(solution)/shard_map/all_to_all | solution.py:251
  46.6 0.0 collective-permute-done.refs_1_
  46.6 0.0 collective-permute-done.1.refs_2_
  46.6 0.0 copy-start.2
  46.6 0.0 copy-done
  46.6 0.6 copy-done.2
  47.3 0.2 collect_near.1
  47.5 2.1 %collective-permute-start.4 = (bf16[3,2,32,1024]{3,2,1,0:T(8,128)(2,1)S(1)}, bf16[3,2,32,1024]{3,2,1,0:T(8,128)(2,1)S(1)}, u32[]{:S(2)}, u32[]{:S(2)}) collective-permute-start(bf16[3,2,32,1024]{3,2,1,0:T(8,128)(2,1)S(1)} %get-tuple-element.11.rest_0_), channel_id=1, source_target_pairs={{0,1},{1,0},{2,3},{3,2},{4,5},{5,4},{6,7},{7,6},{8,9},{9,8},{10,11... | collective-permute-start | bytes 1179656 | tf_op jit(solution)/shard_map/ppermute | solution.py:206
  49.5 2.8 %collective-permute-start.2 = (bf16[3,2,32,1024]{3,2,1,0:T(8,128)(2,1)S(1)}, bf16[3,2,32,1024]{3,2,1,0:T(8,128)(2,1)S(1)}, u32[]{:S(2)}, u32[]{:S(2)}) collective-permute-start(bf16[3,2,32,1024]{3,2,1,0:T(8,128)(2,1)S(1)} %get-tuple-element.11.rest_0_), channel_id=1, source_target_pairs={{0,2},{1,3},{2,0},{3,1},{4,6},{5,7},{6,4},{7,5},{8,10},{9,11},{10,... | collective-permute-start | bytes 1179656 | tf_op jit(solution)/shard_map/ppermute | solution.py:206
  52.3 7.3 %collective-permute-start.3 = (bf16[2,32,1024]{2,1,0:T(8,128)(2,1)S(1)}, bf16[2,32,1024]{2,1,0:T(8,128)(2,1)S(1)}, u32[]{:S(2)}, u32[]{:S(2)}) collective-permute-start(bf16[2,32,1024]{2,1,0:T(8,128)(2,1)S(1)} %get-tuple-element.12), channel_id=1, source_target_pairs={{0,24},{1,25},{2,26},{3,27},{4,28},{5,29},{6,30},{7,31},{8,16},{9,... | collective-permute-start | bytes 393224 | tf_op jit(solution)/shard_map/ppermute | solution.py:206
  59.7 0.0 all-to-all-done.1.rows_ref
  59.7 0.8 accumulate.1.refs_1_
  60.5 8.6 %all-to-all-start.2 = ((bf16[32,4,8,128]{3,2,1,0:T(8,128)(2,1)}), bf16[32,4,8,128]{3,2,1,0:T(8,128)(2,1)S(1)}, u32[]{:S(2)}, u32[]{:S(2)}) async-start(bf16[32,4,8,128]{3,2,1,0:T(8,128)(2,1)} %accumulate.1.refs_1_), calls=%async_computation.2 | async-start | bytes 524288 | tf_op jit(solution)/shard_map/all_to_all | solution.py:282
  69.1 2.0 %collective-permute-done.3.refs_0_ = bf16[2,32,1024]{2,1,0:T(8,128)(2,1)S(1)} collective-permute-done((bf16[2,32,1024]{2,1,0:T(8,128)(2,1)S(1)}, bf16[2,32,1024]{2,1,0:T(8,128)(2,1)S(1)}, u32[]{:S(2)}, u32[]{:S(2)}) %collective-permute-start.3) | collective-permute-done | bytes 131104 | tf_op jit(solution)/shard_map/ppermute | solution.py:206
  71.1 0.0 collective-permute-done.4._.rest_3_
  71.1 0.0 collective-permute-done.2.near_pair_ref
  71.1 1.9 %collective-permute-start.6 = (bf16[4,2,32,1024]{3,2,1,0:T(8,128)(2,1)S(1)}, bf16[4,2,32,1024]{3,2,1,0:T(8,128)(2,1)S(1)}, u32[]{:S(2)}, u32[]{:S(2)}) collective-permute-start(bf16[4,2,32,1024]{3,2,1,0:T(8,128)(2,1)S(1)} %collect_rest.1.rest_1_), channel_id=1, source_target_pairs={{0,1},{1,0},{2,3},{3,2},{4,5},{5,4},{6,7},{7,6},{8,9},{9,8},{10,11... | collective-permute-start | bytes 1572872 | tf_op jit(solution)/shard_map/ppermute | solution.py:206
  73.1 3.1 %collective-permute-start.5 = (bf16[2,32,1024]{2,1,0:T(8,128)(2,1)S(1)}, bf16[2,32,1024]{2,1,0:T(8,128)(2,1)S(1)}, u32[]{:S(2)}, u32[]{:S(2)}) collective-permute-start(bf16[2,32,1024]{2,1,0:T(8,128)(2,1)S(1)} %settle.1.far_ref), channel_id=1, source_target_pairs={{0,2},{1,3},{2,0},{3,1},{4,6},{5,7},{6,4},{7,5},{8,10},{9,11},{10,... | collective-permute-start | bytes 393224 | tf_op jit(solution)/shard_map/ppermute | solution.py:206
  76.2 4.7 %collective-permute-done.5.rest_2_ = bf16[2,32,1024]{2,1,0:T(8,128)(2,1)S(1)} collective-permute-done((bf16[2,32,1024]{2,1,0:T(8,128)(2,1)S(1)}, bf16[2,32,1024]{2,1,0:T(8,128)(2,1)S(1)}, u32[]{:S(2)}, u32[]{:S(2)}) %collective-permute-start.5) | collective-permute-done | bytes 131104 | tf_op jit(solution)/shard_map/ppermute | solution.py:206
  80.9 1.9 %collective-permute-start.7 = (bf16[2,32,1024]{2,1,0:T(8,128)(2,1)S(1)}, bf16[2,32,1024]{2,1,0:T(8,128)(2,1)S(1)}, u32[]{:S(2)}, u32[]{:S(2)}) collective-permute-start(bf16[2,32,1024]{2,1,0:T(8,128)(2,1)S(1)} %collective-permute-done.5.rest_2_), channel_id=1, source_target_pairs={{0,1},{1,0},{2,3},{3,2},{4,5},{5,4},{6,7},{7,6},{8,9},{9,8},{10,11... | collective-permute-start | bytes 393224 | tf_op jit(solution)/shard_map/ppermute | solution.py:206
  82.8 1.3 %collective-permute-done.7.rest_5_ = bf16[2,32,1024]{2,1,0:T(8,128)(2,1)S(1)} collective-permute-done((bf16[2,32,1024]{2,1,0:T(8,128)(2,1)S(1)}, bf16[2,32,1024]{2,1,0:T(8,128)(2,1)S(1)}, u32[]{:S(2)}, u32[]{:S(2)}) %collective-permute-start.7) | collective-permute-done | bytes 131104 | tf_op jit(solution)/shard_map/ppermute | solution.py:206
  84.1 0.0 collective-permute-done.6.rest_4_
  84.1 0.0 all-to-all-done.2.weights_ref
  84.1 0.8 multiply.1
  84.9 3.1 %collective-permute-start.8 = (bf16[64,1024]{1,0:T(8,128)(2,1)S(1)}, bf16[64,1024]{1,0:T(8,128)(2,1)S(1)}, u32[]{:S(2)}, u32[]{:S(2)}) collective-permute-start(bf16[64,1024]{1,0:T(8,128)(2,1)S(1)} %get-tuple-element.14), channel_id=1, source_target_pairs={{0,6},{1,7},{2,4},{3,5},{4,2},{5,3},{6,0},{7,1},{8,14},{9,15},{10,... | collective-permute-start | bytes 393224 | tf_op jit(solution)/shard_map/ppermute | solution.py:206
  87.9 5.6 %collective-permute-done.8 = bf16[64,1024]{1,0:T(8,128)(2,1)S(1)} collective-permute-done((bf16[64,1024]{1,0:T(8,128)(2,1)S(1)}, bf16[64,1024]{1,0:T(8,128)(2,1)S(1)}, u32[]{:S(2)}, u32[]{:S(2)}) %collective-permute-start.8) | collective-permute-done | bytes 131104 | tf_op jit(solution)/shard_map/ppermute | solution.py:206
  93.5 0.7 convert_add_fusion
  (2 shorter events, 0.0 us)
Async XLA Ops:
  0.0 15.3 %copy-start.4 = (bf16[2,32,1024]{2,1,0:T(8,128)(2,1)S(1)}, bf16[2,32,1024]{2,1,0:T(8,128)(2,1)}, u32[]{:S(2)}) copy-start(bf16[2,32,1024]{2,1,0:T(8,128)(2,1)} %refs_0_.1) | copy-start | bytes 393220
  2.2 32.2 %copy-start.1 = (s32[32,32]{1,0:T(8,128)S(1)}, s32[32,32]{1,0:T(8,128)}, u32[]{:S(2)}) copy-start(s32[32,32]{1,0:T(8,128)} %tiles_ref.3) | copy-start | bytes 12292
  2.2 32.2 %copy-start.3 = (s32[32]{0:T(128)S(1)}, s32[32]{0:T(128)}, u32[]{:S(2)}) copy-start(s32[32]{0:T(128)} %count_ref.3) | copy-start | bytes 388
  2.2 32.2 %all-to-all-start = ((bf16[32,8,128]{2,1,0:T(8,128)(2,1)}), bf16[32,8,128]{2,1,0:T(8,128)(2,1)S(1)}, u32[]{:S(2)}, u32[]{:S(2)}) async-start(bf16[32,8,128]{2,1,0:T(8,128)(2,1)} %bitcast.7), calls=%async_computation | async-start | bytes 131072 | tf_op jit(solution)/shard_map/all_to_all | solution.py:225
  15.3 31.3 %collective-permute-start = (bf16[2,32,1024]{2,1,0:T(8,128)(2,1)S(1)}, bf16[2,32,1024]{2,1,0:T(8,128)(2,1)S(1)}, u32[]{:S(2)}, u32[]{:S(2)}) collective-permute-start(bf16[2,32,1024]{2,1,0:T(8,128)(2,1)S(1)} %copy-done.4), channel_id=1, source_target_pairs={{0,8},{1,9},{2,10},{3,11},{4,12},{5,13},{6,14},{7,15},{8,0},{9,1},... | collective-permute-start | bytes 393224 | tf_op jit(solution)/shard_map/ppermute | solution.py:206
  26.2 20.4 %collective-permute-start.1 = (bf16[2,32,1024]{2,1,0:T(8,128)(2,1)S(1)}, bf16[2,32,1024]{2,1,0:T(8,128)(2,1)S(1)}, u32[]{:S(2)}, u32[]{:S(2)}) collective-permute-start(bf16[2,32,1024]{2,1,0:T(8,128)(2,1)S(1)} %copy-done.4), channel_id=1, source_target_pairs={{0,24},{1,25},{2,26},{3,27},{4,28},{5,29},{6,30},{7,31},{8,16},{9,... | collective-permute-start | bytes 393224 | tf_op jit(solution)/shard_map/ppermute | solution.py:206
  36.2 10.4 %copy-start = (s32[32,32]{1,0:T(8,128)S(1)}, s32[32,32]{1,0:T(8,128)}, u32[]{:S(2)}) copy-start(s32[32,32]{1,0:T(8,128)} %refs_6_.1) | copy-start | bytes 12292
  36.2 23.5 %all-to-all-start.1 = ((bf16[32,8,128]{2,1,0:T(8,128)(2,1)}), bf16[32,8,128]{2,1,0:T(8,128)(2,1)S(1)}, u32[]{:S(2)}, u32[]{:S(2)}) async-start(bf16[32,8,128]{2,1,0:T(8,128)(2,1)} %route.1), calls=%async_computation.1 | async-start | bytes 131072 | tf_op jit(solution)/shard_map/all_to_all | solution.py:251
  46.6 0.7 copy-start.2
  47.5 23.6 %collective-permute-start.4 = (bf16[3,2,32,1024]{3,2,1,0:T(8,128)(2,1)S(1)}, bf16[3,2,32,1024]{3,2,1,0:T(8,128)(2,1)S(1)}, u32[]{:S(2)}, u32[]{:S(2)}) collective-permute-start(bf16[3,2,32,1024]{3,2,1,0:T(8,128)(2,1)S(1)} %get-tuple-element.11.rest_0_), channel_id=1, source_target_pairs={{0,1},{1,0},{2,3},{3,2},{4,5},{5,4},{6,7},{7,6},{8,9},{9,8},{10,11... | collective-permute-start | bytes 1179656 | tf_op jit(solution)/shard_map/ppermute | solution.py:206
  49.5 21.5 %collective-permute-start.2 = (bf16[3,2,32,1024]{3,2,1,0:T(8,128)(2,1)S(1)}, bf16[3,2,32,1024]{3,2,1,0:T(8,128)(2,1)S(1)}, u32[]{:S(2)}, u32[]{:S(2)}) collective-permute-start(bf16[3,2,32,1024]{3,2,1,0:T(8,128)(2,1)S(1)} %get-tuple-element.11.rest_0_), channel_id=1, source_target_pairs={{0,2},{1,3},{2,0},{3,1},{4,6},{5,7},{6,4},{7,5},{8,10},{9,11},{10,... | collective-permute-start | bytes 1179656 | tf_op jit(solution)/shard_map/ppermute | solution.py:206
  52.3 18.8 %collective-permute-start.3 = (bf16[2,32,1024]{2,1,0:T(8,128)(2,1)S(1)}, bf16[2,32,1024]{2,1,0:T(8,128)(2,1)S(1)}, u32[]{:S(2)}, u32[]{:S(2)}) collective-permute-start(bf16[2,32,1024]{2,1,0:T(8,128)(2,1)S(1)} %get-tuple-element.12), channel_id=1, source_target_pairs={{0,24},{1,25},{2,26},{3,27},{4,28},{5,29},{6,30},{7,31},{8,16},{9,... | collective-permute-start | bytes 393224 | tf_op jit(solution)/shard_map/ppermute | solution.py:206
  60.5 23.6 %all-to-all-start.2 = ((bf16[32,4,8,128]{3,2,1,0:T(8,128)(2,1)}), bf16[32,4,8,128]{3,2,1,0:T(8,128)(2,1)S(1)}, u32[]{:S(2)}, u32[]{:S(2)}) async-start(bf16[32,4,8,128]{3,2,1,0:T(8,128)(2,1)} %accumulate.1.refs_1_), calls=%async_computation.2 | async-start | bytes 524288 | tf_op jit(solution)/shard_map/all_to_all | solution.py:282
  71.1 13.0 %collective-permute-start.6 = (bf16[4,2,32,1024]{3,2,1,0:T(8,128)(2,1)S(1)}, bf16[4,2,32,1024]{3,2,1,0:T(8,128)(2,1)S(1)}, u32[]{:S(2)}, u32[]{:S(2)}) collective-permute-start(bf16[4,2,32,1024]{3,2,1,0:T(8,128)(2,1)S(1)} %collect_rest.1.rest_1_), channel_id=1, source_target_pairs={{0,1},{1,0},{2,3},{3,2},{4,5},{5,4},{6,7},{7,6},{8,9},{9,8},{10,11... | collective-permute-start | bytes 1572872 | tf_op jit(solution)/shard_map/ppermute | solution.py:206
  73.1 7.8 %collective-permute-start.5 = (bf16[2,32,1024]{2,1,0:T(8,128)(2,1)S(1)}, bf16[2,32,1024]{2,1,0:T(8,128)(2,1)S(1)}, u32[]{:S(2)}, u32[]{:S(2)}) collective-permute-start(bf16[2,32,1024]{2,1,0:T(8,128)(2,1)S(1)} %settle.1.far_ref), channel_id=1, source_target_pairs={{0,2},{1,3},{2,0},{3,1},{4,6},{5,7},{6,4},{7,5},{8,10},{9,11},{10,... | collective-permute-start | bytes 393224 | tf_op jit(solution)/shard_map/ppermute | solution.py:206
  80.9 3.2 %collective-permute-start.7 = (bf16[2,32,1024]{2,1,0:T(8,128)(2,1)S(1)}, bf16[2,32,1024]{2,1,0:T(8,128)(2,1)S(1)}, u32[]{:S(2)}, u32[]{:S(2)}) collective-permute-start(bf16[2,32,1024]{2,1,0:T(8,128)(2,1)S(1)} %collective-permute-done.5.rest_2_), channel_id=1, source_target_pairs={{0,1},{1,0},{2,3},{3,2},{4,5},{5,4},{6,7},{7,6},{8,9},{9,8},{10,11... | collective-permute-start | bytes 393224 | tf_op jit(solution)/shard_map/ppermute | solution.py:206
  84.9 8.7 %collective-permute-start.8 = (bf16[64,1024]{1,0:T(8,128)(2,1)S(1)}, bf16[64,1024]{1,0:T(8,128)(2,1)S(1)}, u32[]{:S(2)}, u32[]{:S(2)}) collective-permute-start(bf16[64,1024]{1,0:T(8,128)(2,1)S(1)} %get-tuple-element.14), channel_id=1, source_target_pairs={{0,6},{1,7},{2,4},{3,5},{4,2},{5,3},{6,0},{7,1},{8,14},{9,15},{10,... | collective-permute-start | bytes 393224 | tf_op jit(solution)/shard_map/ppermute | solution.py:206
